TPU v7x, 128 devices: a whole 4x4x4 slice. The times are simulated.
128 devices in a mesh: chain: 8 (over x, core), sector: 16 (over z, y).
Axes of the slice: x: 4, y: 4, z: 4, core: 2. Of those that a mesh axis runs over, the one named last changes fastest.
Arguments:
- left_env: float32 [8, 16, 128, 128, 128], P('chain', None, 'sector'), may hold values from -3 to 3
- right_env: float32 [8, 16, 128, 128, 128], P('chain', None, 'sector'), may hold values from -3 to 3
- site_block: float32 [8, 128, 128, 128], P('chain', 'sector'), may hold values from -0.5 to 0.5
- start_vec: float32 [8, 128, 128, 128], P('chain', 'sector'), may hold values from -6 to 6
- slot_sector: int32 [128], replicated, may hold values from 0 to 127, each once
- couple: int32 [128, 16], replicated, may hold values from 0 to 127, as said below
- dims: int32 [128], replicated, may hold values from 64 to 128, as said below
- kept: int32 [128], replicated, may hold values from 0 to 1, as said below
Outputs:
- wave: float32 [8, 128, 128, 128], P('chain', 'sector')
- env_next: float32 [8, 16, 128, 128, 128], P('chain', None, 'sector')
- energy: float32 [8], P('chain')
Inputs may be any that keep to these rules, and one draw needn't show every extreme that they name: `slot_sector`: a permutation of the sector ids. couple[s, 0] = s for every sector s (the on-site term). `dims`: at least one sector uses the full block. At least one sector is kept.
All inputs are finite; a program needn't handle non-finite values.
Results may differ from a plain program's by a relative error of at most 0.00013.
Values sent between devices are 32-bit elements; how exact they have to be, the bound alone decides.
No kernel may reach another device: no remote copies, remote signals or barrier semaphores. Data moves between devices by JAX's collectives and lax.ppermute only.
A program may use at most 128 MiB of HBM per device.

v0:
```python
import jax
import jax.numpy as jnp
from jax import lax
from jax.sharding import PartitionSpec as P

ITERS = 2


HI = lax.Precision.HIGHEST


def passed_along(value, axis, steps):
    count = lax.axis_size(axis)
    leading, last = (max(0, -steps), min(count, count - steps))
    return lax.ppermute(value, axis, [(source, source + steps) for source in range(leading, last)])


def update(lenv, site):
    half = jnp.einsum("wsab,sbj->wsaj", lenv, site, precision=HI)
    return jnp.einsum("sai,wsaj->wsij", site, half, precision=HI)


def body(left_env, right_env, site_block, start_vec, slot_sector, couple, dims, kept):
    lenv = left_env[0]
    renv = right_env[0]
    site = site_block[0]
    start = start_vec[0]
    sdev = start.shape[0]
    blk = start.shape[1]
    nsec = slot_sector.shape[0]
    owner = lax.axis_index("sector")
    slots = owner * sdev + jnp.arange(sdev, dtype=jnp.int32)
    sector_ids = jnp.take(slot_sector, slots)
    inverse = jnp.zeros((nsec,), jnp.int32).at[slot_sector].set(jnp.arange(nsec, dtype=jnp.int32))
    source = inverse[couple[sector_ids]]
    limit = dims[sector_ids]
    inside = jnp.arange(blk, dtype=jnp.int32)[None, :] < limit[:, None]
    mask = (inside[:, :, None] & inside[:, None, :]).astype(jnp.float32)
    mask = mask * kept[sector_ids].astype(jnp.float32)[:, None, None]
    updated = update(lenv, site)
    arrived = passed_along(updated, "chain", 1)
    luse = jnp.where(lax.axis_index("chain") == 0, lenv, arrived)

    def apply(vec):
        whole = lax.all_gather(vec, "sector", axis=0, tiled=True)
        picked = whole[source]
        inner = jnp.einsum("swab,wsbc->swac", picked, renv, precision=HI)
        return mask * jnp.einsum("wsia,swac->sic", luse, inner, precision=HI)

    x = mask * start
    x = x / jnp.sqrt(lax.psum(jnp.sum(x * x), "sector") + 1e-06)
    y = apply(x)
    lam = jnp.float32(0.0)
    for step in range(ITERS):
        a = lax.psum(jnp.sum(x * y), "sector")
        resid = y - a * x
        b2 = lax.psum(jnp.sum(resid * resid), "sector") + 1e-06
        b = jnp.sqrt(b2)
        z = apply(resid)
        d = lax.psum(jnp.sum(resid * z), "sector") / b2
        lam = (a + d) / 2 - jnp.sqrt(((a - d) / 2) ** 2 + b2)
        q = lam - a
        n = jnp.sqrt(b2 + q * q)
        x = (b * x + q / b * resid) / n
        y = (b * y + q / b * z) / n
    return (x[None], updated[None], jnp.reshape(lam, (1,)))


def solution(mesh):
    placed = (
        P("chain", None, "sector", None, None),
        P("chain", None, "sector", None, None),
        P("chain", "sector", None, None),
        P("chain", "sector", None, None),
        P(),
        P(),
        P(),
        P(),
    )
    return jax.shard_map(
        body,
        mesh=mesh,
        in_specs=placed,
        out_specs=(
            P("chain", "sector", None, None),
            P("chain", None, "sector", None, None),
            P("chain"),
        ),
        check_vma=False,
    )
```

profile of v0, /device:TPU:0, one launch (start us, length us, event | category | flops | bytes accessed | tf_op | source)
XLA Modules:
  0.0 603.3 jit_solution(2324921091473273037)
XLA Ops:
  13.2 42.6 %psum.49 = f32[]{:T(128)} all-reduce(f32[]{:T(128)} %multiply_reduce_fusion.5), channel_id=1, replica_groups=mesh['chain'=8,'sector'=16] {'sector'}, use_global_device_ids=true, to_apply=%region_1.2 | all-reduce | flops 1 | bytes 8 | tf_op jit(solution)/shard_map/psum | solution.py:51
  58.7 10.5 %fusion.2 = f32[8,128,16,128]{3,1,2,0:T(8,128)S(1)} fusion(f32[1,8,128,128]{3,2,1,0:T(8,128)S(1)} %copy-done, f32[1,16,8,128,128]{4,3,2,1,0:T(8,128)} %param.8), kind=kOutput, calls=%fused_computation.11 | convolution fusion | flops 3221225472 | bytes 17301504 | tf_op jit(solution)/shard_map/wsab,sbj->wsaj/dot_general | solution.py:19
  69.2 9.3 %fusion = f32[8,16,128,128]{3,2,1,0:T(8,128)} fusion(f32[8,128,16,128]{3,1,2,0:T(8,128)S(1)} %fusion.2, f32[1,8,128,128]{3,2,1,0:T(8,128)S(1)} %copy-done), kind=kOutput, calls=%fused_computation.9 | convolution fusion | flops 3221225472 | bytes 17301504 | tf_op jit(solution)/shard_map/sai,wsaj->wsij/dot_general | solution.py:20
  78.4 4.6 collective-permute-start
  83.1 9.2 %copy.23 = f32[1,16,8,128,128]{3,4,1,2,0:T(8,128)} copy(f32[1,16,8,128,128]{4,3,2,1,0:T(8,128)} %param.8) | data formatting | bytes 16777216 | tf_op args[0]
  95.7 9.5 %bitcast_select_fusion = f32[16,8,128,128]{2,3,0,1:T(8,128)} fusion(f32[16,8,128,128]{2,3,0,1:T(8,128)} %collective-permute-done, f32[1,16,8,128,128]{3,4,1,2,0:T(8,128)} %copy.23, pred[]{:T(512)S(6)} %eq.3), kind=kLoop, calls=%fused_computation.13 | loop fusion | flops 2097152 | bytes 25165824 | tf_op jit(solution)/shard_map/jit(_where)/select_n | solution.py:42
  105.1 20.8 %all-gather.4.cloned.1.call-done = f32[128,128,128]{2,1,0:T(8,128)} async-done(((f32[8,128,128]{2,1,0:T(8,128)}), f32[128,128,128]{2,1,0:T(8,128)}) %all-gather.4.cloned.1.call-update) | async-done | bytes 8388624 | tf_op jit(solution)/shard_map/all_gather | solution.py:45
  125.9 7.9 %gather_fusion.5 = f32[128,128,128]{2,1,0:T(8,128)} fusion(f32[128,128,128]{2,1,0:T(8,128)} %all-gather.4.cloned.1.call-done, s32[1024]{0:T(1024)S(1)} %pad_clamp_fusion), kind=kCustom, calls=%fused_computation.5 | custom fusion | bytes 16777728 | tf_op jit(solution)/shard_map/gather | solution.py:46
  133.8 14.5 %fusion.8 = f32[8,16,128,128]{3,2,1,0:T(8,128)} fusion(f32[8,16,128,128]{3,2,1,0:T(8,128)} %bitcast.93, f32[1,16,8,128,128]{4,3,2,1,0:T(8,128)} %param.9), kind=kOutput, calls=%fused_computation.18 | convolution fusion | flops 3221225472 | bytes 25165824 | tf_op jit(solution)/shard_map/swab,wsbc->swac/dot_general | solution.py:47
  148.3 16.7 %multiply_reduce_fusion.4 = (f32[]{:T(128)}, f32[8,128,128]{2,1,0:T(8,128)S(1)}) fusion(f32[8,128,128]{2,1,0:T(8,128)S(1)} %copy-done.7, f32[16,8,128,128]{2,3,0,1:T(8,128)S(1)} %copy-done.3, f32[8,16,128,128]{3,2,1,0:T(8,128)} %fusion.8, f32[8]{0:T(128)S(1)} %convert_element_type.8, pred[8,128]{1,0:T(8,128)(4,1)S(1)} %iota_compare_fusion), kind=kOutput, calls=%fused_computation.40 | convolution fusion | flops 3221880832 | bytes 17826852 | tf_op jit(solution)/shard_map/wsia,swac->sic/dot_general | solution.py:48
  165.0 39.1 %psum.50 = f32[]{:T(128)} all-reduce(f32[]{:T(128)} %get-tuple-element.22), channel_id=1, replica_groups=mesh['chain'=8,'sector'=16] {'sector'}, use_global_device_ids=true, to_apply=%region_4.5 | all-reduce | flops 1 | bytes 8 | tf_op jit(solution)/shard_map/psum | solution.py:55
  205.8 125.2 %all-gather.6.cloned.1.call-done = f32[128,128,128]{2,1,0:T(8,128)} async-done(((f32[8,128,128]{2,1,0:T(8,128)}), f32[128,128,128]{2,1,0:T(8,128)}) %all-gather.6.cloned.1.call-update) | async-done | bytes 8388624 | tf_op jit(solution)/shard_map/all_gather | solution.py:45
  330.9 7.9 %gather_fusion.6 = f32[128,128,128]{2,1,0:T(8,128)} fusion(f32[128,128,128]{2,1,0:T(8,128)} %all-gather.6.cloned.1.call-done, s32[1024]{0:T(1024)S(1)} %pad_clamp_fusion), kind=kCustom, calls=%fused_computation.6 | custom fusion | bytes 16777728 | tf_op jit(solution)/shard_map/gather | solution.py:46
  338.8 11.4 %fusion.6 = f32[8,16,128,128]{3,2,1,0:T(8,128)S(1)} fusion(f32[8,16,128,128]{3,2,1,0:T(8,128)} %bitcast.94, f32[1,16,8,128,128]{4,3,2,1,0:T(8,128)} %param.9), kind=kOutput, calls=%fused_computation.16 | convolution fusion | flops 3221225472 | bytes 25165824 | tf_op jit(solution)/shard_map/swab,wsbc->swac/dot_general | solution.py:47
  350.2 16.4 %multiply_reduce_fusion.2 = (f32[]{:T(128)}, f32[]{:T(128)}, f32[8,128,128]{2,1,0:T(8,128)S(1)}) fusion(f32[8,128,128]{2,1,0:T(8,128)S(1)} %copy-done.4, f32[16,8,128,128]{2,3,0,1:T(8,128)} %bitcast_select_fusion, f32[8,16,128,128]{3,2,1,0:T(8,128)S(1)} %fusion.6, f32[8]{0:T(128)S(1)} %convert_element_type.8, pred[8,128]{1,0:T(8,128)(4,1)S(1)} %iota_compare_fusion), kind=kOutput, calls=%fused_computation.37 | convolution fusion | flops 3222142976 | bytes 17826856 | tf_op jit(solution)/shard_map/wsia,swac->sic/dot_general | solution.py:48
  366.7 39.1 %all-reduce.1 = (f32[]{:T(128)}, f32[]{:T(128)}) all-reduce(f32[]{:T(128)} %get-tuple-element.13, f32[]{:T(128)} %get-tuple-element.12), channel_id=1, replica_groups=mesh['chain'=8,'sector'=16] {'sector'}, use_global_device_ids=true, to_apply=%region_6.7 | all-reduce | flops 2 | bytes 16 | tf_op jit(solution)/shard_map/psum | solution.py:57
  410.1 36.3 %psum.53 = f32[]{:T(128)} all-reduce(f32[]{:T(128)} %get-tuple-element.20), channel_id=1, replica_groups=mesh['chain'=8,'sector'=16] {'sector'}, use_global_device_ids=true, to_apply=%region_10.11 | all-reduce | flops 1 | bytes 8 | tf_op jit(solution)/shard_map/psum | solution.py:55
  446.3 2.2 multiply_reduce_fusion
  448.5 9.3 %copy.33 = f32[1,16,8,128,128]{4,3,2,1,0:T(8,128)} copy(f32[1,16,8,128,128]{3,4,1,2,0:T(8,128)} %bitcast.24) | data formatting | bytes 16777216
  457.8 59.4 %all-gather.8.cloned.1.call-done = f32[128,128,128]{2,1,0:T(8,128)} async-done(((f32[8,128,128]{2,1,0:T(8,128)}), f32[128,128,128]{2,1,0:T(8,128)}) %all-gather.8.cloned.1.call-update) | async-done | bytes 8388624 | tf_op jit(solution)/shard_map/all_gather | solution.py:45
  517.2 7.7 %gather_fusion.7 = f32[128,128,128]{2,1,0:T(8,128)} fusion(f32[128,128,128]{2,1,0:T(8,128)} %all-gather.8.cloned.1.call-done, s32[1024]{0:T(1024)S(1)} %pad_clamp_fusion), kind=kCustom, calls=%fused_computation.7 | custom fusion | bytes 16777728 | tf_op jit(solution)/shard_map/gather | solution.py:46
  524.9 11.0 %fusion.4 = f32[8,16,128,128]{3,2,1,0:T(8,128)S(1)} fusion(f32[8,16,128,128]{3,2,1,0:T(8,128)} %bitcast.92, f32[1,16,8,128,128]{4,3,2,1,0:T(8,128)} %param.9), kind=kOutput, calls=%fused_computation.14 | convolution fusion | flops 3221225472 | bytes 25165824 | tf_op jit(solution)/shard_map/swab,wsbc->swac/dot_general | solution.py:47
  535.9 16.3 %fusion.14 = f32[]{:T(128)} fusion(f32[8,128,128]{2,1,0:T(8,128)S(1)} %copy-done.6, f32[16,8,128,128]{2,3,0,1:T(8,128)} %bitcast_select_fusion, f32[8,16,128,128]{3,2,1,0:T(8,128)S(1)} %fusion.4, f32[8]{0:T(128)S(1)} %convert_element_type.8, pred[8,128]{1,0:T(8,128)(4,1)S(1)} %iota_compare_fusion), kind=kOutput, calls=%fused_computation.28 | convolution fusion | flops 3221880832 | bytes 17302564 | tf_op jit(solution)/shard_map/wsia,swac->sic/dot_general | solution.py:48
  552.2 39.1 %all-reduce = (f32[]{:T(128)}, f32[]{:T(128)}) all-reduce(f32[]{:T(128)} %get-tuple-element.18, f32[]{:T(128)} %fusion.14), channel_id=1, replica_groups=mesh['chain'=8,'sector'=16] {'sector'}, use_global_device_ids=true, to_apply=%region_12.13 | all-reduce | flops 2 | bytes 16 | tf_op jit(solution)/shard_map/psum | solution.py:57
  (52 shorter events, 15.0 us)
Async XLA Ops:
  7.2 51.5 %copy-start = (f32[1,8,128,128]{3,2,1,0:T(8,128)S(1)}, f32[1,8,128,128]{3,2,1,0:T(8,128)}, u32[]{:S(2)}) copy-start(f32[1,8,128,128]{3,2,1,0:T(8,128)} %param.10) | copy-start | bytes 1572868
  7.2 118.7 %all-gather.4.cloned.1.call-start = ((), (), s32[]{:S(2)}) async-start(), calls=%async_computation | async-start | bytes 8912896 | tf_op jit(solution)/shard_map/all_gather | solution.py:45
  58.6 272.3 %all-gather.6.cloned.1.call-start = ((), (), s32[]{:S(2)}) async-start(), calls=%async_computation.1 | async-start | bytes 8912896 | tf_op jit(solution)/shard_map/all_gather | solution.py:45
  78.4 13.8 %copy-start.8 = (s32[128,16]{0,1:T(8,128)S(1)}, s32[128,16]{0,1:T(8,128)}, u32[]{:S(2)}) copy-start(s32[128,16]{0,1:T(8,128)} %param.13) | copy-start | bytes 24580
  78.4 14.6 %copy-start.2 = (s32[128]{0:T(128)S(1)}, s32[128]{0:T(128)}, u32[]{:S(2)}) copy-start(s32[128]{0:T(128)} %param.12) | copy-start | bytes 1540
  78.4 17.2 %collective-permute-start = (f32[16,8,128,128]{2,3,0,1:T(8,128)}, f32[16,8,128,128]{2,3,0,1:T(8,128)}, u32[]{:S(2)}, u32[]{:S(2)}) collective-permute-start(f32[16,8,128,128]{2,3,0,1:T(8,128)} %bitcast.10), channel_id=1, source_target_pairs={{0,16},{16,32},{32,48},{48,64},{64,80},{80,96},{96,112},{1,17},{17... | collective-permute-start | bytes 25165832 | tf_op jit(solution)/shard_map/ppermute | solution.py:15
  133.8 14.5 %copy-start.3 = (f32[16,8,128,128]{2,3,0,1:T(8,128)S(1)}, f32[16,8,128,128]{2,3,0,1:T(8,128)}, u32[]{:S(2)}) copy-start(f32[16,8,128,128]{2,3,0,1:T(8,128)} %bitcast_select_fusion) | copy-start | bytes 25165828
  133.8 14.5 %copy-start.7 = (f32[8,128,128]{2,1,0:T(8,128)S(1)}, f32[8,128,128]{2,1,0:T(8,128)}, u32[]{:S(2)}) copy-start(f32[8,128,128]{2,1,0:T(8,128)} %fusion.17) | copy-start | bytes 1572868
  148.3 55.8 %copy-start.5 = (f32[1,8,128,128]{3,2,1,0:T(8,128)S(1)}, f32[1,8,128,128]{3,2,1,0:T(8,128)}, u32[]{:S(2)}) copy-start(f32[1,8,128,128]{3,2,1,0:T(8,128)} %param.11) | copy-start | bytes 1572868
  205.7 311.5 %all-gather.8.cloned.1.call-start = ((), (), s32[]{:S(2)}) async-start(), calls=%async_computation.2 | async-start | bytes 8912896 | tf_op jit(solution)/shard_map/all_gather | solution.py:45
  338.8 11.4 %copy-start.4 = (f32[8,128,128]{2,1,0:T(8,128)S(1)}, f32[8,128,128]{2,1,0:T(8,128)}, u32[]{:S(2)}) copy-start(f32[8,128,128]{2,1,0:T(8,128)} %multiply_subtract_fusion.1) | copy-start | bytes 1572868
  524.8 11.1 %copy-start.6 = (f32[8,128,128]{2,1,0:T(8,128)S(1)}, f32[8,128,128]{2,1,0:T(8,128)}, u32[]{:S(2)}) copy-start(f32[8,128,128]{2,1,0:T(8,128)} %get-tuple-element.19) | copy-start | bytes 1572868
  524.9 70.6 %copy-start.1 = (f32[1,8,128,128]{3,2,1,0:T(8,128)S(1)}, f32[1,8,128,128]{3,2,1,0:T(8,128)}, u32[]{:S(2)}) copy-start(f32[1,8,128,128]{3,2,1,0:T(8,128)} %param.10) | copy-start | bytes 1572868
Sparse Core Ops, SparseCore 0:
  58.7 67.1 all-gather.3
  205.8 125.0 all-gather.5
  448.6 68.5 all-gather.7
where the time goes:
time: 611 us; the launch traced here: 603 us
  waiting for transfers between devices  205 us (34%)
  blocking collectives  196 us (32%)
  matrix products  106 us (17%)
  local copies, waits for them, and re-layouts  49.2 us (8%)
  between operations  22.7 us (4%)
  other arithmetic  19.1 us (3%)
    all_gather x3, waiting for transfers between devices, apply(): whole = lax.all_gather(vec, 'sector', axis=0, tiled=True)  205 us
    psum x2, blocking collectives, body(): b2 = lax.psum(jnp.sum(resid * resid), 'sector') + 1e-06  78.1 us
    psum x2, blocking collectives, body(): a = lax.psum(jnp.sum(x * y), 'sector')  75.3 us
    dot_general x3, matrix products, apply(): return mask * jnp.einsum('wsia,swac->sic', luse, inner, precision=HI)  49.4 us
    psum x1, blocking collectives, body(): x = x / jnp.sqrt(lax.psum(jnp.sum(x * x), 'sector') + 1e-06)  42.6 us
    dot_general x3, matrix products, apply(): inner = jnp.einsum('swab,wsbc->swac', picked, renv, precision=HI)  36.9 us
    gather x3, local copies, waits for them, and re-layouts, apply(): picked = whole[source]  23.4 us
    unnamed x21, local copies, waits for them, and re-layouts  18.6 us
  transfers between devices with their start and end apart: 4, of which 3 were waited for; matrix products, arithmetic and copies ran while one was open for 8% of the time, Pallas kernels for 0%

commit v1 on v0

v1 whole, which is shorter than its diff:
```python
import functools

import jax
import jax.numpy as jnp
from jax import lax
from jax.experimental import pallas as pl
from jax.experimental.pallas import tpu as pltpu
from jax.sharding import PartitionSpec as P

MIB = 1 << 20


def split(value):
    high = value.astype(jnp.bfloat16)
    low = (value - high.astype(jnp.float32)).astype(jnp.bfloat16)
    return high, low


def dot(left, right):
    return jnp.dot(left, right, preferred_element_type=jnp.float32)


def right_factor(high, low):
    top = jnp.concatenate([high, low], axis=1)
    bottom = jnp.concatenate([high, jnp.zeros_like(low)], axis=1)
    return jnp.concatenate([top, bottom], axis=0)


def folded(value):
    half = value.shape[1] // 2
    return value[:, :half] + value[:, half:]


def update_kernel(left_ref, site_ref, out_ref):
    terms, _, blk, _ = left_ref.shape
    site = site_ref[0]
    factor = right_factor(*split(site))
    high, low = split(site.T)
    outer = jnp.concatenate([high, low, high], axis=1)
    for term in range(0, terms, 2):
        tops = []
        for index in (term, term + 1):
            first = jnp.concatenate(split(left_ref[index, 0]), axis=1)
            half_high, half_low = split(folded(dot(first, factor)))
            tops.append(jnp.concatenate([half_high, half_high, half_low], axis=0))
        both = dot(outer, jnp.concatenate(tops, axis=1))
        out_ref[term, 0] = both[:, :blk]
        out_ref[term + 1, 0] = both[:, blk:]


def update(left, site):
    terms, slots, blk, _ = left.shape
    return pl.pallas_call(
        update_kernel,
        out_shape=jax.ShapeDtypeStruct(left.shape, jnp.float32),
        grid=(slots,),
        in_specs=[
            pl.BlockSpec((terms, 1, blk, blk), lambda s: (0, s, 0, 0)),
            pl.BlockSpec((1, blk, blk), lambda s: (s, 0, 0)),
        ],
        out_specs=pl.BlockSpec((terms, 1, blk, blk), lambda s: (0, s, 0, 0)),
        compiler_params=pltpu.CompilerParams(vmem_limit_bytes=24 * MIB),
        cost_estimate=pl.CostEstimate(
            flops=8 * terms * slots * blk**3, bytes_accessed=8 * left.size, transcendentals=0
        ),
    )(left, site)


def apply_kernel(row_ref, vec_ref, left_ref, right_ref, mask_ref, out_ref, blocks, inner, sems):
    terms, _, blk, _ = left_ref.shape
    slot = pl.program_id(0)
    slots = pl.num_programs(0)

    def fetch(which, buffer, act):
        for term in range(terms):
            row = pl.multiple_of(row_ref[which, term], 8)
            copy = pltpu.make_async_copy(
                vec_ref.at[pl.ds(row, blk), :], blocks.at[buffer, term], sems.at[buffer]
            )
            if act == "start":
                copy.start()
            else:
                copy.wait()

    @pl.when(slot == 0)
    def _():
        fetch(0, 0, "start")

    @pl.when(slot + 1 < slots)
    def _():
        fetch(slot + 1, (slot + 1) % 2, "start")

    now = slot % 2
    fetch(slot, now, "wait")
    for term in range(terms):
        first = jnp.concatenate(split(blocks[now, term]), axis=1)
        value = folded(dot(first, right_factor(*split(right_ref[term, 0]))))
        rows = slice(term * blk, (term + 1) * blk)
        inner[rows, :] = jnp.concatenate(split(value), axis=1)
    total = jnp.zeros((2 * blk, 2 * blk), jnp.float32)
    for term in range(0, terms, 2):
        pairs = [split(left_ref[index, 0]) for index in (term, term + 1)]
        outer = jnp.concatenate(
            [
                jnp.concatenate([pairs[0][0], pairs[1][0]], axis=1),
                jnp.concatenate([pairs[0][1], pairs[1][1]], axis=1),
            ],
            axis=0,
        )
        total = total + dot(outer, inner[term * blk : (term + 2) * blk, :])
    result = total[:blk, :blk] + (total[blk:, :blk] + total[:blk, blk:])
    out_ref[0] = result * mask_ref[0]


def apply(rows, gathered, left, right, mask):
    terms, slots, blk, _ = left.shape
    return pl.pallas_call(
        apply_kernel,
        out_shape=jax.ShapeDtypeStruct((slots, blk, blk), jnp.float32),
        grid_spec=pltpu.PrefetchScalarGridSpec(
            num_scalar_prefetch=1,
            grid=(slots,),
            in_specs=[
                pl.BlockSpec(memory_space=pl.ANY),
                pl.BlockSpec((terms, 1, blk, blk), lambda s, r: (0, s, 0, 0)),
                pl.BlockSpec((terms, 1, blk, blk), lambda s, r: (0, s, 0, 0)),
                pl.BlockSpec((1, blk, blk), lambda s, r: (s, 0, 0)),
            ],
            out_specs=pl.BlockSpec((1, blk, blk), lambda s, r: (s, 0, 0)),
            scratch_shapes=[
                pltpu.VMEM((2, terms, blk, blk), jnp.float32),
                pltpu.VMEM((terms * blk, 2 * blk), jnp.bfloat16),
                pltpu.SemaphoreType.DMA((2,)),
            ],
        ),
        compiler_params=pltpu.CompilerParams(vmem_limit_bytes=24 * MIB),
        cost_estimate=pl.CostEstimate(
            flops=8 * terms * slots * blk**3, bytes_accessed=12 * left.size, transcendentals=0
        ),
    )(rows, gathered, left, right, mask)


def passed_along(value, axis, steps):
    count = lax.axis_size(axis)
    leading, last = (max(0, -steps), min(count, count - steps))
    return lax.ppermute(value, axis, [(source, source + steps) for source in range(leading, last)])


def body(left_env, right_env, site_block, start_vec, slot_sector, couple, dims, kept):
    lenv = left_env[0]
    renv = right_env[0]
    site = site_block[0]
    start = start_vec[0]
    sdev = start.shape[0]
    blk = start.shape[1]
    nsec = slot_sector.shape[0]
    owner = lax.axis_index("sector")
    slots = owner * sdev + jnp.arange(sdev, dtype=jnp.int32)
    sector_ids = jnp.take(slot_sector, slots)
    inverse = jnp.zeros((nsec,), jnp.int32).at[slot_sector].set(jnp.arange(nsec, dtype=jnp.int32))
    source = inverse[couple[sector_ids]]
    limit = dims[sector_ids]
    inside = jnp.arange(blk, dtype=jnp.int32)[None, :] < limit[:, None]
    mask = (inside[:, :, None] & inside[:, None, :]).astype(jnp.float32)
    mask = mask * kept[sector_ids].astype(jnp.float32)[:, None, None]
    updated = update(lenv, site)
    arrived = passed_along(updated, "chain", 1)
    luse = jnp.where(lax.axis_index("chain") == 0, lenv, arrived)
    height = sdev * blk + 8
    rows = (source // sdev) * height + (source % sdev) * blk

    def gather(vec, partial):
        tail = jnp.zeros((8, blk), jnp.float32)
        tail = tail.at[0, : len(partial)].set(jnp.stack(partial))
        packed = jnp.concatenate([vec.reshape(sdev * blk, blk), tail], axis=0)
        whole = lax.all_gather(packed, "sector", axis=0, tiled=True)
        sums = jnp.sum(whole.reshape(-1, height, blk)[:, sdev * blk, : len(partial)], axis=0)
        return whole, [sums[k] for k in range(len(partial))]

    def inner(one, other):
        return jnp.sum(one * other)

    begin = mask * start
    whole, (norm,) = gather(begin, [inner(begin, begin)])
    scale = 1.0 / jnp.sqrt(norm + 1e-06)
    x0 = begin * scale
    y0 = apply(rows, whole, luse, renv, mask) * scale
    whole, (a0,) = gather(y0, [inner(x0, y0)])
    w1 = apply(rows, whole, luse, renv, mask)
    r1 = y0 - a0 * x0
    z1 = w1 - a0 * y0
    whole, (xy, xz, ry, rz, rr) = gather(
        z1, [inner(x0, y0), inner(x0, z1), inner(r1, y0), inner(r1, z1), inner(r1, r1)]
    )

    def mix(a, b2, rz):
        b = jnp.sqrt(b2)
        d = rz / b2
        lam = (a + d) / 2 - jnp.sqrt(((a - d) / 2) ** 2 + b2)
        q = lam - a
        n = jnp.sqrt(b2 + q * q)
        return lam, b / n, (q / b) / n

    _, keep, turn = mix(a0, rr + 1e-06, rz)
    x1 = keep * x0 + turn * r1
    y1 = keep * y0 + turn * z1
    a1 = keep * keep * xy + keep * turn * (xz + ry) + turn * turn * rz
    r2 = y1 - a1 * x1
    w2 = apply(rows, whole, luse, renv, mask)
    z2 = keep * w1 + turn * w2 - a1 * y1
    rr, rz = lax.psum((inner(r2, r2), inner(r2, z2)), "sector")
    lam, keep, turn = mix(a1, rr + 1e-06, rz)
    x2 = keep * x1 + turn * r2
    return (x2[None], updated[None], jnp.reshape(lam, (1,)))


def solution(mesh):
    placed = (
        P("chain", None, "sector", None, None),
        P("chain", None, "sector", None, None),
        P("chain", "sector", None, None),
        P("chain", "sector", None, None),
        P(),
        P(),
        P(),
        P(),
    )
    return jax.shard_map(
        body,
        mesh=mesh,
        in_specs=placed,
        out_specs=(
            P("chain", "sector", None, None),
            P("chain", None, "sector", None, None),
            P("chain"),
        ),
        check_vma=False,
    )
```

time: 611 us -> 442 us (0.72); the launches traced: 603 us -> 441 us
  blocking collectives: 196 us -> 39.1 us
  matrix products: 106 us -> 0 us
  Pallas kernels: 0 us -> 68.4 us
  waiting for transfers between devices: 205 us -> 234 us
  other arithmetic: 19.1 us -> 25.8 us
    psum x5 -> x1, blocking collectives: 196 us -> 39.1 us  [body(): rr, rz = lax.psum((inner(r2, r2), inner(r2, z2)), 'sector')]
    dot_general x8 -> x0, matrix products: 106 us -> none  [the longest x3 49.4 us: apply(): return mask * jnp.einsum('wsia,swac->sic', luse, inner, precision=HI)]
    pallas_call x0 -> x4, Pallas kernels: none -> 68.4 us  [the longest x3 59.5 us: apply(): pl.pallas_call(apply_kernel, out_shape=jax.ShapeDtypeStruct((slots, blk,...]
    gather x3 -> x0, local copies, waits for them, and re-layouts: 23.4 us -> none  [apply(): picked = whole[source]]
    all_gather x3, waiting for transfers between devices: 205 us -> 227 us  [gather(): whole = lax.all_gather(packed, 'sector', axis=0, tiled=True)]
    unnamed x21 -> x33, local copies, waits for them, and re-layouts: 18.6 us -> 35 us
    ppermute x1, waiting for transfers between devices: 0.01 us -> 6.79 us  [passed_along(): lax.ppermute(value, axis, [(source, source + steps) for source in range(l...]
  transfers between devices with their start and end apart: 4 -> 4, of which waited for: 3 -> 4; matrix products, arithmetic and copies ran while one was open for 8% -> 3% of each run, Pallas kernels for 0% -> 2%
where the time goes in v1:
time: 442 us; the launch traced here: 441 us
  waiting for transfers between devices  234 us (53%)
  Pallas kernels  68.4 us (15%)
  local copies, waits for them, and re-layouts  45.2 us (10%)
  blocking collectives  39.1 us (9%)
  other arithmetic  25.8 us (6%)
  between operations  23.2 us (5%)
  starting transfers between devices  4.63 us (1%)
    all_gather x3, waiting for transfers between devices, gather(): whole = lax.all_gather(packed, 'sector', axis=0, tiled=True)  227 us
    pallas_call x3, Pallas kernels, apply(): pl.pallas_call(apply_kernel, out_shape=jax.ShapeDtypeStruct((slots, blk,...  59.5 us
    psum x1, blocking collectives, body(): rr, rz = lax.psum((inner(r2, r2), inner(r2, z2)), 'sector')  39.1 us
    unnamed x33, local copies, waits for them, and re-layouts  35 us
    select_n x1, other arithmetic, body(): luse = jnp.where(lax.axis_index('chain') == 0, lenv, arrived)  9.59 us
    pallas_call x1, Pallas kernels, update(): pl.pallas_call(update_kernel, out_shape=jax.ShapeDtypeStruct(left.shape,...  8.87 us
  transfers between devices with their start and end apart: 4, of which 4 were waited for; matrix products, arithmetic and copies ran while one was open for 3% of the time, Pallas kernels for 2%

profile of v1, /device:TPU:0, one launch (start us, length us, event | category | flops | bytes accessed | tf_op | source)
XLA Modules:
  0.0 440.6 jit_solution(12124534451600934950)
XLA Ops:
  10.7 1.9 and_select_fusion
  15.5 3.4 copy-done.8
  20.0 8.9 %shard_map.103 = f32[16,8,128,128]{3,2,1,0:T(8,128)} custom-call(f32[16,8,128,128]{3,2,1,0:T(8,128)S(1)} %bitcast.71, f32[8,128,128]{2,1,0:T(8,128)S(1)} %bitcast.75), custom_call_target="tpu_custom_call" | custom-call | flops 2147483648 | bytes 16777216 | tf_op jit(solution)/shard_map/pallas_call | solution.py:53
  28.8 4.5 %collective-permute-start = (f32[16,8,128,128]{3,2,1,0:T(8,128)}, f32[16,8,128,128]{3,2,1,0:T(8,128)}, u32[]{:S(2)}, u32[]{:S(2)}) collective-permute-start(f32[16,8,128,128]{3,2,1,0:T(8,128)} %shard_map.103), channel_id=1, source_target_pairs={{0,16},{16,32},{32,48},{48,64},{64,80},{80,96},{96,112},{1,17},{17... | collective-permute-start | bytes 25165832 | tf_op jit(solution)/shard_map/ppermute | solution.py:146
  36.4 6.8 %collective-permute-done = f32[16,8,128,128]{3,2,1,0:T(8,128)} collective-permute-done((f32[16,8,128,128]{3,2,1,0:T(8,128)}, f32[16,8,128,128]{3,2,1,0:T(8,128)}, u32[]{:S(2)}, u32[]{:S(2)}) %collective-permute-start) | collective-permute-done | bytes 8388640 | tf_op jit(solution)/shard_map/ppermute | solution.py:146
  43.2 9.6 %broadcast_select_fusion.left_ref = f32[16,8,128,128]{3,2,1,0:T(8,128)} fusion(f32[16,8,128,128]{3,2,1,0:T(8,128)} %collective-permute-done, pred[]{:T(512)S(6)} %eq.5, f32[1,16,8,128,128]{4,3,2,1,0:T(8,128)} %param.14), kind=kLoop, calls=%fused_computation.6 | loop fusion | flops 2097152 | bytes 25165824 | tf_op jit(solution)/shard_map/jit(_where)/select_n | solution.py:168
  52.8 36.5 %all-gather.4.cloned.1.call-done.vec_ref = f32[16512,128]{1,0:T(8,128)} async-done(((f32[1032,128]{1,0:T(8,128)}), f32[16512,128]{1,0:T(8,128)}) %all-gather.4.cloned.1.call-update) | async-done | bytes 8454160 | tf_op jit(solution)/shard_map/all_gather | solution.py:176
  91.4 3.4 copy-done.2
  94.8 3.4 copy-done.5
  98.2 3.4 copy-done.10
  101.6 19.8 %shard_map.104 = f32[8,128,128]{2,1,0:T(8,128)S(1)} custom-call(s32[8,16]{1,0:T(8,128)S(1)} %fusion.1.row_ref, f32[16512,128]{1,0:T(8,128)S(1)} %copy-done.10, f32[16,8,128,128]{3,2,1,0:T(8,128)S(1)} %copy-done.2, f32[16,8,128,128]{3,2,1,0:T(8,128)S(1)} %bitcast.68, f32[8,128,128]{2,1,0:T(8,128)S(1)} %get-tuple-element.52.mask_ref), custom_call_target="tpu_custom_call" | custom-call | flops 2147483648 | bytes 25165824 | tf_op jit(solution)/shard_map/pallas_call | solution.py:117
  123.8 120.1 %all-gather.6.cloned.1.call-done.vec_ref = f32[16512,128]{1,0:T(8,128)} async-done(((f32[1032,128]{1,0:T(8,128)}), f32[16512,128]{1,0:T(8,128)}) %all-gather.6.cloned.1.call-update) | async-done | bytes 8454160 | tf_op jit(solution)/shard_map/all_gather | solution.py:176
  245.4 3.4 copy-done.3
  248.8 3.4 copy-done.6
  252.1 3.4 copy-done.11
  255.5 19.8 %shard_map.105 = f32[8,128,128]{2,1,0:T(8,128)S(1)} custom-call(s32[8,16]{1,0:T(8,128)S(1)} %fusion.1.row_ref, f32[16512,128]{1,0:T(8,128)S(1)} %copy-done.11, f32[16,8,128,128]{3,2,1,0:T(8,128)S(1)} %copy-done.3, f32[16,8,128,128]{3,2,1,0:T(8,128)S(1)} %bitcast.69, f32[8,128,128]{2,1,0:T(8,128)S(1)} %get-tuple-element.52.mask_ref), custom_call_target="tpu_custom_call" | custom-call | flops 2147483648 | bytes 25165824 | tf_op jit(solution)/shard_map/pallas_call | solution.py:117
  277.1 3.2 stack.25
  281.2 70.9 %all-gather.8.cloned.1.call-done.vec_ref = f32[16512,128]{1,0:T(8,128)} async-done(((f32[1032,128]{1,0:T(8,128)}), f32[16512,128]{1,0:T(8,128)}) %all-gather.8.cloned.1.call-update) | async-done | bytes 8454160 | tf_op jit(solution)/shard_map/all_gather | solution.py:176
  359.6 3.4 copy-done.4
  363.0 3.4 copy-done.7
  366.4 3.4 copy-done.9
  369.8 19.8 %shard_map.106 = f32[8,128,128]{2,1,0:T(8,128)S(1)} custom-call(s32[8,16]{1,0:T(8,128)S(1)} %fusion.1.row_ref, f32[16512,128]{1,0:T(8,128)S(1)} %copy-done.9, f32[16,8,128,128]{3,2,1,0:T(8,128)S(1)} %copy-done.4, f32[16,8,128,128]{3,2,1,0:T(8,128)S(1)} %bitcast.70, f32[8,128,128]{2,1,0:T(8,128)S(1)} %get-tuple-element.52.mask_ref), custom_call_target="tpu_custom_call" | custom-call | flops 2147483648 | bytes 25165824 | tf_op jit(solution)/shard_map/pallas_call | solution.py:117
  389.6 1.8 multiply_reduce_fusion.1
  391.4 39.1 %all-reduce.3 = (f32[]{:T(128)}, f32[]{:T(128)}) all-reduce(f32[]{:T(128)} %get-tuple-element.44, f32[]{:T(128)} %get-tuple-element.43), channel_id=1, replica_groups=mesh['chain'=8,'sector'=16] {'sector'}, use_global_device_ids=true, to_apply=%region_13.14 | all-reduce | flops 2 | bytes 16 | tf_op jit(solution)/shard_map/psum | solution.py:211
  (60 shorter events, 20.8 us)
Async XLA Ops:
  7.2 1.4 copy-start
  7.2 82.1 %all-gather.4.cloned.1.call-start = ((), (), s32[]{:S(2)}) async-start(), calls=%async_computation | async-start | bytes 8982528 | tf_op jit(solution)/shard_map/all_gather | solution.py:176
  15.5 228.4 %all-gather.6.cloned.1.call-start = ((), (), s32[]{:S(2)}) async-start(), calls=%async_computation.1 | async-start | bytes 8982528 | tf_op jit(solution)/shard_map/all_gather | solution.py:176
  15.5 3.4 copy-start.8
  18.9 1.0 copy-start.12
  20.0 13.4 %copy-start.15 = (s32[128,16]{0,1:T(8,128)S(1)}, s32[128,16]{0,1:T(8,128)}, u32[]{:S(2)}) copy-start(s32[128,16]{0,1:T(8,128)} %param.19) | copy-start | bytes 24580
  20.0 14.1 %copy-start.13 = (s32[128]{0:T(128)S(1)}, s32[128]{0:T(128)}, u32[]{:S(2)}) copy-start(s32[128]{0:T(128)} %param.18) | copy-start | bytes 1540
  28.8 14.4 %collective-permute-start = (f32[16,8,128,128]{3,2,1,0:T(8,128)}, f32[16,8,128,128]{3,2,1,0:T(8,128)}, u32[]{:S(2)}, u32[]{:S(2)}) collective-permute-start(f32[16,8,128,128]{3,2,1,0:T(8,128)} %shard_map.103), channel_id=1, source_target_pairs={{0,16},{16,32},{32,48},{48,64},{64,80},{80,96},{96,112},{1,17},{17... | collective-permute-start | bytes 25165832 | tf_op jit(solution)/shard_map/ppermute | solution.py:146
  91.4 3.4 copy-start.2
  94.8 3.4 copy-start.5
  98.2 3.4 copy-start.10
  101.6 19.8 %copy-start.14 = (f32[1,8,128,128]{3,2,1,0:T(8,128)S(1)}, f32[1,8,128,128]{3,2,1,0:T(8,128)}, u32[]{:S(2)}) copy-start(f32[1,8,128,128]{3,2,1,0:T(8,128)} %param.17) | copy-start | bytes 1572868
  123.8 228.3 %all-gather.8.cloned.1.call-start = ((), (), s32[]{:S(2)}) async-start(), calls=%async_computation.2 | async-start | bytes 8982528 | tf_op jit(solution)/shard_map/all_gather | solution.py:176
  245.4 3.4 copy-start.3
  248.8 3.4 copy-start.6
  252.1 3.4 copy-start.11
  359.6 3.4 copy-start.4
  363.0 3.4 copy-start.7
  366.4 3.4 copy-start.9
  369.8 63.1 %copy-start.1 = (s32[128]{0:T(128)S(1)}, s32[128]{0:T(128)}, u32[]{:S(2)}) copy-start(s32[128]{0:T(128)} %param.20) | copy-start | bytes 1540
Sparse Core Ops, SparseCore 0:
  15.6 73.6 all-gather.3
  123.9 119.9 all-gather.5
  281.3 70.7 all-gather.7

commit v2 on v1

v2 whole, which is shorter than its diff:
```python
import functools

import jax
import jax.numpy as jnp
from jax import lax
from jax.experimental import pallas as pl
from jax.experimental.pallas import tpu as pltpu
from jax.sharding import PartitionSpec as P

MIB = 1 << 20
TAIL = 8
PARTS = 4
SIDE = 4
ORDERS = ((("y", 1), ("y", 3), ("z", 1), ("z", 3)), (("y", 3), ("y", 1), ("z", 3), ("z", 1)),
          (("z", 1), ("z", 3), ("y", 1), ("y", 3)), (("z", 3), ("z", 1), ("y", 3), ("y", 1)))


def split(value):
    high = value.astype(jnp.bfloat16)
    low = (value - high.astype(jnp.float32)).astype(jnp.bfloat16)
    return high, low


def dot(left, right):
    return jnp.dot(left, right, preferred_element_type=jnp.float32)


def right_factor(high, low):
    top = jnp.concatenate([high, low], axis=1)
    bottom = jnp.concatenate([high, jnp.zeros_like(low)], axis=1)
    return jnp.concatenate([top, bottom], axis=0)


def folded(value):
    half = value.shape[1] // 2
    return value[:, :half] + value[:, half:]


def update_kernel(left_ref, site_ref, out_ref):
    terms, _, blk, _ = left_ref.shape
    site = site_ref[0]
    factor = right_factor(*split(site))
    high, low = split(site.T)
    outer = jnp.concatenate([high, low, high], axis=1)
    for term in range(0, terms, 2):
        tops = []
        for index in (term, term + 1):
            first = jnp.concatenate(split(left_ref[index, 0]), axis=1)
            half_high, half_low = split(folded(dot(first, factor)))
            tops.append(jnp.concatenate([half_high, half_high, half_low], axis=0))
        both = dot(outer, jnp.concatenate(tops, axis=1))
        out_ref[term, 0] = both[:, :blk]
        out_ref[term + 1, 0] = both[:, blk:]


def update(left, site):
    terms, slots, blk, _ = left.shape
    return pl.pallas_call(
        update_kernel,
        out_shape=jax.ShapeDtypeStruct(left.shape, jnp.float32),
        grid=(slots,),
        in_specs=[
            pl.BlockSpec((terms, 1, blk, blk), lambda s: (0, s, 0, 0)),
            pl.BlockSpec((1, blk, blk), lambda s: (s, 0, 0)),
        ],
        out_specs=pl.BlockSpec((terms, 1, blk, blk), lambda s: (0, s, 0, 0)),
        compiler_params=pltpu.CompilerParams(vmem_limit_bytes=16 * MIB),
        cost_estimate=pl.CostEstimate(
            flops=8 * terms * slots * blk**3, bytes_accessed=8 * left.size, transcendentals=0
        ),
    )(left, site)


def masked(value, limit):
    rows = lax.broadcasted_iota(jnp.int32, value.shape, 0)
    columns = lax.broadcasted_iota(jnp.int32, value.shape, 1)
    return jnp.where(jnp.maximum(rows, columns) < limit, value, 0.0)


def put_quarter(slot, value, quarters):
    blk = value.shape[0]
    per = pl.num_programs(0) // PARTS
    at = pl.ds(pl.multiple_of((slot % per) * blk, blk), blk)
    for part, quarter in enumerate(quarters):
        @pl.when(slot // per == part)
        def _(quarter=quarter):
            quarter[at, :] = value


def put_sums(slot, products, tail):
    rows = [jnp.sum(product, axis=0, keepdims=True) for product in products]
    rows.append(jnp.zeros((TAIL - len(rows), rows[0].shape[1]), jnp.float32))
    block = jnp.concatenate(rows, axis=0)
    tail[...] = jnp.where(slot == 0, 0.0, tail[...]) + block


def begin_kernel(limit_ref, start_ref, full_ref, *quarters):
    slot = pl.program_id(0)
    value = masked(start_ref[0], limit_ref[slot])
    full_ref[0] = value
    put_quarter(slot, value, quarters)
    put_sums(slot, [value * value], quarters[0].at[pl.ds(quarters[0].shape[0] - TAIL, TAIL), :])


def heights(slots, blk):
    per = slots // PARTS * blk
    return [per + TAIL] + [per] * (PARTS - 1)


def whole_spec(shape):
    return pl.BlockSpec(shape, lambda s, *_: (0,) * len(shape))


def begin(limit, start):
    slots, blk, _ = start.shape
    sizes = heights(slots, blk)
    outs = pl.pallas_call(
        begin_kernel,
        out_shape=[jax.ShapeDtypeStruct(start.shape, jnp.float32)]
        + [jax.ShapeDtypeStruct((size, blk), jnp.float32) for size in sizes],
        grid_spec=pltpu.PrefetchScalarGridSpec(
            num_scalar_prefetch=1,
            grid=(slots,),
            in_specs=[pl.BlockSpec((1, blk, blk), lambda s, _: (s, 0, 0))],
            out_specs=[pl.BlockSpec((1, blk, blk), lambda s, _: (s, 0, 0))]
            + [whole_spec((size, blk)) for size in sizes],
        ),
    )(limit, start)
    return outs[0], outs[1:]


def apply_kernel(mode, rows_ref, limit_ref, coef_ref, *refs):
    pieces, refs = refs[: 2 * PARTS], refs[2 * PARTS :]
    left_ref, right_ref, refs = refs[0], refs[1], refs[2:]
    states, outs = refs[:mode], refs[mode:-3]
    blocks, inner, sems = refs[-3:]
    terms, _, blk, _ = left_ref.shape
    slot = pl.program_id(0)

    @pl.when(slot == 0)
    def _():
        copies = []
        at = 0
        for number, piece in enumerate(pieces):
            size = piece.shape[0]
            copies.append(
                pltpu.make_async_copy(piece, blocks.at[pl.ds(at, size), :], sems.at[number])
            )
            at += size
        for copy in copies:
            copy.start()
        for copy in copies:
            copy.wait()

    for term in range(terms):
        row = pl.multiple_of(rows_ref[slot, term], 8)
        first = jnp.concatenate(split(blocks[pl.ds(row, blk), :]), axis=1)
        value = folded(dot(first, right_factor(*split(right_ref[term, slot]))))
        inner[term * blk : (term + 1) * blk, :] = jnp.concatenate(split(value), axis=1)
    result = None
    for term in range(0, terms, 2):
        (high0, low0), (high1, low1) = (split(left_ref[index, slot]) for index in (term, term + 1))
        below = inner[term * blk : (term + 2) * blk, :]
        part = folded(dot(jnp.concatenate([high0, high1], axis=1), below))
        part = part + dot(jnp.concatenate([low0, low1], axis=1), below[:, :blk])
        result = part if result is None else result + part
    value = masked(result, limit_ref[slot])

    x0 = states[0][0] * coef_ref[0]
    if mode == 1:
        y0 = value * coef_ref[0]
        products = [x0 * y0]
        send = y0
    else:
        a0 = coef_ref[1]
        y0 = states[1][0]
        r1 = y0 - a0 * x0
        if mode == 2:
            z1 = value - a0 * y0
            products = [x0 * z1, r1 * y0, r1 * z1, r1 * r1]
            send = z1
        else:
            keep, turn, a1 = coef_ref[2], coef_ref[3], coef_ref[4]
            z1 = states[2][0]
            x1 = keep * x0 + turn * r1
            y1 = keep * y0 + turn * z1
            r2 = y1 - a1 * x1
            z2 = keep * (z1 + a0 * y0) + turn * value - a1 * y1
            products = [r2 * r2, r2 * z2]
            outs[0][0] = x1
            outs[1][0] = r2
            put_sums(slot, products, outs[2])
            return
    outs[0][0] = send
    put_quarter(slot, send, outs[1:])
    put_sums(slot, products, outs[1].at[pl.ds(outs[1].shape[0] - TAIL, TAIL), :])


def apply(rows, limit, coefs, pieces, left, right, states):
    mode = len(states)
    terms, slots, blk, _ = left.shape
    vector = jax.ShapeDtypeStruct((slots, blk, blk), jnp.float32)
    vector_spec = pl.BlockSpec((1, blk, blk), lambda s, *_: (s, 0, 0))
    if mode < 3:
        sizes = heights(slots, blk)
        out_shape = [vector] + [jax.ShapeDtypeStruct((size, blk), jnp.float32) for size in sizes]
        out_specs = [vector_spec] + [whole_spec((size, blk)) for size in sizes]
    else:
        out_shape = [vector, vector, jax.ShapeDtypeStruct((TAIL, blk), jnp.float32)]
        out_specs = [vector_spec, vector_spec, whole_spec((TAIL, blk))]
    total = sum(piece.shape[0] for piece in pieces)
    return pl.pallas_call(
        functools.partial(apply_kernel, mode),
        out_shape=out_shape,
        grid_spec=pltpu.PrefetchScalarGridSpec(
            num_scalar_prefetch=3,
            grid=(slots,),
            in_specs=[pl.BlockSpec(memory_space=pl.ANY)] * len(pieces)
            + [pl.BlockSpec(memory_space=pltpu.VMEM)] * 2
            + [vector_spec] * mode,
            out_specs=out_specs,
            scratch_shapes=[
                pltpu.VMEM((total, blk), jnp.float32),
                pltpu.VMEM((terms * blk, 2 * blk), jnp.bfloat16),
                pltpu.SemaphoreType.DMA((len(pieces),)),
            ],
        ),
        compiler_params=pltpu.CompilerParams(vmem_limit_bytes=20 * MIB),
        cost_estimate=pl.CostEstimate(
            flops=8 * terms * slots * blk**3, bytes_accessed=8 * left.size, transcendentals=0
        ),
    )(rows, limit, coefs, *pieces, left, right, *states)


def partner(index, move):
    axis, flip = move
    z, y = index // SIDE, index % SIDE
    return z * SIDE + (y ^ flip) if axis == "y" else (z ^ flip) * SIDE + y


def swap(value, move, count):
    return lax.ppermute(value, "sector", [(index, partner(index, move)) for index in range(count)])


def gather(quarters, count):
    held = list(quarters)
    for step in range(len(ORDERS[0])):
        came = [swap(value, order[step], count) for value, order in zip(held, ORDERS)]
        if step == len(ORDERS[0]) - 1:
            return [piece for pair in zip(held, came) for piece in pair]
        held = [jnp.concatenate(pair, axis=0) for pair in zip(held, came)]


def place_of(apart, flips):
    first, second = flips
    both = first ^ second
    return jnp.where(apart == first, 1, jnp.where(apart == second, 2, jnp.where(apart == both, 3, 0)))


def block_rows(source, owner, sdev, blk):
    device, slot = source // sdev, source % sdev
    apart = device ^ owner
    apart = {"z": apart // SIDE, "y": apart % SIDE}
    per = sdev // PARTS
    sizes = heights(sdev, blk)
    rows = jnp.zeros_like(source)
    base = 0
    for part, order in enumerate(ORDERS):
        (near, one), (_, two), (far, three), (_, four) = order
        unit = place_of(apart[near], (one, two)) + SIDE * place_of(apart[far], (three, four))
        here = base + unit * sizes[part] + (slot % per) * blk
        rows = jnp.where(slot // per == part, here, rows)
        base += SIDE * SIDE * sizes[part]
    return rows


def passed_along(value, axis, steps):
    count = lax.axis_size(axis)
    leading, last = (max(0, -steps), min(count, count - steps))
    return lax.ppermute(value, axis, [(source, source + steps) for source in range(leading, last)])


def mix(a, b2, rz):
    b = jnp.sqrt(b2)
    d = rz / b2
    lam = (a + d) / 2 - jnp.sqrt(((a - d) / 2) ** 2 + b2)
    q = lam - a
    n = jnp.sqrt(b2 + q * q)
    return lam, b / n, (q / b) / n


def body(left_env, right_env, site_block, start_vec, slot_sector, couple, dims, kept):
    lenv = left_env[0]
    renv = right_env[0]
    site = site_block[0]
    start = start_vec[0]
    sdev = start.shape[0]
    blk = start.shape[1]
    nsec = slot_sector.shape[0]
    devices = nsec // sdev
    owner = lax.axis_index("sector")
    slots = owner * sdev + jnp.arange(sdev, dtype=jnp.int32)
    sector_ids = jnp.take(slot_sector, slots)
    limit = dims[sector_ids] * kept[sector_ids]
    inverse = jnp.zeros((nsec,), jnp.int32).at[slot_sector].set(jnp.arange(nsec, dtype=jnp.int32))
    rows = block_rows(inverse[couple[sector_ids]], owner, sdev, blk)

    def totals(pieces, number):
        size = heights(sdev, blk)[0]
        tails = [piece.reshape(-1, size, blk)[:, size - TAIL : size - TAIL + number] for piece in pieces[:2]]
        found = jnp.sum(tails[0] + tails[1], axis=(0, 2))
        return [found[k] for k in range(number)]

    def coefs(*values):
        return jnp.stack(values + (jnp.float32(0),) * (8 - len(values)))

    updated = update(lenv, site)
    arrived = passed_along(updated, "chain", 1)
    luse = jnp.where(lax.axis_index("chain") == 0, lenv, arrived)
    luse = pltpu.with_memory_space_constraint(luse, pltpu.VMEM)
    ruse = pltpu.with_memory_space_constraint(renv, pltpu.VMEM)

    k0, quarters = begin(limit, start)
    pieces = gather(quarters, devices)
    (norm,) = totals(pieces, 1)
    scale = 1.0 / jnp.sqrt(norm + 1e-06)
    y0, *quarters = apply(rows, limit, coefs(scale), pieces, luse, ruse, [k0])
    pieces = gather(quarters, devices)
    (a0,) = totals(pieces, 1)
    z1, *quarters = apply(rows, limit, coefs(scale, a0), pieces, luse, ruse, [k0, y0])
    pieces = gather(quarters, devices)
    xz, ry, rz, rr = totals(pieces, 4)
    _, keep, turn = mix(a0, rr + 1e-06, rz)
    a1 = keep * keep * a0 + keep * turn * (xz + ry) + turn * turn * rz
    x1, r2, sums = apply(
        rows, limit, coefs(scale, a0, keep, turn, a1), pieces, luse, ruse, [k0, y0, z1]
    )
    for move in ORDERS[0]:
        sums = sums + swap(sums, move, devices)
    sums = jnp.sum(sums, axis=1)
    lam, keep, turn = mix(a1, sums[0] + 1e-06, sums[1])
    x2 = keep * x1 + turn * r2
    return (x2[None], updated[None], jnp.reshape(lam, (1,)))


def solution(mesh):
    placed = (
        P("chain", None, "sector", None, None),
        P("chain", None, "sector", None, None),
        P("chain", "sector", None, None),
        P("chain", "sector", None, None),
        P(),
        P(),
        P(),
        P(),
    )
    return jax.shard_map(
        body,
        mesh=mesh,
        in_specs=placed,
        out_specs=(
            P("chain", "sector", None, None),
            P("chain", None, "sector", None, None),
            P("chain"),
        ),
        check_vma=False,
    )
```

time: 442 us -> 314 us (0.71)
  waiting for transfers between devices: 234 us -> 128 us
  starting transfers between devices: 4.63 us -> 67.1 us
  blocking collectives: 39.1 us -> 0 us
  Pallas kernels: 68.4 us -> 43.9 us
  between operations: 23.2 us -> 10.5 us
  other arithmetic: 25.8 us -> 15.2 us
    all_gather x3 -> x0, waiting for transfers between devices: 227 us -> none  [gather(): whole = lax.all_gather(packed, 'sector', axis=0, tiled=True)]
    ppermute x0 -> x52, waiting for transfers between devices: none -> 128 us  [swap(): lax.ppermute(value, 'sector', [(index, partner(index, move)) for index in...]
    ppermute x0 -> x52, starting transfers between devices: none -> 62.4 us  [swap(): lax.ppermute(value, 'sector', [(index, partner(index, move)) for index in...]
    psum x1 -> x0, blocking collectives: 39.1 us -> none  [body(): rr, rz = lax.psum((inner(r2, r2), inner(r2, z2)), 'sector')]
    pallas_call x3 -> x4, Pallas kernels: 59.5 us -> 35.1 us  [the longest x3 29.4 us: apply(): pl.pallas_call(functools.partial(apply_kernel, mode), out_shape=out_shape...]
    ppermute x1, waiting for transfers between devices: 6.79 us -> 0.01 us  [passed_along(): lax.ppermute(value, axis, [(source, source + steps) for source in range(l...]
    reduce_sum x6 -> x4, other arithmetic: 8.11 us -> 1.53 us  [the longest x3 1.41 us: totals(): found = jnp.sum(tails[0] + tails[1], axis=(0, 2))]
    concatenate x0 -> x12, local copies, waits for them, and re-layouts: none -> 5.26 us  [gather(): held = [jnp.concatenate(pair, axis=0) for pair in zip(held, came)]]
  transfers between devices with their start and end apart: 4 -> 53, of which waited for: 4 -> 25; matrix products, arithmetic and copies ran while one was open for 3% -> 12% of each run, Pallas kernels for 2% -> 2%
where the time goes in v2:
time: 314 us; the launch traced here: 313 us
  waiting for transfers between devices  128 us (41%)
  starting transfers between devices  67.1 us (21%)
  local copies, waits for them, and re-layouts  48.3 us (15%)
  Pallas kernels  43.9 us (14%)
  other arithmetic  15.2 us (5%)
  between operations  10.5 us (3%)
    ppermute x52, waiting for transfers between devices, swap(): lax.ppermute(value, 'sector', [(index, partner(index, move)) for index in...  128 us
    ppermute x52, starting transfers between devices, swap(): lax.ppermute(value, 'sector', [(index, partner(index, move)) for index in...  62.4 us
    unnamed x92, local copies, waits for them, and re-layouts  36.1 us
    pallas_call x3, Pallas kernels, apply(): pl.pallas_call(functools.partial(apply_kernel, mode), out_shape=out_shape...  29.4 us
    select_n x1, other arithmetic, body(): luse = jnp.where(lax.axis_index('chain') == 0, lenv, arrived)  9.59 us
    pallas_call x1, Pallas kernels, update(): pl.pallas_call(update_kernel, out_shape=jax.ShapeDtypeStruct(left.shape,...  8.86 us
  transfers between devices with their start and end apart: 53, of which 25 were waited for; matrix products, arithmetic and copies ran while one was open for 12% of the time, Pallas kernels for 2%

profile of v2, /device:TPU:0, one launch (start us, length us, event | category | flops | bytes accessed | tf_op | source)
XLA Modules:
  0.0 313.1 jit_solution(7322246575345861660)
XLA Ops:
  5.1 8.9 %shard_map.104 = f32[16,8,128,128]{3,2,1,0:T(8,128)} custom-call(f32[16,8,128,128]{3,2,1,0:T(8,128)S(1)} %bitcast.43, f32[8,128,128]{2,1,0:T(8,128)S(1)} %bitcast.50), custom_call_target="tpu_custom_call" | custom-call | flops 2147483648 | bytes 16777216 | tf_op jit(solution)/shard_map/pallas_call | solution.py:58
  13.9 4.7 %collective-permute-start.16 = (f32[16,8,128,128]{3,2,1,0:T(8,128)}, f32[16,8,128,128]{3,2,1,0:T(8,128)}, u32[]{:S(2)}, u32[]{:S(2)}) collective-permute-start(f32[16,8,128,128]{3,2,1,0:T(8,128)} %shard_map.104), channel_id=1, source_target_pairs={{0,16},{16,32},{32,48},{48,64},{64,80},{80,96},{96,112},{1,17},{17... | collective-permute-start | bytes 25165832 | tf_op jit(solution)/shard_map/ppermute | solution.py:280
  21.2 5.7 %shard_map.103 = (f32[8,128,128]{2,1,0:T(8,128)}, f32[264,128]{1,0:T(8,128)}, f32[256,128]{1,0:T(8,128)}, f32[256,128]{1,0:T(8,128)}, f32[256,128]{1,0:T(8,128)}) custom-call(s32[8]{0:T(128)} %mul.86.limit_ref, f32[8,128,128]{2,1,0:T(8,128)} %bitcast.52), custom_call_target="tpu_custom_call" | custom-call | tf_op jit(solution)/shard_map/pallas_call | solution.py:117
  26.8 3.6 %collective-permute-start.4 = (f32[256,128]{1,0:T(8,128)}, f32[256,128]{1,0:T(8,128)S(1)}, u32[]{:S(2)}, u32[]{:S(2)}) collective-permute-start(f32[256,128]{1,0:T(8,128)} %get-tuple-element.22), channel_id=1, source_target_pairs={{0,3},{1,2},{2,1},{3,0},{4,7},{5,6},{6,5},{7,4},{8,11},{9,10},{10,... | collective-permute-start | bytes 393224 | tf_op jit(solution)/shard_map/ppermute | solution.py:242
  43.0 4.9 %collective-permute-done.1 = f32[528,128]{1,0:T(8,128)S(1)} collective-permute-done((f32[528,128]{1,0:T(8,128)S(1)}, f32[528,128]{1,0:T(8,128)S(1)}, u32[]{:S(2)}, u32[]{:S(2)}) %collective-permute-start.1) | collective-permute-done | bytes 270368 | tf_op jit(solution)/shard_map/ppermute | solution.py:242
  51.1 9.6 %collective-permute-done.2 = f32[1056,128]{1,0:T(8,128)S(1)} collective-permute-done((f32[1056,128]{1,0:T(8,128)S(1)}, f32[1056,128]{1,0:T(8,128)S(1)}, u32[]{:S(2)}, u32[]{:S(2)}) %collective-permute-start.2) | collective-permute-done | bytes 540704 | tf_op jit(solution)/shard_map/ppermute | solution.py:242
  67.8 5.7 %collective-permute-done.14 = f32[1024,128]{1,0:T(8,128)S(1)} collective-permute-done((f32[1024,128]{1,0:T(8,128)S(1)}, f32[1024,128]{1,0:T(8,128)S(1)}, u32[]{:S(2)}, u32[]{:S(2)}) %collective-permute-start.14) | collective-permute-done | bytes 524320 | tf_op jit(solution)/shard_map/ppermute | solution.py:242
  78.6 17.9 %collective-permute-done.6 = f32[1024,128]{1,0:T(8,128)S(1)} collective-permute-done((f32[1024,128]{1,0:T(8,128)S(1)}, f32[1024,128]{1,0:T(8,128)S(1)}, u32[]{:S(2)}, u32[]{:S(2)}) %collective-permute-start.6) | collective-permute-done | bytes 524320 | tf_op jit(solution)/shard_map/ppermute | solution.py:242
  100.0 9.6 %broadcast_select_fusion.refs_8_ = f32[16,8,128,128]{3,2,1,0:T(8,128)} fusion(f32[16,8,128,128]{3,2,1,0:T(8,128)} %collective-permute-done.16, pred[]{:T(512)S(6)} %eq.68, f32[1,16,8,128,128]{4,3,2,1,0:T(8,128)} %param.8), kind=kLoop, calls=%fused_computation.6 | loop fusion | flops 2097152 | bytes 25165824 | tf_op jit(solution)/shard_map/jit(_where)/select_n | solution.py:319
  109.6 10.0 %collective-permute-done.7.refs_3_ = f32[2048,128]{1,0:T(8,128)} collective-permute-done((f32[2048,128]{1,0:T(8,128)}, f32[2048,128]{1,0:T(8,128)}, u32[]{:S(2)}, u32[]{:S(2)}) %collective-permute-start.7) | collective-permute-done | bytes 1048608 | tf_op jit(solution)/shard_map/ppermute | solution.py:242
  119.5 3.4 %copy-done.2 = f32[16,8,128,128]{3,2,1,0:T(8,128)S(1)} copy-done((f32[16,8,128,128]{3,2,1,0:T(8,128)S(1)}, f32[16,8,128,128]{3,2,1,0:T(8,128)}, u32[]{:S(2)}) %copy-start.2) | copy-done | bytes 8388632
  122.9 3.4 %copy-done.5 = f32[1,16,8,128,128]{4,3,2,1,0:T(8,128)S(1)} copy-done((f32[1,16,8,128,128]{4,3,2,1,0:T(8,128)S(1)}, f32[1,16,8,128,128]{4,3,2,1,0:T(8,128)}, u32[]{:S(2)}) %copy-start.5) | copy-done | bytes 8388632
  127.5 10.8 %shard_map.105 = (f32[8,128,128]{2,1,0:T(8,128)S(1)}, f32[264,128]{1,0:T(8,128)S(1)}, f32[256,128]{1,0:T(8,128)S(1)}, f32[256,128]{1,0:T(8,128)S(1)}, f32[256,128]{1,0:T(8,128)S(1)}) custom-call(s32[8,16]{1,0:T(8,128)S(1)} %select_select_fusion.4.rows_ref, s32[8]{0:T(128)S(1)} %copy-done.18, f32[8]{0:T(128)S(1)} %pad_maximum_fusion.25.coef_ref, ...), custom_call_target="tpu_custom_call" | custom-call | flops 2147483648 | bytes 16777216 | tf_op jit(solution)/shard_map/pallas_call | solution.py:212
  139.7 6.2 %collective-permute-done.21 = f32[256,128]{1,0:T(8,128)S(1)} collective-permute-done((f32[256,128]{1,0:T(8,128)S(1)}, f32[256,128]{1,0:T(8,128)S(1)}, u32[]{:S(2)}, u32[]{:S(2)}) %collective-permute-start.21) | collective-permute-done | bytes 131104 | tf_op jit(solution)/shard_map/ppermute | solution.py:242
  149.3 5.3 %collective-permute-done.22 = f32[512,128]{1,0:T(8,128)S(1)} collective-permute-done((f32[512,128]{1,0:T(8,128)S(1)}, f32[512,128]{1,0:T(8,128)S(1)}, u32[]{:S(2)}, u32[]{:S(2)}) %collective-permute-start.22) | collective-permute-done | bytes 262176 | tf_op jit(solution)/shard_map/ppermute | solution.py:242
  160.9 12.0 %collective-permute-done.19 = f32[1056,128]{1,0:T(8,128)S(1)} collective-permute-done((f32[1056,128]{1,0:T(8,128)S(1)}, f32[1056,128]{1,0:T(8,128)S(1)}, u32[]{:S(2)}, u32[]{:S(2)}) %collective-permute-start.19) | collective-permute-done | bytes 540704 | tf_op jit(solution)/shard_map/ppermute | solution.py:242
  179.3 19.7 %collective-permute-done.20.refs_1_ = f32[2112,128]{1,0:T(8,128)S(1)} collective-permute-done((f32[2112,128]{1,0:T(8,128)S(1)}, f32[2112,128]{1,0:T(8,128)S(1)}, u32[]{:S(2)}, u32[]{:S(2)}) %collective-permute-start.20) | collective-permute-done | bytes 1081376 | tf_op jit(solution)/shard_map/ppermute | solution.py:242
  202.1 8.3 %shard_map.106 = (f32[8,128,128]{2,1,0:T(8,128)S(1)}, f32[264,128]{1,0:T(8,128)S(1)}, f32[256,128]{1,0:T(8,128)S(1)}, f32[256,128]{1,0:T(8,128)S(1)}, f32[256,128]{1,0:T(8,128)S(1)}) custom-call(s32[8,16]{1,0:T(8,128)S(1)} %select_select_fusion.4.rows_ref, s32[8]{0:T(128)S(1)} %copy-done.18, f32[8]{0:T(128)S(1)} %pad_maximum_fusion.24.coef_ref, ...), custom_call_target="tpu_custom_call" | custom-call | flops 2147483648 | bytes 16777216 | tf_op jit(solution)/shard_map/pallas_call | solution.py:212
  232.3 3.5 %collective-permute-start.35 = (f32[1056,128]{1,0:T(8,128)S(1)}, f32[1056,128]{1,0:T(8,128)S(1)}, u32[]{:S(2)}, u32[]{:S(2)}) collective-permute-start(f32[1056,128]{1,0:T(8,128)S(1)} %pad_maximum_fusion.2), channel_id=1, source_target_pairs={{0,4},{1,5},{2,6},{3,7},{4,0},{5,1},{6,2},{7,3},{8,12},{9,13},{10,... | collective-permute-start | bytes 1622024 | tf_op jit(solution)/shard_map/ppermute | solution.py:242
  238.4 4.7 %collective-permute-done.35 = f32[1056,128]{1,0:T(8,128)S(1)} collective-permute-done((f32[1056,128]{1,0:T(8,128)S(1)}, f32[1056,128]{1,0:T(8,128)S(1)}, u32[]{:S(2)}, u32[]{:S(2)}) %collective-permute-start.35) | collective-permute-done | bytes 540704 | tf_op jit(solution)/shard_map/ppermute | solution.py:242
  244.4 3.9 %collective-permute-done.47 = f32[1024,128]{1,0:T(8,128)S(1)} collective-permute-done((f32[1024,128]{1,0:T(8,128)S(1)}, f32[1024,128]{1,0:T(8,128)S(1)}, u32[]{:S(2)}, u32[]{:S(2)}) %collective-permute-start.47) | collective-permute-done | bytes 524320 | tf_op jit(solution)/shard_map/ppermute | solution.py:242
  254.5 8.0 %collective-permute-done.36.refs_1_ = f32[2112,128]{1,0:T(8,128)S(1)} collective-permute-done((f32[2112,128]{1,0:T(8,128)S(1)}, f32[2112,128]{1,0:T(8,128)S(1)}, u32[]{:S(2)}, u32[]{:S(2)}) %collective-permute-start.36) | collective-permute-done | bytes 1081376 | tf_op jit(solution)/shard_map/ppermute | solution.py:242
  274.2 3.4 %copy-done.6 = f32[1,16,8,128,128]{4,3,2,1,0:T(8,128)S(1)} copy-done((f32[1,16,8,128,128]{4,3,2,1,0:T(8,128)S(1)}, f32[1,16,8,128,128]{4,3,2,1,0:T(8,128)}, u32[]{:S(2)}) %copy-start.6) | copy-done | bytes 8388632
  278.8 10.3 %shard_map.107 = (f32[8,128,128]{2,1,0:T(8,128)S(1)}, f32[8,128,128]{2,1,0:T(8,128)S(1)}, f32[8,128]{1,0:T(8,128)S(1)}) custom-call(s32[8,16]{1,0:T(8,128)S(1)} %select_select_fusion.4.rows_ref, s32[8]{0:T(128)S(1)} %copy-done.18, f32[8]{0:T(128)S(1)} %stack.29.coef_ref, f32[2112,128]{1,0:T(8,128)S(1)} %constant_dynamic-update-slice_fusion.32.refs_0_, ...), custom_call_target="tpu_custom_call" | custom-call | flops 2147483648 | bytes 16777216 | tf_op jit(solution)/shard_map/pallas_call | solution.py:212
  (250 shorter events, 119.2 us)
Async XLA Ops:
  13.9 86.0 %collective-permute-start.16 = (f32[16,8,128,128]{3,2,1,0:T(8,128)}, f32[16,8,128,128]{3,2,1,0:T(8,128)}, u32[]{:S(2)}, u32[]{:S(2)}) collective-permute-start(f32[16,8,128,128]{3,2,1,0:T(8,128)} %shard_map.104), channel_id=1, source_target_pairs={{0,16},{16,32},{32,48},{48,64},{64,80},{80,96},{96,112},{1,17},{17... | collective-permute-start | bytes 25165832 | tf_op jit(solution)/shard_map/ppermute | solution.py:280
  26.8 14.0 %collective-permute-start.4 = (f32[256,128]{1,0:T(8,128)}, f32[256,128]{1,0:T(8,128)S(1)}, u32[]{:S(2)}, u32[]{:S(2)}) collective-permute-start(f32[256,128]{1,0:T(8,128)} %get-tuple-element.22), channel_id=1, source_target_pairs={{0,3},{1,2},{2,1},{3,0},{4,7},{5,6},{6,5},{7,4},{8,11},{9,10},{10,... | collective-permute-start | bytes 393224 | tf_op jit(solution)/shard_map/ppermute | solution.py:242
  40.8 24.0 %collective-permute-start.5 = (f32[512,128]{1,0:T(8,128)S(1)}, f32[512,128]{1,0:T(8,128)S(1)}, u32[]{:S(2)}, u32[]{:S(2)}) collective-permute-start(f32[512,128]{1,0:T(8,128)S(1)} %pad_maximum_fusion.15), channel_id=1, source_target_pairs={{0,1},{1,0},{2,3},{3,2},{4,5},{5,4},{6,7},{7,6},{8,9},{9,8},{10,11... | collective-permute-start | bytes 786440 | tf_op jit(solution)/shard_map/ppermute | solution.py:242
  41.8 22.6 %collective-permute-start.9 = (f32[512,128]{1,0:T(8,128)S(1)}, f32[512,128]{1,0:T(8,128)S(1)}, u32[]{:S(2)}, u32[]{:S(2)}) collective-permute-start(f32[512,128]{1,0:T(8,128)S(1)} %pad_maximum_fusion.16), channel_id=1, source_target_pairs={{0,12},{1,13},{2,14},{3,15},{4,8},{5,9},{6,10},{7,11},{8,4},{9,5},... | collective-permute-start | bytes 786440 | tf_op jit(solution)/shard_map/ppermute | solution.py:242
  42.6 19.4 %collective-permute-start.13 = (f32[512,128]{1,0:T(8,128)S(1)}, f32[512,128]{1,0:T(8,128)S(1)}, u32[]{:S(2)}, u32[]{:S(2)}) collective-permute-start(f32[512,128]{1,0:T(8,128)S(1)} %pad_maximum_fusion.17), channel_id=1, source_target_pairs={{0,4},{1,5},{2,6},{3,7},{4,0},{5,1},{6,2},{7,3},{8,12},{9,13},{10,... | collective-permute-start | bytes 786440 | tf_op jit(solution)/shard_map/ppermute | solution.py:242
  60.7 36.7 %collective-permute-start.3 = (f32[2112,128]{1,0:T(8,128)S(1)}, f32[2112,128]{1,0:T(8,128)S(1)}, u32[]{:S(2)}, u32[]{:S(2)}) collective-permute-start(f32[2112,128]{1,0:T(8,128)S(1)} %constant_dynamic-update-slice_fusion.refs_0_), channel_id=1, source_target_pairs={{0,12},{1,13},{2,14},{3,15},{4,8},{5,9},{6,10},{7,11},{8,4},{9,5},... | collective-permute-start | bytes 3244040 | tf_op jit(solution)/shard_map/ppermute | solution.py:242
  64.9 31.7 %collective-permute-start.6 = (f32[1024,128]{1,0:T(8,128)S(1)}, f32[1024,128]{1,0:T(8,128)S(1)}, u32[]{:S(2)}, u32[]{:S(2)}) collective-permute-start(f32[1024,128]{1,0:T(8,128)S(1)} %pad_maximum_fusion.3), channel_id=1, source_target_pairs={{0,12},{1,13},{2,14},{3,15},{4,8},{5,9},{6,10},{7,11},{8,4},{9,5},... | collective-permute-start | bytes 1572872 | tf_op jit(solution)/shard_map/ppermute | solution.py:242
  74.4 35.2 %collective-permute-start.15 = (f32[2048,128]{1,0:T(8,128)}, f32[2048,128]{1,0:T(8,128)}, u32[]{:S(2)}, u32[]{:S(2)}) collective-permute-start(f32[2048,128]{1,0:T(8,128)} %constant_dynamic-update-slice_fusion.12.refs_6_), channel_id=1, source_target_pairs={{0,1},{1,0},{2,3},{3,2},{4,5},{5,4},{6,7},{7,6},{8,9},{9,8},{10,11... | collective-permute-start | bytes 3145736 | tf_op jit(solution)/shard_map/ppermute | solution.py:242
  75.6 34.0 %collective-permute-start.11 = (f32[2048,128]{1,0:T(8,128)}, f32[2048,128]{1,0:T(8,128)}, u32[]{:S(2)}, u32[]{:S(2)}) collective-permute-start(f32[2048,128]{1,0:T(8,128)} %constant_dynamic-update-slice_fusion.8.refs_4_), channel_id=1, source_target_pairs={{0,3},{1,2},{2,1},{3,0},{4,7},{5,6},{6,5},{7,4},{8,11},{9,10},{10,... | collective-permute-start | bytes 3145736 | tf_op jit(solution)/shard_map/ppermute | solution.py:242
  97.4 22.1 %collective-permute-start.7 = (f32[2048,128]{1,0:T(8,128)}, f32[2048,128]{1,0:T(8,128)}, u32[]{:S(2)}, u32[]{:S(2)}) collective-permute-start(f32[2048,128]{1,0:T(8,128)} %constant_dynamic-update-slice_fusion.4.refs_2_), channel_id=1, source_target_pairs={{0,4},{1,5},{2,6},{3,7},{4,0},{5,1},{6,2},{7,3},{8,12},{9,13},{10,... | collective-permute-start | bytes 3145736 | tf_op jit(solution)/shard_map/ppermute | solution.py:242
  154.6 23.5 %collective-permute-start.23 = (f32[1024,128]{1,0:T(8,128)S(1)}, f32[1024,128]{1,0:T(8,128)S(1)}, u32[]{:S(2)}, u32[]{:S(2)}) collective-permute-start(f32[1024,128]{1,0:T(8,128)S(1)} %pad_maximum_fusion.6), channel_id=1, source_target_pairs={{0,12},{1,13},{2,14},{3,15},{4,8},{5,9},{6,10},{7,11},{8,4},{9,5},... | collective-permute-start | bytes 1572872 | tf_op jit(solution)/shard_map/ppermute | solution.py:242
  156.1 19.5 %collective-permute-start.27 = (f32[1024,128]{1,0:T(8,128)S(1)}, f32[1024,128]{1,0:T(8,128)S(1)}, u32[]{:S(2)}, u32[]{:S(2)}) collective-permute-start(f32[1024,128]{1,0:T(8,128)S(1)} %pad_maximum_fusion.7), channel_id=1, source_target_pairs={{0,1},{1,0},{2,3},{3,2},{4,5},{5,4},{6,7},{7,6},{8,9},{9,8},{10,11... | collective-permute-start | bytes 1572872 | tf_op jit(solution)/shard_map/ppermute | solution.py:242
  158.8 14.1 %collective-permute-start.19 = (f32[1056,128]{1,0:T(8,128)S(1)}, f32[1056,128]{1,0:T(8,128)S(1)}, u32[]{:S(2)}, u32[]{:S(2)}) collective-permute-start(f32[1056,128]{1,0:T(8,128)S(1)} %pad_maximum_fusion.1), channel_id=1, source_target_pairs={{0,4},{1,5},{2,6},{3,7},{4,0},{5,1},{6,2},{7,3},{8,12},{9,13},{10,... | collective-permute-start | bytes 1622024 | tf_op jit(solution)/shard_map/ppermute | solution.py:242
  159.0 15.1 %collective-permute-start.31 = (f32[1024,128]{1,0:T(8,128)S(1)}, f32[1024,128]{1,0:T(8,128)S(1)}, u32[]{:S(2)}, u32[]{:S(2)}) collective-permute-start(f32[1024,128]{1,0:T(8,128)S(1)} %pad_maximum_fusion.8), channel_id=1, source_target_pairs={{0,3},{1,2},{2,1},{3,0},{4,7},{5,6},{6,5},{7,4},{8,11},{9,10},{10,... | collective-permute-start | bytes 1572872 | tf_op jit(solution)/shard_map/ppermute | solution.py:242
  173.0 26.0 %collective-permute-start.20 = (f32[2112,128]{1,0:T(8,128)S(1)}, f32[2112,128]{1,0:T(8,128)S(1)}, u32[]{:S(2)}, u32[]{:S(2)}) collective-permute-start(f32[2112,128]{1,0:T(8,128)S(1)} %constant_dynamic-update-slice_fusion.16.refs_0_), channel_id=1, source_target_pairs={{0,12},{1,13},{2,14},{3,15},{4,8},{5,9},{6,10},{7,11},{8,4},{9,5},... | collective-permute-start | bytes 3244040 | tf_op jit(solution)/shard_map/ppermute | solution.py:242
  174.1 26.2 %collective-permute-start.32 = (f32[2048,128]{1,0:T(8,128)S(1)}, f32[2048,128]{1,0:T(8,128)S(1)}, u32[]{:S(2)}, u32[]{:S(2)}) collective-permute-start(f32[2048,128]{1,0:T(8,128)S(1)} %constant_dynamic-update-slice_fusion.28.refs_6_), channel_id=1, source_target_pairs={{0,1},{1,0},{2,3},{3,2},{4,5},{5,4},{6,7},{7,6},{8,9},{9,8},{10,11... | collective-permute-start | bytes 3145736 | tf_op jit(solution)/shard_map/ppermute | solution.py:242
  175.7 26.2 %collective-permute-start.28 = (f32[2048,128]{1,0:T(8,128)S(1)}, f32[2048,128]{1,0:T(8,128)S(1)}, u32[]{:S(2)}, u32[]{:S(2)}) collective-permute-start(f32[2048,128]{1,0:T(8,128)S(1)} %constant_dynamic-update-slice_fusion.24.refs_4_), channel_id=1, source_target_pairs={{0,3},{1,2},{2,1},{3,0},{4,7},{5,6},{6,5},{7,4},{8,11},{9,10},{10,... | collective-permute-start | bytes 3145736 | tf_op jit(solution)/shard_map/ppermute | solution.py:242
  178.1 23.9 %collective-permute-start.24 = (f32[2048,128]{1,0:T(8,128)S(1)}, f32[2048,128]{1,0:T(8,128)S(1)}, u32[]{:S(2)}, u32[]{:S(2)}) collective-permute-start(f32[2048,128]{1,0:T(8,128)S(1)} %constant_dynamic-update-slice_fusion.20.refs_2_), channel_id=1, source_target_pairs={{0,4},{1,5},{2,6},{3,7},{4,0},{5,1},{6,2},{7,3},{8,12},{9,13},{10,... | collective-permute-start | bytes 3145736 | tf_op jit(solution)/shard_map/ppermute | solution.py:242
  225.6 28.1 %collective-permute-start.39 = (f32[1024,128]{1,0:T(8,128)S(1)}, f32[1024,128]{1,0:T(8,128)S(1)}, u32[]{:S(2)}, u32[]{:S(2)}) collective-permute-start(f32[1024,128]{1,0:T(8,128)S(1)} %pad_maximum_fusion.9), channel_id=1, source_target_pairs={{0,12},{1,13},{2,14},{3,15},{4,8},{5,9},{6,10},{7,11},{8,4},{9,5},... | collective-permute-start | bytes 1572872 | tf_op jit(solution)/shard_map/ppermute | solution.py:242
  228.2 23.4 %collective-permute-start.43 = (f32[1024,128]{1,0:T(8,128)S(1)}, f32[1024,128]{1,0:T(8,128)S(1)}, u32[]{:S(2)}, u32[]{:S(2)}) collective-permute-start(f32[1024,128]{1,0:T(8,128)S(1)} %pad_maximum_fusion.10), channel_id=1, source_target_pairs={{0,1},{1,0},{2,3},{3,2},{4,5},{5,4},{6,7},{7,6},{8,9},{9,8},{10,11... | collective-permute-start | bytes 1572872 | tf_op jit(solution)/shard_map/ppermute | solution.py:242
  243.2 19.3 %collective-permute-start.36 = (f32[2112,128]{1,0:T(8,128)S(1)}, f32[2112,128]{1,0:T(8,128)S(1)}, u32[]{:S(2)}, u32[]{:S(2)}) collective-permute-start(f32[2112,128]{1,0:T(8,128)S(1)} %constant_dynamic-update-slice_fusion.32.refs_0_), channel_id=1, source_target_pairs={{0,12},{1,13},{2,14},{3,15},{4,8},{5,9},{6,10},{7,11},{8,4},{9,5},... | collective-permute-start | bytes 3244040 | tf_op jit(solution)/shard_map/ppermute | solution.py:242
  249.1 21.7 %collective-permute-start.48 = (f32[2048,128]{1,0:T(8,128)}, f32[2048,128]{1,0:T(8,128)}, u32[]{:S(2)}, u32[]{:S(2)}) collective-permute-start(f32[2048,128]{1,0:T(8,128)} %constant_dynamic-update-slice_fusion.44.refs_6_), channel_id=1, source_target_pairs={{0,1},{1,0},{2,3},{3,2},{4,5},{5,4},{6,7},{7,6},{8,9},{9,8},{10,11... | collective-permute-start | bytes 3145736 | tf_op jit(solution)/shard_map/ppermute | solution.py:242
  252.4 18.4 %collective-permute-start.44 = (f32[2048,128]{1,0:T(8,128)}, f32[2048,128]{1,0:T(8,128)}, u32[]{:S(2)}, u32[]{:S(2)}) collective-permute-start(f32[2048,128]{1,0:T(8,128)} %constant_dynamic-update-slice_fusion.40.refs_4_), channel_id=1, source_target_pairs={{0,3},{1,2},{2,1},{3,0},{4,7},{5,6},{6,5},{7,4},{8,11},{9,10},{10,... | collective-permute-start | bytes 3145736 | tf_op jit(solution)/shard_map/ppermute | solution.py:242
  254.5 16.2 %collective-permute-start.40 = (f32[2048,128]{1,0:T(8,128)}, f32[2048,128]{1,0:T(8,128)}, u32[]{:S(2)}, u32[]{:S(2)}) collective-permute-start(f32[2048,128]{1,0:T(8,128)} %constant_dynamic-update-slice_fusion.36.refs_2_), channel_id=1, source_target_pairs={{0,4},{1,5},{2,6},{3,7},{4,0},{5,1},{6,2},{7,3},{8,12},{9,13},{10,... | collective-permute-start | bytes 3145736 | tf_op jit(solution)/shard_map/ppermute | solution.py:242
  (57 other events, 669.7 us)

commit v3 on v2

v3 whole, which is shorter than its diff:
```python
import functools

import jax
import jax.numpy as jnp
from jax import lax
from jax.experimental import pallas as pl
from jax.experimental.pallas import tpu as pltpu
from jax.sharding import PartitionSpec as P

MIB = 1 << 20
TAIL = 8
PARTS = 4
SIDE = 4
PAIR = 2
AHEAD = 3
ORDERS = ((("y", 1), ("y", 3), ("z", 1), ("z", 3)), (("y", 3), ("y", 1), ("z", 3), ("z", 1)),
          (("z", 1), ("z", 3), ("y", 1), ("y", 3)), (("z", 3), ("z", 1), ("y", 3), ("y", 1)))


def split(value):
    high = value.astype(jnp.bfloat16)
    low = (value - high.astype(jnp.float32)).astype(jnp.bfloat16)
    return high, low


def dot(left, right):
    return jnp.dot(left, right, preferred_element_type=jnp.float32)


def right_factor(high, low):
    top = jnp.concatenate([high, low], axis=1)
    bottom = jnp.concatenate([high, jnp.zeros_like(low)], axis=1)
    return jnp.concatenate([top, bottom], axis=0)


def folded(value):
    half = value.shape[1] // 2
    return value[:, :half] + value[:, half:]


def update_kernel(left_ref, site_ref, out_ref, inner, outer):
    terms, slots, blk, _ = left_ref.shape

    @pl.when(pl.program_id(0) == 0)
    def _():
        for slot in range(slots):
            site = site_ref[slot]
            inner[slot] = right_factor(*split(site))
            high, low = split(site.T)
            outer[slot] = jnp.concatenate([high, low, high], axis=1)

    for slot in range(slots):
        first = [jnp.concatenate(split(left_ref[index, slot]), axis=1) for index in range(terms)]
        half = folded(dot(jnp.concatenate(first, axis=0), inner[slot]))
        high, low = split(half)
        columns = []
        for index in range(terms):
            rows = slice(index * blk, (index + 1) * blk)
            columns.append(jnp.concatenate([high[rows], high[rows], low[rows]], axis=0))
        both = dot(outer[slot], jnp.concatenate(columns, axis=1))
        for index in range(terms):
            value = both[:, index * blk : (index + 1) * blk]
            out_ref[index, slot] = value


def update(left, site, at, some):
    _, slots, blk, _ = left.shape
    pair = PAIR
    return pl.pallas_call(
        update_kernel,
        out_shape=jax.ShapeDtypeStruct((some, slots, blk, blk), jnp.float32),
        grid=(some // pair,),
        in_specs=[
            pl.BlockSpec((pair, slots, blk, blk), lambda t: (at // pair + t, 0, 0, 0)),
            pl.BlockSpec((slots, blk, blk), lambda t: (0, 0, 0)),
        ],
        out_specs=pl.BlockSpec((pair, slots, blk, blk), lambda t: (t, 0, 0, 0)),
        scratch_shapes=[
            pltpu.VMEM((slots, 2 * blk, 2 * blk), jnp.bfloat16),
            pltpu.VMEM((slots, blk, 3 * blk), jnp.bfloat16),
        ],
        compiler_params=pltpu.CompilerParams(vmem_limit_bytes=12 * MIB),
        cost_estimate=pl.CostEstimate(
            flops=8 * some * slots * blk**3,
            bytes_accessed=8 * some * slots * blk * blk,
            transcendentals=0,
        ),
    )(left, site)


def join_kernel(starts, *refs):
    parts, out_ref = refs[: len(starts) - 1], refs[-1]
    step = pl.program_id(0)
    for part, start, end in zip(parts, starts, starts[1:]):
        @pl.when((step >= start) & (step < end))
        def _(part=part):
            out_ref[...] = part[...]


def join(parts, after):
    shape = parts[0].shape[1:]
    starts = [0]
    for part in parts:
        starts.append(starts[-1] + part.shape[0] // PAIR)
    specs = [
        pl.BlockSpec(
            (PAIR,) + shape, lambda t, start=start, end=end: (jnp.clip(t - start, 0, end - start - 1), 0, 0, 0)
        )
        for start, end in zip(starts, starts[1:])
    ]
    return pl.pallas_call(
        functools.partial(join_kernel, starts),
        out_shape=jax.ShapeDtypeStruct((PAIR * starts[-1],) + shape, jnp.float32),
        grid=(starts[-1],),
        in_specs=specs + [pl.BlockSpec(memory_space=pl.ANY)],
        out_specs=pl.BlockSpec((PAIR,) + shape, lambda t: (t, 0, 0, 0)),
        compiler_params=pltpu.CompilerParams(vmem_limit_bytes=12 * MIB),
        cost_estimate=pl.CostEstimate(
            flops=0, bytes_accessed=8 * sum(part.size for part in parts), transcendentals=0
        ),
    )(*parts, after)


def masked(value, limit):
    rows = lax.broadcasted_iota(jnp.int32, value.shape, 0)
    columns = lax.broadcasted_iota(jnp.int32, value.shape, 1)
    return jnp.where(jnp.maximum(rows, columns) < limit, value, 0.0)


def put_quarter(slot, value, quarters):
    blk = value.shape[0]
    per = pl.num_programs(0) // PARTS
    at = pl.ds(pl.multiple_of((slot % per) * blk, blk), blk)
    for part, quarter in enumerate(quarters):
        @pl.when(slot // per == part)
        def _(quarter=quarter):
            quarter[at, :] = value


def tail_of(products):
    rows = [jnp.sum(product, axis=0, keepdims=True) for product in products]
    rows.append(jnp.zeros((TAIL - len(rows), rows[0].shape[1]), jnp.float32))
    return jnp.concatenate(rows, axis=0)


def put_sums(slot, products, tail):
    tail[...] = jnp.where(slot == 0, 0.0, tail[...]) + tail_of(products)


def begin_kernel(owner_ref, sector_ref, dims_ref, kept_ref, start_ref, full_ref, limit_ref, packed_ref):
    slots, blk, _ = start_ref.shape
    total = jnp.zeros((blk, blk), jnp.float32)
    for slot in range(slots):
        sector = sector_ref[owner_ref[0] * slots + slot]
        limit = dims_ref[sector] * kept_ref[sector]
        limit_ref[slot] = limit
        value = masked(start_ref[slot], limit)
        full_ref[slot] = value
        packed_ref[slot * blk : (slot + 1) * blk, :] = value
        total = total + value * value
    packed_ref[slots * blk :, :] = tail_of([total])


def heights(slots, blk):
    per = slots // PARTS * blk
    return [per + TAIL] + [per] * (PARTS - 1)


def whole_spec(shape):
    return pl.BlockSpec(shape, lambda s, *_: (0,) * len(shape))


def begin(owner, slot_sector, dims, kept, start):
    slots, blk, _ = start.shape
    vmem = pl.BlockSpec(memory_space=pltpu.VMEM)
    smem = pl.BlockSpec(memory_space=pltpu.SMEM)
    return pl.pallas_call(
        begin_kernel,
        out_shape=[
            jax.ShapeDtypeStruct(start.shape, jnp.float32),
            jax.ShapeDtypeStruct((slots,), jnp.int32),
        ]
        + [jax.ShapeDtypeStruct((slots * blk + TAIL, blk), jnp.float32)],
        in_specs=[smem] * 4 + [vmem],
        out_specs=[vmem, smem, vmem],
        compiler_params=pltpu.CompilerParams(vmem_limit_bytes=4 * MIB),
    )(owner, slot_sector, dims, kept, start)


def start_fetch(slot, which, lefts, right, left_copy, right_copy, sems):
    own, near, far = lefts
    pltpu.make_async_copy(right.at[:, slot], right_copy.at[:, slot], sems.at[0, slot]).start()
    for number in range(3):
        @pl.when(which == number)
        def _(number=number):
            at = 0
            for part, ref in enumerate((near, far)[number - 1] if number else near):
                here = slice(at, at + ref.shape[0])
                source = ref.at[:, slot] if number else own.at[here, slot]
                at += ref.shape[0]
                pltpu.make_async_copy(
                    source, left_copy.at[here, slot], sems.at[1 + part, slot]
                ).start()


def wait_fetch(slot, lefts, right, left_copy, right_copy, sems):
    pltpu.make_async_copy(right.at[:, slot], right_copy.at[:, slot], sems.at[0, slot]).wait()
    own, near, _ = lefts
    at = 0
    for part, ref in enumerate(near):
        here = slice(at, at + ref.shape[0])
        pltpu.make_async_copy(
            own.at[here, slot], left_copy.at[here, slot], sems.at[1 + part, slot]
        ).wait()
        at += ref.shape[0]


def mix(a, b2, rz):
    b = jnp.sqrt(b2)
    d = rz / b2
    lam = (a + d) / 2 - jnp.sqrt(((a - d) / 2) ** 2 + b2)
    q = lam - a
    n = jnp.sqrt(b2 + q * q)
    return lam, b / n, (q / b) / n


def next_coefs(mode, known, sums):
    row = lambda value, k: value[k : k + 1, :]
    total = jnp.broadcast_to(jnp.sum(sums, axis=1, keepdims=True), sums.shape)
    rows = [row(known, k) for k in range(5)]
    if mode == 1:
        rows[0] = 1.0 / jnp.sqrt(row(total, 0) + 1e-06)
    elif mode == 2:
        rows[1] = row(total, 0)
    else:
        xz, ry, rz, rr = (row(total, k) for k in range(4))
        a0 = rows[1]
        _, keep, turn = mix(a0, rr + 1e-06, rz)
        rows[2:4] = keep, turn
        rows[4] = keep * keep * a0 + keep * turn * (xz + ry) + turn * turn * rz
    rows.append(jnp.zeros((TAIL - len(rows), sums.shape[1]), jnp.float32))
    return jnp.concatenate(rows, axis=0)


def apply_kernel(mode, counts, tails, rows_ref, limit_ref, which_ref, *refs):
    refs = list(refs)
    pieces, own, near, far = ([refs.pop(0) for _ in range(count)] for count in counts)
    lefts = own[0], near, far
    right, known_ref = refs.pop(0), refs.pop(0)
    states, outs = refs[:mode], refs[mode:-6]
    blocks, left_copy, right_copy, inner, sems, piece_sems = refs[-6:]
    terms, _, blk, _ = left_copy.shape
    slot = pl.program_id(0)
    coef_ref = outs[0]
    outs = outs[1:]

    @pl.when(slot == 0)
    def _():
        copies = []
        at = 0
        for number, piece in enumerate(pieces):
            size = piece.shape[0]
            copies.append(
                pltpu.make_async_copy(piece, blocks.at[pl.ds(at, size), :], piece_sems.at[number])
            )
            at += size
        for copy in copies:
            copy.start()
        for early in range(AHEAD):
            start_fetch(early, which_ref[0], lefts, right, left_copy, right_copy, sems)
        for copy in copies:
            copy.wait()
        sums = blocks[tails[0] : tails[0] + TAIL, :]
        for tail in tails[1:]:
            sums = sums + blocks[tail : tail + TAIL, :]
        coef_ref[...] = next_coefs(mode, known_ref[...], sums)

    @pl.when(slot + AHEAD < pl.num_programs(0))
    def _():
        start_fetch(slot + AHEAD, which_ref[0], lefts, right, left_copy, right_copy, sems)

    wait_fetch(slot, lefts, right, left_copy, right_copy, sems)
    for term in range(terms):
        row = pl.multiple_of(rows_ref[slot, term], 8)
        first = jnp.concatenate(split(blocks[pl.ds(row, blk), :]), axis=1)
        value = folded(dot(first, right_factor(*split(right_copy[term, slot]))))
        inner[term * blk : (term + 1) * blk, :] = jnp.concatenate(split(value), axis=1)
    result = None
    for term in range(0, terms, 2):
        (high0, low0), (high1, low1) = (
            split(left_copy[index, slot]) for index in (term, term + 1)
        )
        below = inner[term * blk : (term + 2) * blk, :]
        part = folded(dot(jnp.concatenate([high0, high1], axis=1), below))
        part = part + dot(jnp.concatenate([low0, low1], axis=1), below[:, :blk])
        result = part if result is None else result + part
    value = masked(result, limit_ref[slot])

    scale, a0, keep, turn, a1 = (coef_ref[k : k + 1, :] for k in range(5))
    x0 = states[0][0] * scale
    if mode == 1:
        y0 = value * scale
        products = [x0 * y0]
        send = y0
    else:
        y0 = states[1][0]
        r1 = y0 - a0 * x0
        if mode == 2:
            z1 = value - a0 * y0
            products = [x0 * z1, r1 * y0, r1 * z1, r1 * r1]
            send = z1
        else:
            z1 = states[2][0]
            x1 = keep * x0 + turn * r1
            y1 = keep * y0 + turn * z1
            r2 = y1 - a1 * x1
            z2 = keep * (z1 + a0 * y0) + turn * value - a1 * y1
            outs[0][0] = x1
            outs[1][0] = r2
            put_sums(slot, [r2 * r2, r2 * z2], outs[2])
            return
    outs[0][0] = send
    put_quarter(slot, send, outs[1:])
    put_sums(slot, products, outs[1].at[pl.ds(outs[1].shape[0] - TAIL, TAIL), :])


def apply(rows, limit, which, tails, pieces, lefts, right, known, states):
    mode = len(states)
    terms, slots, blk, _ = right.shape
    vector = jax.ShapeDtypeStruct((slots, blk, blk), jnp.float32)
    vector_spec = pl.BlockSpec((1, blk, blk), lambda s, *_: (s, 0, 0))
    few = jax.ShapeDtypeStruct((TAIL, blk), jnp.float32)
    few_spec = whole_spec((TAIL, blk))
    if mode < 3:
        sizes = heights(slots, blk)
        out_shape = [few, vector]
        out_shape += [jax.ShapeDtypeStruct((size, blk), jnp.float32) for size in sizes]
        out_specs = [few_spec, vector_spec] + [whole_spec((size, blk)) for size in sizes]
    else:
        out_shape = [few, vector, vector, few]
        out_specs = [few_spec, vector_spec, vector_spec, few_spec]
    total = sum(piece.shape[0] for piece in pieces)
    own, near, far = lefts
    counts = (len(pieces), 1, len(near), len(far))
    return pl.pallas_call(
        functools.partial(apply_kernel, mode, counts, tails),
        out_shape=out_shape,
        grid_spec=pltpu.PrefetchScalarGridSpec(
            num_scalar_prefetch=3,
            grid=(slots,),
            in_specs=[pl.BlockSpec(memory_space=pl.ANY)] * (sum(counts) + 1)
            + [few_spec]
            + [vector_spec] * mode,
            out_specs=out_specs,
            scratch_shapes=[
                pltpu.VMEM((total, blk), jnp.float32),
                pltpu.VMEM(right.shape, jnp.float32),
                pltpu.VMEM(right.shape, jnp.float32),
                pltpu.VMEM((terms * blk, 2 * blk), jnp.bfloat16),
                pltpu.SemaphoreType.DMA((1 + len(near), slots)),
                pltpu.SemaphoreType.DMA((len(pieces),)),
            ],
        ),
        compiler_params=pltpu.CompilerParams(vmem_limit_bytes=30 * MIB),
        cost_estimate=pl.CostEstimate(
            flops=8 * terms * slots * blk**3, bytes_accessed=12 * right.size, transcendentals=0
        ),
    )(rows, limit, which, *pieces, own, *near, *far, right, known, *states)


def finish_kernel(sums_ref, coef_ref, one_ref, other_ref, out_ref, energy_ref):
    sums = jnp.sum(sums_ref[...], axis=0)
    total = jnp.broadcast_to(jnp.sum(sums, axis=1, keepdims=True), sums.shape)
    lam, keep, turn = mix(coef_ref[4:5, :], total[0:1, :] + 1e-06, total[1:2, :])
    energy_ref[...] = jnp.broadcast_to(lam, energy_ref.shape)
    for slot in range(one_ref.shape[0]):
        out_ref[slot] = keep * one_ref[slot] + turn * other_ref[slot]


def finish(sums, coefs, one, other):
    return pl.pallas_call(
        finish_kernel,
        out_shape=[
            jax.ShapeDtypeStruct(one.shape, jnp.float32),
            jax.ShapeDtypeStruct(coefs.shape, jnp.float32),
        ],
        compiler_params=pltpu.CompilerParams(vmem_limit_bytes=4 * MIB),
    )(sums, coefs, one, other)


def partner(index, move):
    axis, flip = move
    z, y = index // SIDE, index % SIDE
    return z * SIDE + (y ^ flip) if axis == "y" else (z ^ flip) * SIDE + y


def swap(value, move, count):
    return lax.ppermute(value, "sector", [(index, partner(index, move)) for index in range(count)])


def gather(quarters, count):
    held = list(quarters)
    for step in range(len(ORDERS[0])):
        last = step == len(ORDERS[0]) - 1
        came = [swap(value, order[step], count) for value, order in zip(held, ORDERS)]
        if last:
            return [piece for pair in zip(held, came) for piece in pair]
        held = [jnp.concatenate(pair, axis=0) for pair in zip(held, came)]


def place_of(apart, flips):
    first, second = flips
    both = first ^ second
    return jnp.where(apart == first, 1, jnp.where(apart == second, 2, jnp.where(apart == both, 3, 0)))


def block_rows(source, owner, sdev, blk):
    device, slot = source // sdev, source % sdev
    apart = device ^ owner
    apart = {"z": apart // SIDE, "y": apart % SIDE}
    per = sdev // PARTS
    sizes = heights(sdev, blk)
    rows = jnp.zeros_like(source)
    base = 0
    for part, order in enumerate(ORDERS):
        (near, one), (_, two), (far, three), (_, four) = order
        unit = place_of(apart[near], (one, two)) + SIDE * place_of(apart[far], (three, four))
        here = base + unit * sizes[part] + (slot % per) * blk
        rows = jnp.where(slot // per == part, here, rows)
        base += SIDE * SIDE * sizes[part]
    return rows


def to_next(value):
    count = lax.axis_size("chain")
    return lax.ppermute(value, "chain", [(source, source + 1) for source in range(count - 1)])


def to_next_round(value):
    count = lax.axis_size("chain")
    inside = [(source, source + 1) for source in range(0, count, 2)]
    places = [(source - 3) % count for source in range(1, count - 1, 2)]
    pairs = inside + list(zip(range(1, count - 1, 2), places))
    near = value = lax.ppermute(value, "chain", pairs)
    for _ in range(count // 2 - 2):
        pairs = [(place, (place - 2) % count) for place in places]
        value = lax.ppermute(value, "chain", pairs)
        places = [place for _, place in pairs]
    return near, value


def body(left_env, right_env, site_block, start_vec, slot_sector, couple, dims, kept):
    lenv = left_env[0]
    renv = right_env[0]
    site = site_block[0]
    start = start_vec[0]
    sdev = start.shape[0]
    blk = start.shape[1]
    nsec = slot_sector.shape[0]
    devices = nsec // sdev
    owner = lax.axis_index("sector")
    slots = owner * sdev + jnp.arange(sdev, dtype=jnp.int32)
    sector_ids = jnp.take(slot_sector, slots)
    inverse = jnp.zeros((nsec,), jnp.int32).at[slot_sector].set(jnp.arange(nsec, dtype=jnp.int32))
    source = inverse[couple[sector_ids]]
    rows = block_rows(source, owner, sdev, blk)

    chain = lax.axis_index("chain")
    which = jnp.where(chain == 0, 0, jnp.where(chain % 2 == 1, 1, 2)).astype(jnp.int32).reshape(1)
    terms = lenv.shape[0]

    def in_hbm(value):
        return pltpu.with_memory_space_constraint(value, pltpu.HBM)

    k0, limit, packed = begin(
        owner.astype(jnp.int32).reshape(1),
        *(in_hbm(value) for value in (slot_sector, dims, kept, start)),
    )
    site, k0 = lax.optimization_barrier((site, k0))
    lenv = in_hbm(lenv)
    whole = lax.all_gather(packed, "sector", axis=0, tiled=True)
    some = terms // 8
    sizes = [terms // 2, terms - terms // 2 - 2 * some, some, some]
    built = {}
    for number in (0, 2, 3, 1):
        part = update(lenv, site, sum(sizes[:number]), sizes[number])
        if number < 2:
            near = far = to_next(part)
        else:
            near, far = to_next_round(part)
        built[number] = tuple(in_hbm(value) for value in (part, near, far))
    parts, nears, fars = ([built[number][k] for number in range(len(sizes))] for k in range(3))
    lefts = lenv, nears, fars
    right = in_hbm(renv)

    height = sdev * blk + TAIL
    tails = [device * height + height - TAIL for device in range(devices)]
    first_rows = (source // sdev) * height + (source % sdev) * blk
    known = jnp.zeros((TAIL, blk), jnp.float32)
    known, y0, *quarters = apply(
        first_rows, limit, which, tails, [whole], lefts, right, known, [k0]
    )
    height = heights(sdev, blk)[0]
    tails = [unit * height + height - TAIL for unit in range(SIDE * SIDE)]
    pieces = gather(quarters, devices)
    updated = join(parts, pieces[0])
    pieces, updated = lax.optimization_barrier((pieces, updated))
    known, z1, *quarters = apply(rows, limit, which, tails, pieces, lefts, right, known, [k0, y0])
    pieces = gather(quarters, devices)
    known, x1, r2, sums = apply(
        rows, limit, which, tails, pieces, lefts, right, known, [k0, y0, z1]
    )
    for axis in ("y", "z"):
        others = [swap(sums, (axis, flip), devices) for flip in range(1, SIDE)]
        if axis == "y":
            sums = (sums + others[0]) + (others[1] + others[2])
    x2, energy = finish(jnp.stack([sums] + others), known, x1, r2)
    return (x2[None], updated[None], energy[0, :1])


def solution(mesh):
    placed = (
        P("chain", None, "sector", None, None),
        P("chain", None, "sector", None, None),
        P("chain", "sector", None, None),
        P("chain", "sector", None, None),
        P(),
        P(),
        P(),
        P(),
    )
    return jax.shard_map(
        body,
        mesh=mesh,
        in_specs=placed,
        out_specs=(
            P("chain", "sector", None, None),
            P("chain", None, "sector", None, None),
            P("chain"),
        ),
        check_vma=False,
    )
```

time: 314 us -> 260 us (0.83)
  local copies, waits for them, and re-layouts: 48.3 us -> 8.2 us
  waiting for transfers between devices: 128 us -> 96.3 us
  starting transfers between devices: 67.1 us -> 83.4 us
  other arithmetic: 15.2 us -> 0.52 us
  Pallas kernels: 43.9 us -> 56.6 us
  between operations: 10.5 us -> 14.6 us
    ppermute x52 -> x38, waiting for transfers between devices: 128 us -> 58.1 us  [swap(): lax.ppermute(value, 'sector', [(index, partner(index, move)) for index in...]
    ppermute x1 -> x8, waiting for transfers between devices: 0.01 us -> 38.2 us  [the longest x2 20.7 us: to_next_round(): near = value = lax.ppermute(value, 'chain', pairs)]
    unnamed x92 -> x38, local copies, waits for them, and re-layouts: 36.1 us -> 3.85 us
    ppermute x1 -> x8, starting transfers between devices: 4.7 us -> 27 us  [the longest x4 15.7 us: to_next_round(): value = lax.ppermute(value, 'chain', pairs)]
    pallas_call x4 -> x9, Pallas kernels: 38.3 us -> 54.6 us  [the longest x3 30.1 us: apply(): pl.pallas_call(functools.partial(apply_kernel, mode, counts, tails), out_...]
    select_n x4 -> x2, other arithmetic: 9.64 us -> 0.01 us  [body(): source = inverse[couple[sector_ids]]]
    ppermute x52 -> x38, starting transfers between devices: 62.4 us -> 56.4 us  [swap(): lax.ppermute(value, 'sector', [(index, partner(index, move)) for index in...]
    concatenate x12 -> x8, local copies, waits for them, and re-layouts: 5.26 us -> 0.28 us  [gather(): held = [jnp.concatenate(pair, axis=0) for pair in zip(held, came)]]
  transfers between devices with their start and end apart: 53 -> 47, of which waited for: 25 -> 27; matrix products, arithmetic and copies ran while one was open for 12% -> 2% of each run, Pallas kernels for 2% -> 9%
where the time goes in v3:
time: 260 us
  waiting for transfers between devices  96.3 us (37%)
  starting transfers between devices  83.4 us (32%)
  Pallas kernels  56.6 us (22%)
  between operations  14.6 us (6%)
  local copies, waits for them, and re-layouts  8.2 us (3%)
    ppermute x38, waiting for transfers between devices, swap(): lax.ppermute(value, 'sector', [(index, partner(index, move)) for index in...  58.1 us
    ppermute x38, starting transfers between devices, swap(): lax.ppermute(value, 'sector', [(index, partner(index, move)) for index in...  56.4 us
    pallas_call x3, Pallas kernels, apply(): pl.pallas_call(functools.partial(apply_kernel, mode, counts, tails), out_...  30.1 us
    ppermute x2, waiting for transfers between devices, to_next_round(): near = value = lax.ppermute(value, 'chain', pairs)  20.7 us
    ppermute x4, waiting for transfers between devices, to_next_round(): value = lax.ppermute(value, 'chain', pairs)  17.5 us
    ppermute x4, starting transfers between devices, to_next_round(): value = lax.ppermute(value, 'chain', pairs)  15.7 us
    pallas_call x4, Pallas kernels, update(): pl.pallas_call(update_kernel, out_shape=jax.ShapeDtypeStruct((some, slots...  14.5 us
    pallas_call x1, Pallas kernels, join(): pl.pallas_call(functools.partial(join_kernel, starts), out_shape=jax.Shap...  9.04 us
  transfers between devices with their start and end apart: 47, of which 27 were waited for; matrix products, arithmetic and copies ran while one was open for 2% of the time, Pallas kernels for 9%

profile of v3, /device:TPU:0, one launch (start us, length us, event | category | flops | bytes accessed | tf_op | source)
XLA Modules:
  0.0 259.6 jit_solution(15843229264108070074)
XLA Ops:
  9.3 6.8 %shard_map.104.refs_0_ = f32[8,8,128,128]{3,2,1,0:T(8,128)} custom-call(f32[16,8,128,128]{3,2,1,0:T(8,128)} %bitcast.29, f32[8,128,128]{2,1,0:T(8,128)S(1)} %bitcast.25), custom_call_target="tpu_custom_call" | custom-call | flops 1073741824 | bytes 8388608 | tf_op jit(solution)/shard_map/pallas_call | solution.py:69
  16.1 3.3 %collective-permute-start = (f32[8,8,128,128]{3,2,1,0:T(8,128)}, f32[8,8,128,128]{3,2,1,0:T(8,128)}, u32[]{:S(2)}, u32[]{:S(2)}) collective-permute-start(f32[8,8,128,128]{3,2,1,0:T(8,128)} %shard_map.104.refs_0_), channel_id=1, source_target_pairs={{0,16},{16,32},{32,48},{48,64},{64,80},{80,96},{96,112},{1,17},{17... | collective-permute-start | bytes 12582920 | tf_op jit(solution)/shard_map/ppermute | solution.py:436
  26.1 3.2 %collective-permute-start.3 = (f32[2,8,128,128]{3,2,1,0:T(8,128)S(1)}, f32[2,8,128,128]{3,2,1,0:T(8,128)}, u32[]{:S(2)}, u32[]{:S(2)}) collective-permute-start(f32[2,8,128,128]{3,2,1,0:T(8,128)S(1)} %shard_map.107.refs_3_), channel_id=1, source_target_pairs={{0,16},{32,48},{64,80},{96,112},{16,96},{48,0},{80,32},{1,17},{33,... | collective-permute-start | bytes 3145736 | tf_op jit(solution)/shard_map/ppermute | solution.py:444
  29.3 8.6 %collective-permute-done.2.refs_4_.refs_11_ = f32[2,8,128,128]{3,2,1,0:T(8,128)} collective-permute-done((f32[2,8,128,128]{3,2,1,0:T(8,128)S(1)}, f32[2,8,128,128]{3,2,1,0:T(8,128)}, u32[]{:S(2)}, u32[]{:S(2)}) %collective-permute-start.2) | collective-permute-done | bytes 1048608 | tf_op jit(solution)/shard_map/ppermute | solution.py:444
  37.8 4.5 %collective-permute-start.4 = (f32[2,8,128,128]{3,2,1,0:T(8,128)}, f32[2,8,128,128]{3,2,1,0:T(8,128)}, u32[]{:S(2)}, u32[]{:S(2)}) collective-permute-start(f32[2,8,128,128]{3,2,1,0:T(8,128)} %collective-permute-done.2.refs_4_.refs_11_), channel_id=1, source_target_pairs={{96,64},{0,96},{32,0},{97,65},{1,97},{33,1},{98,66},{2,98},{34,2},... | collective-permute-start | bytes 3145736 | tf_op jit(solution)/shard_map/ppermute | solution.py:447
  42.3 12.1 %collective-permute-done.3.refs_5_.refs_12_ = f32[2,8,128,128]{3,2,1,0:T(8,128)} collective-permute-done((f32[2,8,128,128]{3,2,1,0:T(8,128)S(1)}, f32[2,8,128,128]{3,2,1,0:T(8,128)}, u32[]{:S(2)}, u32[]{:S(2)}) %collective-permute-start.3) | collective-permute-done | bytes 1048608 | tf_op jit(solution)/shard_map/ppermute | solution.py:444
  54.5 3.3 %collective-permute-start.6 = (f32[2,8,128,128]{3,2,1,0:T(8,128)}, f32[2,8,128,128]{3,2,1,0:T(8,128)}, u32[]{:S(2)}, u32[]{:S(2)}) collective-permute-start(f32[2,8,128,128]{3,2,1,0:T(8,128)} %collective-permute-done.3.refs_5_.refs_12_), channel_id=1, source_target_pairs={{96,64},{0,96},{32,0},{97,65},{1,97},{33,1},{98,66},{2,98},{34,2},... | collective-permute-start | bytes 3145736 | tf_op jit(solution)/shard_map/ppermute | solution.py:447
  57.8 3.3 %shard_map.105.refs_1_ = f32[4,8,128,128]{3,2,1,0:T(8,128)S(1)} custom-call(f32[16,8,128,128]{3,2,1,0:T(8,128)} %bitcast.32, f32[8,128,128]{2,1,0:T(8,128)S(1)} %bitcast.28), custom_call_target="tpu_custom_call" | custom-call | flops 536870912 | bytes 4194304 | tf_op jit(solution)/shard_map/pallas_call | solution.py:69
  66.8 4.7 %collective-permute-done.6 = f32[2,8,128,128]{3,2,1,0:T(8,128)} collective-permute-done((f32[2,8,128,128]{3,2,1,0:T(8,128)}, f32[2,8,128,128]{3,2,1,0:T(8,128)}, u32[]{:S(2)}, u32[]{:S(2)}) %collective-permute-start.6) | collective-permute-done | bytes 1048608 | tf_op jit(solution)/shard_map/ppermute | solution.py:447
  71.5 5.5 %collective-permute-start.7 = (f32[2,8,128,128]{3,2,1,0:T(8,128)}, f32[2,8,128,128]{3,2,1,0:T(8,128)}, u32[]{:S(2)}, u32[]{:S(2)}) collective-permute-start(f32[2,8,128,128]{3,2,1,0:T(8,128)} %collective-permute-done.6), channel_id=1, source_target_pairs={{64,32},{96,64},{0,96},{65,33},{97,65},{1,97},{66,34},{98,66},{2,9... | collective-permute-start | bytes 3145736 | tf_op jit(solution)/shard_map/ppermute | solution.py:447
  81.7 11.2 %collective-permute-done.7.refs_9_.refs_16_ = f32[2,8,128,128]{3,2,1,0:T(8,128)} collective-permute-done((f32[2,8,128,128]{3,2,1,0:T(8,128)}, f32[2,8,128,128]{3,2,1,0:T(8,128)}, u32[]{:S(2)}, u32[]{:S(2)}) %collective-permute-start.7) | collective-permute-done | bytes 1048608 | tf_op jit(solution)/shard_map/ppermute | solution.py:447
  92.9 3.4 %copy-done = f32[16512,128]{1,0:T(8,128)S(1)} copy-done((f32[16512,128]{1,0:T(8,128)S(1)}, f32[16512,128]{1,0:T(8,128)}, u32[]{:S(2)}) %copy-start) | copy-done | bytes 8454168
  96.3 10.1 %shard_map.108 = (f32[8,128]{1,0:T(8,128)S(1)}, f32[8,128,128]{2,1,0:T(8,128)S(1)}, f32[264,128]{1,0:T(8,128)S(1)}, f32[256,128]{1,0:T(8,128)S(1)}, f32[256,128]{1,0:T(8,128)S(1)}, /*index=5*/f32[256,128]{1,0:T(8,128)S(1)}) custom-call(s32[8,16]{1,0:T(8,128)S(1)} %get-tuple-element.67.rows_ref, s32[8]{0:T(128)S(1)} %get-tuple-element.35.limit_ref, ...), custom_call_target="tpu_custom_call" | custom-call | flops 2147483648 | bytes 25165824 | tf_op jit(solution)/shard_map/pallas_call | solution.py:345
  106.5 4.2 %collective-permute-start.20 = (f32[256,128]{1,0:T(8,128)S(1)}, f32[256,128]{1,0:T(8,128)S(1)}, u32[]{:S(2)}, u32[]{:S(2)}) collective-permute-start(f32[256,128]{1,0:T(8,128)S(1)} %get-tuple-element.43), channel_id=1, source_target_pairs={{0,12},{1,13},{2,14},{3,15},{4,8},{5,9},{6,10},{7,11},{8,4},{9,5},... | collective-permute-start | bytes 393224 | tf_op jit(solution)/shard_map/ppermute | solution.py:398
  131.2 6.8 %collective-permute-done.22 = f32[1024,128]{1,0:T(8,128)S(1)} collective-permute-done((f32[1024,128]{1,0:T(8,128)S(1)}, f32[1024,128]{1,0:T(8,128)S(1)}, u32[]{:S(2)}, u32[]{:S(2)}) %collective-permute-start.22) | collective-permute-done | bytes 524320 | tf_op jit(solution)/shard_map/ppermute | solution.py:398
  142.3 4.1 %collective-permute-start.11 = (f32[2112,128]{1,0:T(8,128)S(1)}, f32[2112,128]{1,0:T(8,128)S(1)}, u32[]{:S(2)}, u32[]{:S(2)}) collective-permute-start(f32[2112,128]{1,0:T(8,128)S(1)} %constant_dynamic-update-slice_fusion.refs_4_.refs_0_), channel_id=1, source_target_pairs={{0,12},{1,13},{2,14},{3,15},{4,8},{5,9},{6,10},{7,11},{8,4},{9,5},... | collective-permute-start | bytes 3244040 | tf_op jit(solution)/shard_map/ppermute | solution.py:398
  147.5 9.0 %shard_map.109 = f32[16,8,128,128]{3,2,1,0:T(8,128)} custom-call(f32[8,8,128,128]{3,2,1,0:T(8,128)} %shard_map.104.refs_0_, f32[4,8,128,128]{3,2,1,0:T(8,128)} %copy-done.1, f32[2,8,128,128]{3,2,1,0:T(8,128)} %copy-done.3, f32[2,8,128,128]{3,2,1,0:T(8,128)} %copy-done.4, f32[2112,128]{1,0:T(8,128)S(1)} %constant_dynamic-update-slice_fusion.refs_4_.refs_0_), custom_call_target="tpu_custom_call" | custom-call | bytes 16777216 | tf_op jit(solution)/shard_map/pallas_call | solution.py:111
  157.8 3.7 %collective-permute-done.15.refs_3_ = f32[2048,128]{1,0:T(8,128)S(1)} collective-permute-done((f32[2048,128]{1,0:T(8,128)S(1)}, f32[2048,128]{1,0:T(8,128)S(1)}, u32[]{:S(2)}, u32[]{:S(2)}) %collective-permute-start.15) | collective-permute-done | bytes 1048608 | tf_op jit(solution)/shard_map/ppermute | solution.py:398
  162.3 10.1 %shard_map.110 = (f32[8,128]{1,0:T(8,128)S(1)}, f32[8,128,128]{2,1,0:T(8,128)S(1)}, f32[264,128]{1,0:T(8,128)S(1)}, f32[256,128]{1,0:T(8,128)S(1)}, f32[256,128]{1,0:T(8,128)S(1)}, /*index=5*/f32[256,128]{1,0:T(8,128)S(1)}) custom-call(s32[8,16]{1,0:T(8,128)S(1)} %get-tuple-element.68.rows_ref, s32[8]{0:T(128)S(1)} %get-tuple-element.35.limit_ref, ...), custom_call_target="tpu_custom_call" | custom-call | flops 2147483648 | bytes 25165824 | tf_op jit(solution)/shard_map/pallas_call | solution.py:345
  193.5 9.2 %collective-permute-done.38 = f32[1024,128]{1,0:T(8,128)S(1)} collective-permute-done((f32[1024,128]{1,0:T(8,128)S(1)}, f32[1024,128]{1,0:T(8,128)S(1)}, u32[]{:S(2)}, u32[]{:S(2)}) %collective-permute-start.38) | collective-permute-done | bytes 524320 | tf_op jit(solution)/shard_map/ppermute | solution.py:398
  210.3 7.9 %collective-permute-done.39.refs_7_ = f32[2048,128]{1,0:T(8,128)S(1)} collective-permute-done((f32[2048,128]{1,0:T(8,128)S(1)}, f32[2048,128]{1,0:T(8,128)S(1)}, u32[]{:S(2)}, u32[]{:S(2)}) %collective-permute-start.39) | collective-permute-done | bytes 1048608 | tf_op jit(solution)/shard_map/ppermute | solution.py:398
  218.2 3.2 %collective-permute-done.35.refs_5_ = f32[2048,128]{1,0:T(8,128)S(1)} collective-permute-done((f32[2048,128]{1,0:T(8,128)S(1)}, f32[2048,128]{1,0:T(8,128)S(1)}, u32[]{:S(2)}, u32[]{:S(2)}) %collective-permute-start.35) | collective-permute-done | bytes 1048608 | tf_op jit(solution)/shard_map/ppermute | solution.py:398
  221.4 3.6 %collective-permute-done.31.refs_3_ = f32[2048,128]{1,0:T(8,128)S(1)} collective-permute-done((f32[2048,128]{1,0:T(8,128)S(1)}, f32[2048,128]{1,0:T(8,128)S(1)}, u32[]{:S(2)}, u32[]{:S(2)}) %collective-permute-start.31) | collective-permute-done | bytes 1048608 | tf_op jit(solution)/shard_map/ppermute | solution.py:398
  225.1 9.8 %shard_map.111 = (f32[8,128]{1,0:T(8,128)S(1)}, f32[8,128,128]{2,1,0:T(8,128)S(1)}, f32[8,128,128]{2,1,0:T(8,128)S(1)}, f32[8,128]{1,0:T(8,128)S(1)}) custom-call(s32[8,16]{1,0:T(8,128)S(1)} %get-tuple-element.68.rows_ref, s32[8]{0:T(128)S(1)} %get-tuple-element.35.limit_ref, s32[1]{0:T(128)} %bitcast.6.which_ref, ...), custom_call_target="tpu_custom_call" | custom-call | flops 2147483648 | bytes 25165824 | tf_op jit(solution)/shard_map/pallas_call | solution.py:345
  (162 shorter events, 93.2 us)
Async XLA Ops:
  7.2 85.8 %all-gather.2.cloned.1.call-start = ((), (), s32[]{:S(2)}) async-start(), calls=%async_computation | async-start | bytes 8982528 | tf_op jit(solution)/shard_map/all_gather | solution.py:481
  16.1 76.8 %collective-permute-start = (f32[8,8,128,128]{3,2,1,0:T(8,128)}, f32[8,8,128,128]{3,2,1,0:T(8,128)}, u32[]{:S(2)}, u32[]{:S(2)}) collective-permute-start(f32[8,8,128,128]{3,2,1,0:T(8,128)} %shard_map.104.refs_0_), channel_id=1, source_target_pairs={{0,16},{16,32},{32,48},{48,64},{64,80},{80,96},{96,112},{1,17},{17... | collective-permute-start | bytes 12582920 | tf_op jit(solution)/shard_map/ppermute | solution.py:436
  21.6 16.2 %collective-permute-start.2 = (f32[2,8,128,128]{3,2,1,0:T(8,128)S(1)}, f32[2,8,128,128]{3,2,1,0:T(8,128)}, u32[]{:S(2)}, u32[]{:S(2)}) collective-permute-start(f32[2,8,128,128]{3,2,1,0:T(8,128)S(1)} %shard_map.106.refs_2_), channel_id=1, source_target_pairs={{0,16},{32,48},{64,80},{96,112},{16,96},{48,0},{80,32},{1,17},{33,... | collective-permute-start | bytes 3145736 | tf_op jit(solution)/shard_map/ppermute | solution.py:444
  26.1 28.4 %collective-permute-start.3 = (f32[2,8,128,128]{3,2,1,0:T(8,128)S(1)}, f32[2,8,128,128]{3,2,1,0:T(8,128)}, u32[]{:S(2)}, u32[]{:S(2)}) collective-permute-start(f32[2,8,128,128]{3,2,1,0:T(8,128)S(1)} %shard_map.107.refs_3_), channel_id=1, source_target_pairs={{0,16},{32,48},{64,80},{96,112},{16,96},{48,0},{80,32},{1,17},{33,... | collective-permute-start | bytes 3145736 | tf_op jit(solution)/shard_map/ppermute | solution.py:444
  37.8 26.7 %collective-permute-start.4 = (f32[2,8,128,128]{3,2,1,0:T(8,128)}, f32[2,8,128,128]{3,2,1,0:T(8,128)}, u32[]{:S(2)}, u32[]{:S(2)}) collective-permute-start(f32[2,8,128,128]{3,2,1,0:T(8,128)} %collective-permute-done.2.refs_4_.refs_11_), channel_id=1, source_target_pairs={{96,64},{0,96},{32,0},{97,65},{1,97},{33,1},{98,66},{2,98},{34,2},... | collective-permute-start | bytes 3145736 | tf_op jit(solution)/shard_map/ppermute | solution.py:447
  54.5 17.1 %collective-permute-start.6 = (f32[2,8,128,128]{3,2,1,0:T(8,128)}, f32[2,8,128,128]{3,2,1,0:T(8,128)}, u32[]{:S(2)}, u32[]{:S(2)}) collective-permute-start(f32[2,8,128,128]{3,2,1,0:T(8,128)} %collective-permute-done.3.refs_5_.refs_12_), channel_id=1, source_target_pairs={{96,64},{0,96},{32,0},{97,65},{1,97},{33,1},{98,66},{2,98},{34,2},... | collective-permute-start | bytes 3145736 | tf_op jit(solution)/shard_map/ppermute | solution.py:447
  61.1 19.0 %collective-permute-start.1 = (f32[4,8,128,128]{3,2,1,0:T(8,128)S(1)}, f32[4,8,128,128]{3,2,1,0:T(8,128)}, u32[]{:S(2)}, u32[]{:S(2)}) collective-permute-start(f32[4,8,128,128]{3,2,1,0:T(8,128)S(1)} %shard_map.105.refs_1_), channel_id=1, source_target_pairs={{0,16},{16,32},{32,48},{48,64},{64,80},{80,96},{96,112},{1,17},{17... | collective-permute-start | bytes 6291464 | tf_op jit(solution)/shard_map/ppermute | solution.py:436
  64.5 17.2 %collective-permute-start.5 = (f32[2,8,128,128]{3,2,1,0:T(8,128)}, f32[2,8,128,128]{3,2,1,0:T(8,128)}, u32[]{:S(2)}, u32[]{:S(2)}) collective-permute-start(f32[2,8,128,128]{3,2,1,0:T(8,128)} %collective-permute-done.4), channel_id=1, source_target_pairs={{64,32},{96,64},{0,96},{65,33},{97,65},{1,97},{66,34},{98,66},{2,9... | collective-permute-start | bytes 3145736 | tf_op jit(solution)/shard_map/ppermute | solution.py:447
  71.5 21.4 %collective-permute-start.7 = (f32[2,8,128,128]{3,2,1,0:T(8,128)}, f32[2,8,128,128]{3,2,1,0:T(8,128)}, u32[]{:S(2)}, u32[]{:S(2)}) collective-permute-start(f32[2,8,128,128]{3,2,1,0:T(8,128)} %collective-permute-done.6), channel_id=1, source_target_pairs={{64,32},{96,64},{0,96},{65,33},{97,65},{1,97},{66,34},{98,66},{2,9... | collective-permute-start | bytes 3145736 | tf_op jit(solution)/shard_map/ppermute | solution.py:447
  122.5 15.4 %collective-permute-start.22 = (f32[1024,128]{1,0:T(8,128)S(1)}, f32[1024,128]{1,0:T(8,128)S(1)}, u32[]{:S(2)}, u32[]{:S(2)}) collective-permute-start(f32[1024,128]{1,0:T(8,128)S(1)} %pad_maximum_fusion.4), channel_id=1, source_target_pairs={{0,3},{1,2},{2,1},{3,0},{4,7},{5,6},{6,5},{7,4},{8,11},{9,10},{10,... | collective-permute-start | bytes 1572872 | tf_op jit(solution)/shard_map/ppermute | solution.py:398
  126.0 13.8 %collective-permute-start.18 = (f32[1024,128]{1,0:T(8,128)S(1)}, f32[1024,128]{1,0:T(8,128)S(1)}, u32[]{:S(2)}, u32[]{:S(2)}) collective-permute-start(f32[1024,128]{1,0:T(8,128)S(1)} %pad_maximum_fusion.3), channel_id=1, source_target_pairs={{0,1},{1,0},{2,3},{3,2},{4,5},{5,4},{6,7},{7,6},{8,9},{9,8},{10,11... | collective-permute-start | bytes 1572872 | tf_op jit(solution)/shard_map/ppermute | solution.py:398
  128.7 17.7 %collective-permute-start.14 = (f32[1024,128]{1,0:T(8,128)S(1)}, f32[1024,128]{1,0:T(8,128)S(1)}, u32[]{:S(2)}, u32[]{:S(2)}) collective-permute-start(f32[1024,128]{1,0:T(8,128)S(1)} %pad_maximum_fusion.2), channel_id=1, source_target_pairs={{0,12},{1,13},{2,14},{3,15},{4,8},{5,9},{6,10},{7,11},{8,4},{9,5},... | collective-permute-start | bytes 1572872 | tf_op jit(solution)/shard_map/ppermute | solution.py:398
  138.0 19.8 %collective-permute-start.23 = (f32[2048,128]{1,0:T(8,128)S(1)}, f32[2048,128]{1,0:T(8,128)S(1)}, u32[]{:S(2)}, u32[]{:S(2)}) collective-permute-start(f32[2048,128]{1,0:T(8,128)S(1)} %constant_dynamic-update-slice_fusion.12.refs_6_), channel_id=1, source_target_pairs={{0,1},{1,0},{2,3},{3,2},{4,5},{5,4},{6,7},{7,6},{8,9},{9,8},{10,11... | collective-permute-start | bytes 3145736 | tf_op jit(solution)/shard_map/ppermute | solution.py:398
  139.9 17.9 %collective-permute-start.19 = (f32[2048,128]{1,0:T(8,128)S(1)}, f32[2048,128]{1,0:T(8,128)S(1)}, u32[]{:S(2)}, u32[]{:S(2)}) collective-permute-start(f32[2048,128]{1,0:T(8,128)S(1)} %constant_dynamic-update-slice_fusion.8.refs_4_), channel_id=1, source_target_pairs={{0,3},{1,2},{2,1},{3,0},{4,7},{5,6},{6,5},{7,4},{8,11},{9,10},{10,... | collective-permute-start | bytes 3145736 | tf_op jit(solution)/shard_map/ppermute | solution.py:398
  142.3 20.0 %collective-permute-start.11 = (f32[2112,128]{1,0:T(8,128)S(1)}, f32[2112,128]{1,0:T(8,128)S(1)}, u32[]{:S(2)}, u32[]{:S(2)}) collective-permute-start(f32[2112,128]{1,0:T(8,128)S(1)} %constant_dynamic-update-slice_fusion.refs_4_.refs_0_), channel_id=1, source_target_pairs={{0,12},{1,13},{2,14},{3,15},{4,8},{5,9},{6,10},{7,11},{8,4},{9,5},... | collective-permute-start | bytes 3244040 | tf_op jit(solution)/shard_map/ppermute | solution.py:398
  146.4 15.1 %collective-permute-start.15 = (f32[2048,128]{1,0:T(8,128)S(1)}, f32[2048,128]{1,0:T(8,128)S(1)}, u32[]{:S(2)}, u32[]{:S(2)}) collective-permute-start(f32[2048,128]{1,0:T(8,128)S(1)} %constant_dynamic-update-slice_fusion.4.refs_2_), channel_id=1, source_target_pairs={{0,4},{1,5},{2,6},{3,7},{4,0},{5,1},{6,2},{7,3},{8,12},{9,13},{10,... | collective-permute-start | bytes 3145736 | tf_op jit(solution)/shard_map/ppermute | solution.py:398
  187.3 15.4 %collective-permute-start.38 = (f32[1024,128]{1,0:T(8,128)S(1)}, f32[1024,128]{1,0:T(8,128)S(1)}, u32[]{:S(2)}, u32[]{:S(2)}) collective-permute-start(f32[1024,128]{1,0:T(8,128)S(1)} %pad_maximum_fusion.7), channel_id=1, source_target_pairs={{0,3},{1,2},{2,1},{3,0},{4,7},{5,6},{6,5},{7,4},{8,11},{9,10},{10,... | collective-permute-start | bytes 1572872 | tf_op jit(solution)/shard_map/ppermute | solution.py:398
  190.4 14.9 %collective-permute-start.34 = (f32[1024,128]{1,0:T(8,128)S(1)}, f32[1024,128]{1,0:T(8,128)S(1)}, u32[]{:S(2)}, u32[]{:S(2)}) collective-permute-start(f32[1024,128]{1,0:T(8,128)S(1)} %pad_maximum_fusion.6), channel_id=1, source_target_pairs={{0,1},{1,0},{2,3},{3,2},{4,5},{5,4},{6,7},{7,6},{8,9},{9,8},{10,11... | collective-permute-start | bytes 1572872 | tf_op jit(solution)/shard_map/ppermute | solution.py:398
  191.4 18.8 %collective-permute-start.30 = (f32[1024,128]{1,0:T(8,128)S(1)}, f32[1024,128]{1,0:T(8,128)S(1)}, u32[]{:S(2)}, u32[]{:S(2)}) collective-permute-start(f32[1024,128]{1,0:T(8,128)S(1)} %pad_maximum_fusion.5), channel_id=1, source_target_pairs={{0,12},{1,13},{2,14},{3,15},{4,8},{5,9},{6,10},{7,11},{8,4},{9,5},... | collective-permute-start | bytes 1572872 | tf_op jit(solution)/shard_map/ppermute | solution.py:398
  193.2 15.3 %collective-permute-start.26 = (f32[1056,128]{1,0:T(8,128)S(1)}, f32[1056,128]{1,0:T(8,128)S(1)}, u32[]{:S(2)}, u32[]{:S(2)}) collective-permute-start(f32[1056,128]{1,0:T(8,128)S(1)} %pad_maximum_fusion.1), channel_id=1, source_target_pairs={{0,4},{1,5},{2,6},{3,7},{4,0},{5,1},{6,2},{7,3},{8,12},{9,13},{10,... | collective-permute-start | bytes 1622024 | tf_op jit(solution)/shard_map/ppermute | solution.py:398
  202.7 15.5 %collective-permute-start.39 = (f32[2048,128]{1,0:T(8,128)S(1)}, f32[2048,128]{1,0:T(8,128)S(1)}, u32[]{:S(2)}, u32[]{:S(2)}) collective-permute-start(f32[2048,128]{1,0:T(8,128)S(1)} %constant_dynamic-update-slice_fusion.28.refs_6_), channel_id=1, source_target_pairs={{0,1},{1,0},{2,3},{3,2},{4,5},{5,4},{6,7},{7,6},{8,9},{9,8},{10,11... | collective-permute-start | bytes 3145736 | tf_op jit(solution)/shard_map/ppermute | solution.py:398
  205.3 16.1 %collective-permute-start.35 = (f32[2048,128]{1,0:T(8,128)S(1)}, f32[2048,128]{1,0:T(8,128)S(1)}, u32[]{:S(2)}, u32[]{:S(2)}) collective-permute-start(f32[2048,128]{1,0:T(8,128)S(1)} %constant_dynamic-update-slice_fusion.24.refs_4_), channel_id=1, source_target_pairs={{0,3},{1,2},{2,1},{3,0},{4,7},{5,6},{6,5},{7,4},{8,11},{9,10},{10,... | collective-permute-start | bytes 3145736 | tf_op jit(solution)/shard_map/ppermute | solution.py:398
  208.5 16.6 %collective-permute-start.27 = (f32[2112,128]{1,0:T(8,128)S(1)}, f32[2112,128]{1,0:T(8,128)S(1)}, u32[]{:S(2)}, u32[]{:S(2)}) collective-permute-start(f32[2112,128]{1,0:T(8,128)S(1)} %constant_dynamic-update-slice_fusion.16.refs_0_), channel_id=1, source_target_pairs={{0,12},{1,13},{2,14},{3,15},{4,8},{5,9},{6,10},{7,11},{8,4},{9,5},... | collective-permute-start | bytes 3244040 | tf_op jit(solution)/shard_map/ppermute | solution.py:398
  210.2 14.9 %collective-permute-start.31 = (f32[2048,128]{1,0:T(8,128)S(1)}, f32[2048,128]{1,0:T(8,128)S(1)}, u32[]{:S(2)}, u32[]{:S(2)}) collective-permute-start(f32[2048,128]{1,0:T(8,128)S(1)} %constant_dynamic-update-slice_fusion.20.refs_2_), channel_id=1, source_target_pairs={{0,4},{1,5},{2,6},{3,7},{4,0},{5,1},{6,2},{7,3},{8,12},{9,13},{10,... | collective-permute-start | bytes 3145736 | tf_op jit(solution)/shard_map/ppermute | solution.py:398
  (30 other events, 312.6 us)
Sparse Core Ops, SparseCore 0:
  10.8 73.6 all-gather.1

commit v4 on v3

--- a/solution.py
+++ b/solution.py
@@ -244,7 +244,9 @@
 
 def apply_kernel(mode, counts, tails, rows_ref, limit_ref, which_ref, *refs):
     refs = list(refs)
-    pieces, own, near, far = ([refs.pop(0) for _ in range(count)] for count in counts)
+    whole, pieces, own, near, far = ([refs.pop(0) for _ in range(count)] for count in counts)
+    whole = whole[0]
+    split_row = whole.shape[0]
     lefts = own[0], near, far
     right, known_ref = refs.pop(0), refs.pop(0)
     states, outs = refs[:mode], refs[mode:-6]
@@ -253,6 +255,13 @@
     slot = pl.program_id(0)
     coef_ref = outs[0]
     outs = outs[1:]
+
+    def rows_of(row, number):
+        if not pieces:
+            return whole[pl.ds(row, number), :]
+        early = whole[pl.ds(pl.multiple_of(jnp.minimum(row, split_row - number), 8), number), :]
+        late = blocks[pl.ds(pl.multiple_of(jnp.maximum(row - split_row, 0), 8), number), :]
+        return jnp.where(row < split_row, early, late)
 
     @pl.when(slot == 0)
     def _():
@@ -270,9 +279,11 @@
             start_fetch(early, which_ref[0], lefts, right, left_copy, right_copy, sems)
         for copy in copies:
             copy.wait()
-        sums = blocks[tails[0] : tails[0] + TAIL, :]
-        for tail in tails[1:]:
-            sums = sums + blocks[tail : tail + TAIL, :]
+        sums = None
+        for tail in tails:
+            source, at = (whole, tail) if tail < split_row else (blocks, tail - split_row)
+            part = source[at : at + TAIL, :]
+            sums = part if sums is None else sums + part
         coef_ref[...] = next_coefs(mode, known_ref[...], sums)
 
     @pl.when(slot + AHEAD < pl.num_programs(0))
@@ -282,7 +293,7 @@
     wait_fetch(slot, lefts, right, left_copy, right_copy, sems)
     for term in range(terms):
         row = pl.multiple_of(rows_ref[slot, term], 8)
-        first = jnp.concatenate(split(blocks[pl.ds(row, blk), :]), axis=1)
+        first = jnp.concatenate(split(rows_of(row, blk)), axis=1)
         value = folded(dot(first, right_factor(*split(right_copy[term, slot]))))
         inner[term * blk : (term + 1) * blk, :] = jnp.concatenate(split(value), axis=1)
     result = None
@@ -324,7 +335,7 @@
     put_sums(slot, products, outs[1].at[pl.ds(outs[1].shape[0] - TAIL, TAIL), :])
 
 
-def apply(rows, limit, which, tails, pieces, lefts, right, known, states):
+def apply(rows, limit, which, tails, whole, pieces, lefts, right, known, states):
     mode = len(states)
     terms, slots, blk, _ = right.shape
     vector = jax.ShapeDtypeStruct((slots, blk, blk), jnp.float32)
@@ -339,16 +350,17 @@
     else:
         out_shape = [few, vector, vector, few]
         out_specs = [few_spec, vector_spec, vector_spec, few_spec]
-    total = sum(piece.shape[0] for piece in pieces)
+    total = sum(piece.shape[0] for piece in pieces) or TAIL
     own, near, far = lefts
-    counts = (len(pieces), 1, len(near), len(far))
+    counts = (1, len(pieces), 1, len(near), len(far))
     return pl.pallas_call(
         functools.partial(apply_kernel, mode, counts, tails),
         out_shape=out_shape,
         grid_spec=pltpu.PrefetchScalarGridSpec(
             num_scalar_prefetch=3,
             grid=(slots,),
-            in_specs=[pl.BlockSpec(memory_space=pl.ANY)] * (sum(counts) + 1)
+            in_specs=[pl.BlockSpec(memory_space=pltpu.VMEM)]
+            + [pl.BlockSpec(memory_space=pl.ANY)] * sum(counts)
             + [few_spec]
             + [vector_spec] * mode,
             out_specs=out_specs,
@@ -358,14 +370,19 @@
                 pltpu.VMEM(right.shape, jnp.float32),
                 pltpu.VMEM((terms * blk, 2 * blk), jnp.bfloat16),
                 pltpu.SemaphoreType.DMA((1 + len(near), slots)),
-                pltpu.SemaphoreType.DMA((len(pieces),)),
+                pltpu.SemaphoreType.DMA((max(len(pieces), 1),)),
             ],
         ),
-        compiler_params=pltpu.CompilerParams(vmem_limit_bytes=30 * MIB),
+        compiler_params=pltpu.CompilerParams(vmem_limit_bytes=26 * MIB),
         cost_estimate=pl.CostEstimate(
             flops=8 * terms * slots * blk**3, bytes_accessed=12 * right.size, transcendentals=0
         ),
-    )(rows, limit, which, *pieces, own, *near, *far, right, known, *states)
+    )(
+        rows,
+        limit,
+        which,
+        pltpu.with_memory_space_constraint(whole, pltpu.VMEM),
+        *pieces, own, *near, *far, right, known, *states)
 
 
 def finish_kernel(sums_ref, coef_ref, one_ref, other_ref, out_ref, energy_ref):
@@ -398,13 +415,41 @@
     return lax.ppermute(value, "sector", [(index, partner(index, move)) for index in range(count)])
 
 
+def lay_kernel(*refs):
+    parts, (out_ref, sems) = refs[:-2], refs[-2:]
+    copies = []
+    at = 0
+    for number, part in enumerate(parts):
+        size = part.shape[0]
+        copies.append(
+            pltpu.make_async_copy(part, out_ref.at[pl.ds(at, size), :], sems.at[number])
+        )
+        at += size
+    for copy in copies:
+        copy.start()
+    for copy in copies:
+        copy.wait()
+
+
+def lay(parts):
+    total = sum(part.shape[0] for part in parts)
+    return pl.pallas_call(
+        lay_kernel,
+        out_shape=pltpu.VMEM((total, parts[0].shape[1]), jnp.float32),
+        in_specs=[pl.BlockSpec(memory_space=pl.ANY)] * len(parts),
+        out_specs=pl.BlockSpec(memory_space=pltpu.VMEM),
+        scratch_shapes=[pltpu.SemaphoreType.DMA((len(parts),))],
+        compiler_params=pltpu.CompilerParams(vmem_limit_bytes=1 * MIB),
+        cost_estimate=pl.CostEstimate(flops=0, bytes_accessed=8 * total * 128, transcendentals=0),
+    )(*parts)
+
+
 def gather(quarters, count):
     held = list(quarters)
     for step in range(len(ORDERS[0])):
-        last = step == len(ORDERS[0]) - 1
         came = [swap(value, order[step], count) for value, order in zip(held, ORDERS)]
-        if last:
-            return [piece for pair in zip(held, came) for piece in pair]
+        if step == len(ORDERS[0]) - 1:
+            return lay(held), came, held[0]
         held = [jnp.concatenate(pair, axis=0) for pair in zip(held, came)]
 
 
@@ -420,14 +465,16 @@
     apart = {"z": apart // SIDE, "y": apart % SIDE}
     per = sdev // PARTS
     sizes = heights(sdev, blk)
+    units = SIDE * SIDE // 2
     rows = jnp.zeros_like(source)
     base = 0
     for part, order in enumerate(ORDERS):
         (near, one), (_, two), (far, three), (_, four) = order
         unit = place_of(apart[near], (one, two)) + SIDE * place_of(apart[far], (three, four))
-        here = base + unit * sizes[part] + (slot % per) * blk
+        here = base + unit % units * sizes[part] + unit // units * units * sum(sizes)
+        here = here + (slot % per) * blk
         rows = jnp.where(slot // per == part, here, rows)
-        base += SIDE * SIDE * sizes[part]
+        base += units * sizes[part]
     return rows
 
 
@@ -498,17 +545,24 @@
     first_rows = (source // sdev) * height + (source % sdev) * blk
     known = jnp.zeros((TAIL, blk), jnp.float32)
     known, y0, *quarters = apply(
-        first_rows, limit, which, tails, [whole], lefts, right, known, [k0]
+        first_rows, limit, which, tails, whole, [], lefts, right, known, [k0]
     )
-    height = heights(sdev, blk)[0]
-    tails = [unit * height + height - TAIL for unit in range(SIDE * SIDE)]
-    pieces = gather(quarters, devices)
-    updated = join(parts, pieces[0])
-    pieces, updated = lax.optimization_barrier((pieces, updated))
-    known, z1, *quarters = apply(rows, limit, which, tails, pieces, lefts, right, known, [k0, y0])
-    pieces = gather(quarters, devices)
+    sizes = heights(sdev, blk)
+    units = SIDE * SIDE // 2
+    tails = [
+        half * units * sum(sizes) + unit * sizes[0] + sizes[0] - TAIL
+        for half in range(2)
+        for unit in range(units)
+    ]
+    held, came, first = gather(quarters, devices)
+    updated = join(parts, first)
+    held, came, updated = lax.optimization_barrier((held, came, updated))
+    known, z1, *quarters = apply(
+        rows, limit, which, tails, held, came, lefts, right, known, [k0, y0]
+    )
+    held, came, _ = gather(quarters, devices)
     known, x1, r2, sums = apply(
-        rows, limit, which, tails, pieces, lefts, right, known, [k0, y0, z1]
+        rows, limit, which, tails, held, came, lefts, right, known, [k0, y0, z1]
     )
     for axis in ("y", "z"):
         others = [swap(sums, (axis, flip), devices) for flip in range(1, SIDE)]

time: 260 us -> 258 us (level)
  starting transfers between devices: 83.4 us -> 78.3 us
  waiting for transfers between devices: 96.3 us -> 99.6 us
    ppermute x38, starting transfers between devices: 56.4 us -> 51.2 us  [swap(): lax.ppermute(value, 'sector', [(index, partner(index, move)) for index in...]
    ppermute x38, waiting for transfers between devices: 58.1 us -> 61.3 us  [swap(): lax.ppermute(value, 'sector', [(index, partner(index, move)) for index in...]
  transfers between devices with their start and end apart: 47 -> 47, of which waited for: 27 -> 26; matrix products, arithmetic and copies ran while one was open for 2% -> 2% of each run, Pallas kernels for 9% -> 9%
where the time goes in v4:
time: 258 us; the launch traced here: 257 us
  waiting for transfers between devices  99.6 us (39%)
  starting transfers between devices  78.3 us (30%)
  Pallas kernels  56 us (22%)
  between operations  14.7 us (6%)
  local copies, waits for them, and re-layouts  8.21 us (3%)
    ppermute x38, waiting for transfers between devices, swap(): lax.ppermute(value, 'sector', [(index, partner(index, move)) for index in...  61.3 us
    ppermute x38, starting transfers between devices, swap(): lax.ppermute(value, 'sector', [(index, partner(index, move)) for index in...  51.2 us
    pallas_call x3, Pallas kernels, apply(): pl.pallas_call(functools.partial(apply_kernel, mode, counts, tails), out_...  28.8 us
    ppermute x2, waiting for transfers between devices, to_next_round(): near = value = lax.ppermute(value, 'chain', pairs)  20.7 us
    ppermute x4, waiting for transfers between devices, to_next_round(): value = lax.ppermute(value, 'chain', pairs)  17.5 us
    ppermute x4, starting transfers between devices, to_next_round(): value = lax.ppermute(value, 'chain', pairs)  15.7 us
    pallas_call x4, Pallas kernels, update(): pl.pallas_call(update_kernel, out_shape=jax.ShapeDtypeStruct((some, slots...  14.5 us
    pallas_call x1, Pallas kernels, join(): pl.pallas_call(functools.partial(join_kernel, starts), out_shape=jax.Shap...  9.06 us
  transfers between devices with their start and end apart: 47, of which 26 were waited for; matrix products, arithmetic and copies ran while one was open for 2% of the time, Pallas kernels for 9%

profile of v4, /device:TPU:0, one launch (start us, length us, event | category | flops | bytes accessed | tf_op | source)
XLA Modules:
  0.0 257.3 jit_solution(13897647258946609846)
XLA Ops:
  9.3 6.8 %shard_map.104.refs_0_ = f32[8,8,128,128]{3,2,1,0:T(8,128)} custom-call(f32[16,8,128,128]{3,2,1,0:T(8,128)} %bitcast.30, f32[8,128,128]{2,1,0:T(8,128)S(1)} %bitcast.26), custom_call_target="tpu_custom_call" | custom-call | flops 1073741824 | bytes 8388608 | tf_op jit(solution)/shard_map/pallas_call | solution.py:69
  16.1 3.3 %collective-permute-start = (f32[8,8,128,128]{3,2,1,0:T(8,128)}, f32[8,8,128,128]{3,2,1,0:T(8,128)}, u32[]{:S(2)}, u32[]{:S(2)}) collective-permute-start(f32[8,8,128,128]{3,2,1,0:T(8,128)} %shard_map.104.refs_0_), channel_id=1, source_target_pairs={{0,16},{16,32},{32,48},{48,64},{64,80},{80,96},{96,112},{1,17},{17... | collective-permute-start | bytes 12582920 | tf_op jit(solution)/shard_map/ppermute | solution.py:483
  26.1 3.2 %collective-permute-start.3 = (f32[2,8,128,128]{3,2,1,0:T(8,128)S(1)}, f32[2,8,128,128]{3,2,1,0:T(8,128)}, u32[]{:S(2)}, u32[]{:S(2)}) collective-permute-start(f32[2,8,128,128]{3,2,1,0:T(8,128)S(1)} %shard_map.107.refs_3_), channel_id=1, source_target_pairs={{0,16},{32,48},{64,80},{96,112},{16,96},{48,0},{80,32},{1,17},{33,... | collective-permute-start | bytes 3145736 | tf_op jit(solution)/shard_map/ppermute | solution.py:491
  29.3 8.6 %collective-permute-done.2.refs_4_.refs_8_ = f32[2,8,128,128]{3,2,1,0:T(8,128)} collective-permute-done((f32[2,8,128,128]{3,2,1,0:T(8,128)S(1)}, f32[2,8,128,128]{3,2,1,0:T(8,128)}, u32[]{:S(2)}, u32[]{:S(2)}) %collective-permute-start.2) | collective-permute-done | bytes 1048608 | tf_op jit(solution)/shard_map/ppermute | solution.py:491
  37.8 4.5 %collective-permute-start.4 = (f32[2,8,128,128]{3,2,1,0:T(8,128)}, f32[2,8,128,128]{3,2,1,0:T(8,128)}, u32[]{:S(2)}, u32[]{:S(2)}) collective-permute-start(f32[2,8,128,128]{3,2,1,0:T(8,128)} %collective-permute-done.2.refs_4_.refs_8_), channel_id=1, source_target_pairs={{96,64},{0,96},{32,0},{97,65},{1,97},{33,1},{98,66},{2,98},{34,2},... | collective-permute-start | bytes 3145736 | tf_op jit(solution)/shard_map/ppermute | solution.py:494
  42.3 12.1 %collective-permute-done.3.refs_5_.refs_9_ = f32[2,8,128,128]{3,2,1,0:T(8,128)} collective-permute-done((f32[2,8,128,128]{3,2,1,0:T(8,128)S(1)}, f32[2,8,128,128]{3,2,1,0:T(8,128)}, u32[]{:S(2)}, u32[]{:S(2)}) %collective-permute-start.3) | collective-permute-done | bytes 1048608 | tf_op jit(solution)/shard_map/ppermute | solution.py:491
  54.5 3.3 %collective-permute-start.6 = (f32[2,8,128,128]{3,2,1,0:T(8,128)}, f32[2,8,128,128]{3,2,1,0:T(8,128)}, u32[]{:S(2)}, u32[]{:S(2)}) collective-permute-start(f32[2,8,128,128]{3,2,1,0:T(8,128)} %collective-permute-done.3.refs_5_.refs_9_), channel_id=1, source_target_pairs={{96,64},{0,96},{32,0},{97,65},{1,97},{33,1},{98,66},{2,98},{34,2},... | collective-permute-start | bytes 3145736 | tf_op jit(solution)/shard_map/ppermute | solution.py:494
  57.8 3.3 %shard_map.105.refs_1_ = f32[4,8,128,128]{3,2,1,0:T(8,128)S(1)} custom-call(f32[16,8,128,128]{3,2,1,0:T(8,128)} %bitcast.33, f32[8,128,128]{2,1,0:T(8,128)S(1)} %bitcast.29), custom_call_target="tpu_custom_call" | custom-call | flops 536870912 | bytes 4194304 | tf_op jit(solution)/shard_map/pallas_call | solution.py:69
  66.8 4.7 %collective-permute-done.6 = f32[2,8,128,128]{3,2,1,0:T(8,128)} collective-permute-done((f32[2,8,128,128]{3,2,1,0:T(8,128)}, f32[2,8,128,128]{3,2,1,0:T(8,128)}, u32[]{:S(2)}, u32[]{:S(2)}) %collective-permute-start.6) | collective-permute-done | bytes 1048608 | tf_op jit(solution)/shard_map/ppermute | solution.py:494
  71.5 5.5 %collective-permute-start.7 = (f32[2,8,128,128]{3,2,1,0:T(8,128)}, f32[2,8,128,128]{3,2,1,0:T(8,128)}, u32[]{:S(2)}, u32[]{:S(2)}) collective-permute-start(f32[2,8,128,128]{3,2,1,0:T(8,128)} %collective-permute-done.6), channel_id=1, source_target_pairs={{64,32},{96,64},{0,96},{65,33},{97,65},{1,97},{66,34},{98,66},{2,9... | collective-permute-start | bytes 3145736 | tf_op jit(solution)/shard_map/ppermute | solution.py:494
  81.7 11.2 %collective-permute-done.7.refs_9_.refs_13_ = f32[2,8,128,128]{3,2,1,0:T(8,128)} collective-permute-done((f32[2,8,128,128]{3,2,1,0:T(8,128)}, f32[2,8,128,128]{3,2,1,0:T(8,128)}, u32[]{:S(2)}, u32[]{:S(2)}) %collective-permute-start.7) | collective-permute-done | bytes 1048608 | tf_op jit(solution)/shard_map/ppermute | solution.py:494
  92.9 3.4 %copy-done = f32[16512,128]{1,0:T(8,128)S(1)} copy-done((f32[16512,128]{1,0:T(8,128)S(1)}, f32[16512,128]{1,0:T(8,128)}, u32[]{:S(2)}) %copy-start) | copy-done | bytes 8454168
  96.3 9.4 %shard_map.108 = (f32[8,128]{1,0:T(8,128)S(1)}, f32[8,128,128]{2,1,0:T(8,128)S(1)}, f32[264,128]{1,0:T(8,128)S(1)}, f32[256,128]{1,0:T(8,128)S(1)}, f32[256,128]{1,0:T(8,128)S(1)}, /*index=5*/f32[256,128]{1,0:T(8,128)S(1)}) custom-call(s32[8,16]{1,0:T(8,128)S(1)} %get-tuple-element.61.rows_ref, s32[8]{0:T(128)S(1)} %get-tuple-element.32.limit_ref, ...), custom_call_target="tpu_custom_call" | custom-call | flops 2147483648 | bytes 25165824 | tf_op jit(solution)/shard_map/pallas_call | solution.py:356
  105.7 3.1 %collective-permute-start.11 = (f32[256,128]{1,0:T(8,128)S(1)}, f32[256,128]{1,0:T(8,128)S(1)}, u32[]{:S(2)}, u32[]{:S(2)}) collective-permute-start(f32[256,128]{1,0:T(8,128)S(1)} %get-tuple-element.38), channel_id=1, source_target_pairs={{0,3},{1,2},{2,1},{3,0},{4,7},{5,6},{6,5},{7,4},{8,11},{9,10},{10,... | collective-permute-start | bytes 393224 | tf_op jit(solution)/shard_map/ppermute | solution.py:415
  115.6 3.6 %collective-permute-start.15 = (f32[512,128]{1,0:T(8,128)S(1)}, f32[512,128]{1,0:T(8,128)S(1)}, u32[]{:S(2)}, u32[]{:S(2)}) collective-permute-start(f32[512,128]{1,0:T(8,128)S(1)} %pad_maximum_fusion.11), channel_id=1, source_target_pairs={{0,12},{1,13},{2,14},{3,15},{4,8},{5,9},{6,10},{7,11},{8,4},{9,5},... | collective-permute-start | bytes 786440 | tf_op jit(solution)/shard_map/ppermute | solution.py:415
  131.3 11.8 %collective-permute-done.19 = f32[1024,128]{1,0:T(8,128)S(1)} collective-permute-done((f32[1024,128]{1,0:T(8,128)S(1)}, f32[1024,128]{1,0:T(8,128)S(1)}, u32[]{:S(2)}, u32[]{:S(2)}) %collective-permute-start.19) | collective-permute-done | bytes 524320 | tf_op jit(solution)/shard_map/ppermute | solution.py:415
  143.6 3.4 %collective-permute-start.20 = (f32[2112,128]{1,0:T(8,128)S(1)}, f32[2112,128]{1,0:T(8,128)S(1)}, u32[]{:S(2)}, u32[]{:S(2)}) collective-permute-start(f32[2112,128]{1,0:T(8,128)S(1)} %constant_dynamic-update-slice_fusion.refs_0_.refs_4_), channel_id=1, source_target_pairs={{0,12},{1,13},{2,14},{3,15},{4,8},{5,9},{6,10},{7,11},{8,4},{9,5},... | collective-permute-start | bytes 3244040 | tf_op jit(solution)/shard_map/ppermute | solution.py:415
  147.3 9.1 %shard_map.110 = f32[16,8,128,128]{3,2,1,0:T(8,128)} custom-call(f32[8,8,128,128]{3,2,1,0:T(8,128)} %shard_map.104.refs_0_, f32[4,8,128,128]{3,2,1,0:T(8,128)} %copy-done.1, f32[2,8,128,128]{3,2,1,0:T(8,128)} %copy-done.3, f32[2,8,128,128]{3,2,1,0:T(8,128)} %copy-done.4, f32[2112,128]{1,0:T(8,128)S(1)} %constant_dynamic-update-slice_fusion.refs_0_.refs_4_), custom_call_target="tpu_custom_call" | custom-call | bytes 16777216 | tf_op jit(solution)/shard_map/pallas_call | solution.py:111
  158.1 3.4 %collective-permute-done.22.refs_3_ = f32[2048,128]{1,0:T(8,128)S(1)} collective-permute-done((f32[2048,128]{1,0:T(8,128)S(1)}, f32[2048,128]{1,0:T(8,128)S(1)}, u32[]{:S(2)}, u32[]{:S(2)}) %collective-permute-start.22) | collective-permute-done | bytes 1048608 | tf_op jit(solution)/shard_map/ppermute | solution.py:415
  162.1 9.9 %shard_map.111 = (f32[8,128]{1,0:T(8,128)S(1)}, f32[8,128,128]{2,1,0:T(8,128)S(1)}, f32[264,128]{1,0:T(8,128)S(1)}, f32[256,128]{1,0:T(8,128)S(1)}, f32[256,128]{1,0:T(8,128)S(1)}, /*index=5*/f32[256,128]{1,0:T(8,128)S(1)}) custom-call(s32[8,16]{1,0:T(8,128)S(1)} %get-tuple-element.62.rows_ref, s32[8]{0:T(128)S(1)} %get-tuple-element.32.limit_ref, ...), custom_call_target="tpu_custom_call" | custom-call | flops 2147483648 | bytes 25165824 | tf_op jit(solution)/shard_map/pallas_call | solution.py:356
  185.2 2.9 %collective-permute-done.28 = f32[512,128]{1,0:T(8,128)S(1)} collective-permute-done((f32[512,128]{1,0:T(8,128)S(1)}, f32[512,128]{1,0:T(8,128)S(1)}, u32[]{:S(2)}, u32[]{:S(2)}) %collective-permute-start.28) | collective-permute-done | bytes 262176 | tf_op jit(solution)/shard_map/ppermute | solution.py:415
  194.3 12.6 %collective-permute-done.35 = f32[1024,128]{1,0:T(8,128)S(1)} collective-permute-done((f32[1024,128]{1,0:T(8,128)S(1)}, f32[1024,128]{1,0:T(8,128)S(1)}, u32[]{:S(2)}, u32[]{:S(2)}) %collective-permute-start.35) | collective-permute-done | bytes 524320 | tf_op jit(solution)/shard_map/ppermute | solution.py:415
  212.3 9.5 %collective-permute-done.39.refs_4_ = f32[2048,128]{1,0:T(8,128)S(1)} collective-permute-done((f32[2048,128]{1,0:T(8,128)S(1)}, f32[2048,128]{1,0:T(8,128)S(1)}, u32[]{:S(2)}, u32[]{:S(2)}) %collective-permute-start.39) | collective-permute-done | bytes 1048608 | tf_op jit(solution)/shard_map/ppermute | solution.py:415
  225.5 9.5 %shard_map.113 = (f32[8,128]{1,0:T(8,128)S(1)}, f32[8,128,128]{2,1,0:T(8,128)S(1)}, f32[8,128,128]{2,1,0:T(8,128)S(1)}, f32[8,128]{1,0:T(8,128)S(1)}) custom-call(s32[8,16]{1,0:T(8,128)S(1)} %get-tuple-element.62.rows_ref, s32[8]{0:T(128)S(1)} %get-tuple-element.32.limit_ref, s32[1]{0:T(128)} %bitcast.6.which_ref, f32[8256,128]{1,0:T(8,128)S(1)} %shard_map.112.refs_0_, ...), custom_call_target="tpu_custom_call" | custom-call | flops 2147483648 | bytes 25165824 | tf_op jit(solution)/shard_map/pallas_call | solution.py:356
  (164 shorter events, 84.5 us)
Async XLA Ops:
  7.2 85.8 %all-gather.2.cloned.1.call-start = ((), (), s32[]{:S(2)}) async-start(), calls=%async_computation | async-start | bytes 8982528 | tf_op jit(solution)/shard_map/all_gather | solution.py:528
  16.1 76.8 %collective-permute-start = (f32[8,8,128,128]{3,2,1,0:T(8,128)}, f32[8,8,128,128]{3,2,1,0:T(8,128)}, u32[]{:S(2)}, u32[]{:S(2)}) collective-permute-start(f32[8,8,128,128]{3,2,1,0:T(8,128)} %shard_map.104.refs_0_), channel_id=1, source_target_pairs={{0,16},{16,32},{32,48},{48,64},{64,80},{80,96},{96,112},{1,17},{17... | collective-permute-start | bytes 12582920 | tf_op jit(solution)/shard_map/ppermute | solution.py:483
  21.6 16.2 %collective-permute-start.2 = (f32[2,8,128,128]{3,2,1,0:T(8,128)S(1)}, f32[2,8,128,128]{3,2,1,0:T(8,128)}, u32[]{:S(2)}, u32[]{:S(2)}) collective-permute-start(f32[2,8,128,128]{3,2,1,0:T(8,128)S(1)} %shard_map.106.refs_2_), channel_id=1, source_target_pairs={{0,16},{32,48},{64,80},{96,112},{16,96},{48,0},{80,32},{1,17},{33,... | collective-permute-start | bytes 3145736 | tf_op jit(solution)/shard_map/ppermute | solution.py:491
  26.1 28.4 %collective-permute-start.3 = (f32[2,8,128,128]{3,2,1,0:T(8,128)S(1)}, f32[2,8,128,128]{3,2,1,0:T(8,128)}, u32[]{:S(2)}, u32[]{:S(2)}) collective-permute-start(f32[2,8,128,128]{3,2,1,0:T(8,128)S(1)} %shard_map.107.refs_3_), channel_id=1, source_target_pairs={{0,16},{32,48},{64,80},{96,112},{16,96},{48,0},{80,32},{1,17},{33,... | collective-permute-start | bytes 3145736 | tf_op jit(solution)/shard_map/ppermute | solution.py:491
  37.8 26.7 %collective-permute-start.4 = (f32[2,8,128,128]{3,2,1,0:T(8,128)}, f32[2,8,128,128]{3,2,1,0:T(8,128)}, u32[]{:S(2)}, u32[]{:S(2)}) collective-permute-start(f32[2,8,128,128]{3,2,1,0:T(8,128)} %collective-permute-done.2.refs_4_.refs_8_), channel_id=1, source_target_pairs={{96,64},{0,96},{32,0},{97,65},{1,97},{33,1},{98,66},{2,98},{34,2},... | collective-permute-start | bytes 3145736 | tf_op jit(solution)/shard_map/ppermute | solution.py:494
  54.5 17.1 %collective-permute-start.6 = (f32[2,8,128,128]{3,2,1,0:T(8,128)}, f32[2,8,128,128]{3,2,1,0:T(8,128)}, u32[]{:S(2)}, u32[]{:S(2)}) collective-permute-start(f32[2,8,128,128]{3,2,1,0:T(8,128)} %collective-permute-done.3.refs_5_.refs_9_), channel_id=1, source_target_pairs={{96,64},{0,96},{32,0},{97,65},{1,97},{33,1},{98,66},{2,98},{34,2},... | collective-permute-start | bytes 3145736 | tf_op jit(solution)/shard_map/ppermute | solution.py:494
  61.1 19.0 %collective-permute-start.1 = (f32[4,8,128,128]{3,2,1,0:T(8,128)S(1)}, f32[4,8,128,128]{3,2,1,0:T(8,128)}, u32[]{:S(2)}, u32[]{:S(2)}) collective-permute-start(f32[4,8,128,128]{3,2,1,0:T(8,128)S(1)} %shard_map.105.refs_1_), channel_id=1, source_target_pairs={{0,16},{16,32},{32,48},{48,64},{64,80},{80,96},{96,112},{1,17},{17... | collective-permute-start | bytes 6291464 | tf_op jit(solution)/shard_map/ppermute | solution.py:483
  64.5 17.2 %collective-permute-start.5 = (f32[2,8,128,128]{3,2,1,0:T(8,128)}, f32[2,8,128,128]{3,2,1,0:T(8,128)}, u32[]{:S(2)}, u32[]{:S(2)}) collective-permute-start(f32[2,8,128,128]{3,2,1,0:T(8,128)} %collective-permute-done.4), channel_id=1, source_target_pairs={{64,32},{96,64},{0,96},{65,33},{97,65},{1,97},{66,34},{98,66},{2,9... | collective-permute-start | bytes 3145736 | tf_op jit(solution)/shard_map/ppermute | solution.py:494
  71.5 21.4 %collective-permute-start.7 = (f32[2,8,128,128]{3,2,1,0:T(8,128)}, f32[2,8,128,128]{3,2,1,0:T(8,128)}, u32[]{:S(2)}, u32[]{:S(2)}) collective-permute-start(f32[2,8,128,128]{3,2,1,0:T(8,128)} %collective-permute-done.6), channel_id=1, source_target_pairs={{64,32},{96,64},{0,96},{65,33},{97,65},{1,97},{66,34},{98,66},{2,9... | collective-permute-start | bytes 3145736 | tf_op jit(solution)/shard_map/ppermute | solution.py:494
  121.8 25.2 %collective-permute-start.13 = (f32[1024,128]{1,0:T(8,128)S(1)}, f32[1024,128]{1,0:T(8,128)S(1)}, u32[]{:S(2)}, u32[]{:S(2)}) collective-permute-start(f32[1024,128]{1,0:T(8,128)S(1)} %pad_maximum_fusion.2), channel_id=1, source_target_pairs={{0,12},{1,13},{2,14},{3,15},{4,8},{5,9},{6,10},{7,11},{8,4},{9,5},... | collective-permute-start | bytes 1572872 | tf_op jit(solution)/shard_map/ppermute | solution.py:415
  126.1 17.1 %collective-permute-start.16 = (f32[1024,128]{1,0:T(8,128)S(1)}, f32[1024,128]{1,0:T(8,128)S(1)}, u32[]{:S(2)}, u32[]{:S(2)}) collective-permute-start(f32[1024,128]{1,0:T(8,128)S(1)} %pad_maximum_fusion.3), channel_id=1, source_target_pairs={{0,1},{1,0},{2,3},{3,2},{4,5},{5,4},{6,7},{7,6},{8,9},{9,8},{10,11... | collective-permute-start | bytes 1572872 | tf_op jit(solution)/shard_map/ppermute | solution.py:415
  128.5 14.6 %collective-permute-start.19 = (f32[1024,128]{1,0:T(8,128)S(1)}, f32[1024,128]{1,0:T(8,128)S(1)}, u32[]{:S(2)}, u32[]{:S(2)}) collective-permute-start(f32[1024,128]{1,0:T(8,128)S(1)} %pad_maximum_fusion.4), channel_id=1, source_target_pairs={{0,3},{1,2},{2,1},{3,0},{4,7},{5,6},{6,5},{7,4},{8,11},{9,10},{10,... | collective-permute-start | bytes 1572872 | tf_op jit(solution)/shard_map/ppermute | solution.py:415
  143.2 14.9 %collective-permute-start.23 = (f32[2048,128]{1,0:T(8,128)S(1)}, f32[2048,128]{1,0:T(8,128)S(1)}, u32[]{:S(2)}, u32[]{:S(2)}) collective-permute-start(f32[2048,128]{1,0:T(8,128)S(1)} %constant_dynamic-update-slice_fusion.12.refs_3_), channel_id=1, source_target_pairs={{0,1},{1,0},{2,3},{3,2},{4,5},{5,4},{6,7},{7,6},{8,9},{9,8},{10,11... | collective-permute-start | bytes 3145736 | tf_op jit(solution)/shard_map/ppermute | solution.py:415
  143.3 18.2 %collective-permute-start.22 = (f32[2048,128]{1,0:T(8,128)S(1)}, f32[2048,128]{1,0:T(8,128)S(1)}, u32[]{:S(2)}, u32[]{:S(2)}) collective-permute-start(f32[2048,128]{1,0:T(8,128)S(1)} %constant_dynamic-update-slice_fusion.8.refs_2_), channel_id=1, source_target_pairs={{0,3},{1,2},{2,1},{3,0},{4,7},{5,6},{6,5},{7,4},{8,11},{9,10},{10,... | collective-permute-start | bytes 3145736 | tf_op jit(solution)/shard_map/ppermute | solution.py:415
  143.6 18.5 %collective-permute-start.20 = (f32[2112,128]{1,0:T(8,128)S(1)}, f32[2112,128]{1,0:T(8,128)S(1)}, u32[]{:S(2)}, u32[]{:S(2)}) collective-permute-start(f32[2112,128]{1,0:T(8,128)S(1)} %constant_dynamic-update-slice_fusion.refs_0_.refs_4_), channel_id=1, source_target_pairs={{0,12},{1,13},{2,14},{3,15},{4,8},{5,9},{6,10},{7,11},{8,4},{9,5},... | collective-permute-start | bytes 3244040 | tf_op jit(solution)/shard_map/ppermute | solution.py:415
  147.1 15.1 %collective-permute-start.21 = (f32[2048,128]{1,0:T(8,128)S(1)}, f32[2048,128]{1,0:T(8,128)S(1)}, u32[]{:S(2)}, u32[]{:S(2)}) collective-permute-start(f32[2048,128]{1,0:T(8,128)S(1)} %constant_dynamic-update-slice_fusion.4.refs_1_), channel_id=1, source_target_pairs={{0,4},{1,5},{2,6},{3,7},{4,0},{5,1},{6,2},{7,3},{8,12},{9,13},{10,... | collective-permute-start | bytes 3145736 | tf_op jit(solution)/shard_map/ppermute | solution.py:415
  188.1 22.3 %collective-permute-start.29 = (f32[1024,128]{1,0:T(8,128)S(1)}, f32[1024,128]{1,0:T(8,128)S(1)}, u32[]{:S(2)}, u32[]{:S(2)}) collective-permute-start(f32[1024,128]{1,0:T(8,128)S(1)} %pad_maximum_fusion.5), channel_id=1, source_target_pairs={{0,12},{1,13},{2,14},{3,15},{4,8},{5,9},{6,10},{7,11},{8,4},{9,5},... | collective-permute-start | bytes 1572872 | tf_op jit(solution)/shard_map/ppermute | solution.py:415
  189.5 17.5 %collective-permute-start.32 = (f32[1024,128]{1,0:T(8,128)S(1)}, f32[1024,128]{1,0:T(8,128)S(1)}, u32[]{:S(2)}, u32[]{:S(2)}) collective-permute-start(f32[1024,128]{1,0:T(8,128)S(1)} %pad_maximum_fusion.6), channel_id=1, source_target_pairs={{0,1},{1,0},{2,3},{3,2},{4,5},{5,4},{6,7},{7,6},{8,9},{9,8},{10,11... | collective-permute-start | bytes 1572872 | tf_op jit(solution)/shard_map/ppermute | solution.py:415
  190.7 16.2 %collective-permute-start.35 = (f32[1024,128]{1,0:T(8,128)S(1)}, f32[1024,128]{1,0:T(8,128)S(1)}, u32[]{:S(2)}, u32[]{:S(2)}) collective-permute-start(f32[1024,128]{1,0:T(8,128)S(1)} %pad_maximum_fusion.7), channel_id=1, source_target_pairs={{0,3},{1,2},{2,1},{3,0},{4,7},{5,6},{6,5},{7,4},{8,11},{9,10},{10,... | collective-permute-start | bytes 1572872 | tf_op jit(solution)/shard_map/ppermute | solution.py:415
  192.7 16.3 %collective-permute-start.26 = (f32[1056,128]{1,0:T(8,128)S(1)}, f32[1056,128]{1,0:T(8,128)S(1)}, u32[]{:S(2)}, u32[]{:S(2)}) collective-permute-start(f32[1056,128]{1,0:T(8,128)S(1)} %pad_maximum_fusion.1), channel_id=1, source_target_pairs={{0,4},{1,5},{2,6},{3,7},{4,0},{5,1},{6,2},{7,3},{8,12},{9,13},{10,... | collective-permute-start | bytes 1622024 | tf_op jit(solution)/shard_map/ppermute | solution.py:415
  206.9 14.9 %collective-permute-start.39 = (f32[2048,128]{1,0:T(8,128)S(1)}, f32[2048,128]{1,0:T(8,128)S(1)}, u32[]{:S(2)}, u32[]{:S(2)}) collective-permute-start(f32[2048,128]{1,0:T(8,128)S(1)} %constant_dynamic-update-slice_fusion.28.refs_3_), channel_id=1, source_target_pairs={{0,1},{1,0},{2,3},{3,2},{4,5},{5,4},{6,7},{7,6},{8,9},{9,8},{10,11... | collective-permute-start | bytes 3145736 | tf_op jit(solution)/shard_map/ppermute | solution.py:415
  207.1 16.1 %collective-permute-start.38 = (f32[2048,128]{1,0:T(8,128)S(1)}, f32[2048,128]{1,0:T(8,128)S(1)}, u32[]{:S(2)}, u32[]{:S(2)}) collective-permute-start(f32[2048,128]{1,0:T(8,128)S(1)} %constant_dynamic-update-slice_fusion.24.refs_2_), channel_id=1, source_target_pairs={{0,3},{1,2},{2,1},{3,0},{4,7},{5,6},{6,5},{7,4},{8,11},{9,10},{10,... | collective-permute-start | bytes 3145736 | tf_op jit(solution)/shard_map/ppermute | solution.py:415
  209.0 16.4 %collective-permute-start.36 = (f32[2112,128]{1,0:T(8,128)S(1)}, f32[2112,128]{1,0:T(8,128)S(1)}, u32[]{:S(2)}, u32[]{:S(2)}) collective-permute-start(f32[2112,128]{1,0:T(8,128)S(1)} %constant_dynamic-update-slice_fusion.16.refs_0_), channel_id=1, source_target_pairs={{0,12},{1,13},{2,14},{3,15},{4,8},{5,9},{6,10},{7,11},{8,4},{9,5},... | collective-permute-start | bytes 3244040 | tf_op jit(solution)/shard_map/ppermute | solution.py:415
  210.4 14.9 %collective-permute-start.37 = (f32[2048,128]{1,0:T(8,128)S(1)}, f32[2048,128]{1,0:T(8,128)S(1)}, u32[]{:S(2)}, u32[]{:S(2)}) collective-permute-start(f32[2048,128]{1,0:T(8,128)S(1)} %constant_dynamic-update-slice_fusion.20.refs_1_), channel_id=1, source_target_pairs={{0,4},{1,5},{2,6},{3,7},{4,0},{5,1},{6,2},{7,3},{8,12},{9,13},{10,... | collective-permute-start | bytes 3145736 | tf_op jit(solution)/shard_map/ppermute | solution.py:415
  (30 other events, 315.4 us)
Sparse Core Ops, SparseCore 0:
  10.8 73.6 all-gather.1

commit v5 on v4

--- a/solution.py
+++ b/solution.py
@@ -545,7 +545,7 @@
     first_rows = (source // sdev) * height + (source % sdev) * blk
     known = jnp.zeros((TAIL, blk), jnp.float32)
     known, y0, *quarters = apply(
-        first_rows, limit, which, tails, whole, [], lefts, right, known, [k0]
+        first_rows, limit, which, tails, lay([in_hbm(whole)]), [], lefts, right, known, [k0]
     )
     sizes = heights(sdev, blk)
     units = SIDE * SIDE // 2

time: 258 us -> 255 us (0.988)
  waiting for transfers between devices: 99.6 us -> 96.1 us
  local copies, waits for them, and re-layouts: 8.21 us -> 4.81 us
  Pallas kernels: 56 us -> 59.4 us
    ppermute x4, waiting for transfers between devices: 17.5 us -> 9.7 us  [to_next_round(): value = lax.ppermute(value, 'chain', pairs)]
    all_gather x1, waiting for transfers between devices: 0.01 us -> 4.38 us  [body(): whole = lax.all_gather(packed, 'sector', axis=0, tiled=True)]
    pallas_call x2 -> x3, Pallas kernels: 0.72 us -> 4.13 us  [lay(): pl.pallas_call(lay_kernel, out_shape=pltpu.VMEM((total, parts[0].shape[1]...]
    unnamed x38 -> x36, local copies, waits for them, and re-layouts: 3.85 us -> 0.45 us
  transfers between devices with their start and end apart: 47 -> 47, of which waited for: 26 -> 25; matrix products, arithmetic and copies ran while one was open for 2% -> 2% of each run, Pallas kernels for 9% -> 11%
where the time goes in v5:
time: 255 us; the launch traced here: 254 us
  waiting for transfers between devices  96.1 us (38%)
  starting transfers between devices  78.3 us (31%)
  Pallas kernels  59.4 us (23%)
  between operations  14.7 us (6%)
  local copies, waits for them, and re-layouts  4.81 us (2%)
    ppermute x38, waiting for transfers between devices, swap(): lax.ppermute(value, 'sector', [(index, partner(index, move)) for index in...  61.4 us
    ppermute x38, starting transfers between devices, swap(): lax.ppermute(value, 'sector', [(index, partner(index, move)) for index in...  51.2 us
    pallas_call x3, Pallas kernels, apply(): pl.pallas_call(functools.partial(apply_kernel, mode, counts, tails), out_...  28.8 us
    ppermute x2, waiting for transfers between devices, to_next_round(): near = value = lax.ppermute(value, 'chain', pairs)  20.7 us
    ppermute x4, starting transfers between devices, to_next_round(): value = lax.ppermute(value, 'chain', pairs)  15.7 us
    pallas_call x4, Pallas kernels, update(): pl.pallas_call(update_kernel, out_shape=jax.ShapeDtypeStruct((some, slots...  14.5 us
    ppermute x4, waiting for transfers between devices, to_next_round(): value = lax.ppermute(value, 'chain', pairs)  9.7 us
    pallas_call x1, Pallas kernels, join(): pl.pallas_call(functools.partial(join_kernel, starts), out_shape=jax.Shap...  9.06 us
  transfers between devices with their start and end apart: 47, of which 25 were waited for; matrix products, arithmetic and copies ran while one was open for 2% of the time, Pallas kernels for 11%

profile of v5, /device:TPU:0, one launch (start us, length us, event | category | flops | bytes accessed | tf_op | source)
XLA Modules:
  0.0 253.9 jit_solution(18203843833023716210)
XLA Ops:
  9.3 6.8 %shard_map.105.refs_0_ = f32[8,8,128,128]{3,2,1,0:T(8,128)} custom-call(f32[16,8,128,128]{3,2,1,0:T(8,128)} %bitcast.30, f32[8,128,128]{2,1,0:T(8,128)S(1)} %bitcast.26), custom_call_target="tpu_custom_call" | custom-call | flops 1073741824 | bytes 8388608 | tf_op jit(solution)/shard_map/pallas_call | solution.py:69
  16.1 3.4 %collective-permute-start = (f32[8,8,128,128]{3,2,1,0:T(8,128)}, f32[8,8,128,128]{3,2,1,0:T(8,128)}, u32[]{:S(2)}, u32[]{:S(2)}) collective-permute-start(f32[8,8,128,128]{3,2,1,0:T(8,128)} %shard_map.105.refs_0_), channel_id=1, source_target_pairs={{0,16},{16,32},{32,48},{48,64},{64,80},{80,96},{96,112},{1,17},{17... | collective-permute-start | bytes 12582920 | tf_op jit(solution)/shard_map/ppermute | solution.py:483
  26.1 3.2 %collective-permute-start.3 = (f32[2,8,128,128]{3,2,1,0:T(8,128)S(1)}, f32[2,8,128,128]{3,2,1,0:T(8,128)}, u32[]{:S(2)}, u32[]{:S(2)}) collective-permute-start(f32[2,8,128,128]{3,2,1,0:T(8,128)S(1)} %shard_map.108.refs_3_), channel_id=1, source_target_pairs={{0,16},{32,48},{64,80},{96,112},{16,96},{48,0},{80,32},{1,17},{33,... | collective-permute-start | bytes 3145736 | tf_op jit(solution)/shard_map/ppermute | solution.py:491
  29.3 8.6 %collective-permute-done.2.refs_4_.refs_8_ = f32[2,8,128,128]{3,2,1,0:T(8,128)} collective-permute-done((f32[2,8,128,128]{3,2,1,0:T(8,128)S(1)}, f32[2,8,128,128]{3,2,1,0:T(8,128)}, u32[]{:S(2)}, u32[]{:S(2)}) %collective-permute-start.2) | collective-permute-done | bytes 1048608 | tf_op jit(solution)/shard_map/ppermute | solution.py:491
  37.8 4.5 %collective-permute-start.4 = (f32[2,8,128,128]{3,2,1,0:T(8,128)}, f32[2,8,128,128]{3,2,1,0:T(8,128)}, u32[]{:S(2)}, u32[]{:S(2)}) collective-permute-start(f32[2,8,128,128]{3,2,1,0:T(8,128)} %collective-permute-done.2.refs_4_.refs_8_), channel_id=1, source_target_pairs={{96,64},{0,96},{32,0},{97,65},{1,97},{33,1},{98,66},{2,98},{34,2},... | collective-permute-start | bytes 3145736 | tf_op jit(solution)/shard_map/ppermute | solution.py:494
  42.4 12.1 %collective-permute-done.3.refs_5_.refs_9_ = f32[2,8,128,128]{3,2,1,0:T(8,128)} collective-permute-done((f32[2,8,128,128]{3,2,1,0:T(8,128)S(1)}, f32[2,8,128,128]{3,2,1,0:T(8,128)}, u32[]{:S(2)}, u32[]{:S(2)}) %collective-permute-start.3) | collective-permute-done | bytes 1048608 | tf_op jit(solution)/shard_map/ppermute | solution.py:491
  54.5 3.3 %collective-permute-start.6 = (f32[2,8,128,128]{3,2,1,0:T(8,128)}, f32[2,8,128,128]{3,2,1,0:T(8,128)}, u32[]{:S(2)}, u32[]{:S(2)}) collective-permute-start(f32[2,8,128,128]{3,2,1,0:T(8,128)} %collective-permute-done.3.refs_5_.refs_9_), channel_id=1, source_target_pairs={{96,64},{0,96},{32,0},{97,65},{1,97},{33,1},{98,66},{2,98},{34,2},... | collective-permute-start | bytes 3145736 | tf_op jit(solution)/shard_map/ppermute | solution.py:494
  57.8 3.3 %shard_map.106.refs_1_ = f32[4,8,128,128]{3,2,1,0:T(8,128)S(1)} custom-call(f32[16,8,128,128]{3,2,1,0:T(8,128)} %bitcast.33, f32[8,128,128]{2,1,0:T(8,128)S(1)} %bitcast.29), custom_call_target="tpu_custom_call" | custom-call | flops 536870912 | bytes 4194304 | tf_op jit(solution)/shard_map/pallas_call | solution.py:69
  66.9 4.7 %collective-permute-done.6 = f32[2,8,128,128]{3,2,1,0:T(8,128)} collective-permute-done((f32[2,8,128,128]{3,2,1,0:T(8,128)}, f32[2,8,128,128]{3,2,1,0:T(8,128)}, u32[]{:S(2)}, u32[]{:S(2)}) %collective-permute-start.6) | collective-permute-done | bytes 1048608 | tf_op jit(solution)/shard_map/ppermute | solution.py:494
  71.5 5.5 %collective-permute-start.7 = (f32[2,8,128,128]{3,2,1,0:T(8,128)}, f32[2,8,128,128]{3,2,1,0:T(8,128)}, u32[]{:S(2)}, u32[]{:S(2)}) collective-permute-start(f32[2,8,128,128]{3,2,1,0:T(8,128)} %collective-permute-done.6), channel_id=1, source_target_pairs={{64,32},{96,64},{0,96},{65,33},{97,65},{1,97},{66,34},{98,66},{2,9... | collective-permute-start | bytes 3145736 | tf_op jit(solution)/shard_map/ppermute | solution.py:494
  80.1 4.4 %all-gather.2.cloned.1.call-done.refs_0_ = f32[16512,128]{1,0:T(8,128)} async-done(((f32[1032,128]{1,0:T(8,128)}), f32[16512,128]{1,0:T(8,128)}) %all-gather.2.cloned.1.call-update) | async-done | bytes 8454160 | tf_op jit(solution)/shard_map/all_gather | solution.py:528
  84.5 3.4 %shard_map.104.refs_0_ = f32[16512,128]{1,0:T(8,128)S(1)} custom-call(f32[16512,128]{1,0:T(8,128)} %all-gather.2.cloned.1.call-done.refs_0_), custom_call_target="tpu_custom_call" | custom-call | bytes 16908288 | tf_op jit(solution)/shard_map/pallas_call | solution.py:436
  87.9 5.0 %collective-permute-done.7.refs_9_.refs_13_ = f32[2,8,128,128]{3,2,1,0:T(8,128)} collective-permute-done((f32[2,8,128,128]{3,2,1,0:T(8,128)}, f32[2,8,128,128]{3,2,1,0:T(8,128)}, u32[]{:S(2)}, u32[]{:S(2)}) %collective-permute-start.7) | collective-permute-done | bytes 1048608 | tf_op jit(solution)/shard_map/ppermute | solution.py:494
  92.9 9.4 %shard_map.109 = (f32[8,128]{1,0:T(8,128)S(1)}, f32[8,128,128]{2,1,0:T(8,128)S(1)}, f32[264,128]{1,0:T(8,128)S(1)}, f32[256,128]{1,0:T(8,128)S(1)}, f32[256,128]{1,0:T(8,128)S(1)}, /*index=5*/f32[256,128]{1,0:T(8,128)S(1)}) custom-call(s32[8,16]{1,0:T(8,128)S(1)} %get-tuple-element.61.rows_ref, s32[8]{0:T(128)S(1)} %get-tuple-element.32.limit_ref, ...), custom_call_target="tpu_custom_call" | custom-call | flops 2147483648 | bytes 25165824 | tf_op jit(solution)/shard_map/pallas_call | solution.py:356
  102.3 3.1 %collective-permute-start.11 = (f32[256,128]{1,0:T(8,128)S(1)}, f32[256,128]{1,0:T(8,128)S(1)}, u32[]{:S(2)}, u32[]{:S(2)}) collective-permute-start(f32[256,128]{1,0:T(8,128)S(1)} %get-tuple-element.38), channel_id=1, source_target_pairs={{0,3},{1,2},{2,1},{3,0},{4,7},{5,6},{6,5},{7,4},{8,11},{9,10},{10,... | collective-permute-start | bytes 393224 | tf_op jit(solution)/shard_map/ppermute | solution.py:415
  112.3 3.6 %collective-permute-start.15 = (f32[512,128]{1,0:T(8,128)S(1)}, f32[512,128]{1,0:T(8,128)S(1)}, u32[]{:S(2)}, u32[]{:S(2)}) collective-permute-start(f32[512,128]{1,0:T(8,128)S(1)} %pad_maximum_fusion.11), channel_id=1, source_target_pairs={{0,12},{1,13},{2,14},{3,15},{4,8},{5,9},{6,10},{7,11},{8,4},{9,5},... | collective-permute-start | bytes 786440 | tf_op jit(solution)/shard_map/ppermute | solution.py:415
  127.9 11.9 %collective-permute-done.19 = f32[1024,128]{1,0:T(8,128)S(1)} collective-permute-done((f32[1024,128]{1,0:T(8,128)S(1)}, f32[1024,128]{1,0:T(8,128)S(1)}, u32[]{:S(2)}, u32[]{:S(2)}) %collective-permute-start.19) | collective-permute-done | bytes 524320 | tf_op jit(solution)/shard_map/ppermute | solution.py:415
  140.2 3.4 %collective-permute-start.20 = (f32[2112,128]{1,0:T(8,128)S(1)}, f32[2112,128]{1,0:T(8,128)S(1)}, u32[]{:S(2)}, u32[]{:S(2)}) collective-permute-start(f32[2112,128]{1,0:T(8,128)S(1)} %constant_dynamic-update-slice_fusion.refs_0_.refs_4_), channel_id=1, source_target_pairs={{0,12},{1,13},{2,14},{3,15},{4,8},{5,9},{6,10},{7,11},{8,4},{9,5},... | collective-permute-start | bytes 3244040 | tf_op jit(solution)/shard_map/ppermute | solution.py:415
  143.9 9.1 %shard_map.111 = f32[16,8,128,128]{3,2,1,0:T(8,128)} custom-call(f32[8,8,128,128]{3,2,1,0:T(8,128)} %shard_map.105.refs_0_, f32[4,8,128,128]{3,2,1,0:T(8,128)} %copy-done, f32[2,8,128,128]{3,2,1,0:T(8,128)} %copy-done.2, f32[2,8,128,128]{3,2,1,0:T(8,128)} %copy-done.3, f32[2112,128]{1,0:T(8,128)S(1)} %constant_dynamic-update-slice_fusion.refs_0_.refs_4_), custom_call_target="tpu_custom_call" | custom-call | bytes 16777216 | tf_op jit(solution)/shard_map/pallas_call | solution.py:111
  154.6 3.4 %collective-permute-done.22.refs_3_ = f32[2048,128]{1,0:T(8,128)S(1)} collective-permute-done((f32[2048,128]{1,0:T(8,128)S(1)}, f32[2048,128]{1,0:T(8,128)S(1)}, u32[]{:S(2)}, u32[]{:S(2)}) %collective-permute-start.22) | collective-permute-done | bytes 1048608 | tf_op jit(solution)/shard_map/ppermute | solution.py:415
  158.7 10.0 %shard_map.112 = (f32[8,128]{1,0:T(8,128)S(1)}, f32[8,128,128]{2,1,0:T(8,128)S(1)}, f32[264,128]{1,0:T(8,128)S(1)}, f32[256,128]{1,0:T(8,128)S(1)}, f32[256,128]{1,0:T(8,128)S(1)}, /*index=5*/f32[256,128]{1,0:T(8,128)S(1)}) custom-call(s32[8,16]{1,0:T(8,128)S(1)} %get-tuple-element.62.rows_ref, s32[8]{0:T(128)S(1)} %get-tuple-element.32.limit_ref, ...), custom_call_target="tpu_custom_call" | custom-call | flops 2147483648 | bytes 25165824 | tf_op jit(solution)/shard_map/pallas_call | solution.py:356
  191.1 12.4 %collective-permute-done.35 = f32[1024,128]{1,0:T(8,128)S(1)} collective-permute-done((f32[1024,128]{1,0:T(8,128)S(1)}, f32[1024,128]{1,0:T(8,128)S(1)}, u32[]{:S(2)}, u32[]{:S(2)}) %collective-permute-start.35) | collective-permute-done | bytes 524320 | tf_op jit(solution)/shard_map/ppermute | solution.py:415
  209.0 9.4 %collective-permute-done.39.refs_4_ = f32[2048,128]{1,0:T(8,128)S(1)} collective-permute-done((f32[2048,128]{1,0:T(8,128)S(1)}, f32[2048,128]{1,0:T(8,128)S(1)}, u32[]{:S(2)}, u32[]{:S(2)}) %collective-permute-start.39) | collective-permute-done | bytes 1048608 | tf_op jit(solution)/shard_map/ppermute | solution.py:415
  222.0 9.4 %shard_map.114 = (f32[8,128]{1,0:T(8,128)S(1)}, f32[8,128,128]{2,1,0:T(8,128)S(1)}, f32[8,128,128]{2,1,0:T(8,128)S(1)}, f32[8,128]{1,0:T(8,128)S(1)}) custom-call(s32[8,16]{1,0:T(8,128)S(1)} %get-tuple-element.62.rows_ref, s32[8]{0:T(128)S(1)} %get-tuple-element.32.limit_ref, s32[1]{0:T(128)} %bitcast.6.which_ref, f32[8256,128]{1,0:T(8,128)S(1)} %shard_map.113.refs_0_, ...), custom_call_target="tpu_custom_call" | custom-call | flops 2147483648 | bytes 25165824 | tf_op jit(solution)/shard_map/pallas_call | solution.py:356
  (163 shorter events, 86.1 us)
Async XLA Ops:
  7.2 77.3 %all-gather.2.cloned.1.call-start = ((), (), s32[]{:S(2)}) async-start(), calls=%async_computation | async-start | bytes 8982528 | tf_op jit(solution)/shard_map/all_gather | solution.py:528
  16.1 76.8 %collective-permute-start = (f32[8,8,128,128]{3,2,1,0:T(8,128)}, f32[8,8,128,128]{3,2,1,0:T(8,128)}, u32[]{:S(2)}, u32[]{:S(2)}) collective-permute-start(f32[8,8,128,128]{3,2,1,0:T(8,128)} %shard_map.105.refs_0_), channel_id=1, source_target_pairs={{0,16},{16,32},{32,48},{48,64},{64,80},{80,96},{96,112},{1,17},{17... | collective-permute-start | bytes 12582920 | tf_op jit(solution)/shard_map/ppermute | solution.py:483
  21.6 16.2 %collective-permute-start.2 = (f32[2,8,128,128]{3,2,1,0:T(8,128)S(1)}, f32[2,8,128,128]{3,2,1,0:T(8,128)}, u32[]{:S(2)}, u32[]{:S(2)}) collective-permute-start(f32[2,8,128,128]{3,2,1,0:T(8,128)S(1)} %shard_map.107.refs_2_), channel_id=1, source_target_pairs={{0,16},{32,48},{64,80},{96,112},{16,96},{48,0},{80,32},{1,17},{33,... | collective-permute-start | bytes 3145736 | tf_op jit(solution)/shard_map/ppermute | solution.py:491
  26.1 28.4 %collective-permute-start.3 = (f32[2,8,128,128]{3,2,1,0:T(8,128)S(1)}, f32[2,8,128,128]{3,2,1,0:T(8,128)}, u32[]{:S(2)}, u32[]{:S(2)}) collective-permute-start(f32[2,8,128,128]{3,2,1,0:T(8,128)S(1)} %shard_map.108.refs_3_), channel_id=1, source_target_pairs={{0,16},{32,48},{64,80},{96,112},{16,96},{48,0},{80,32},{1,17},{33,... | collective-permute-start | bytes 3145736 | tf_op jit(solution)/shard_map/ppermute | solution.py:491
  37.8 26.7 %collective-permute-start.4 = (f32[2,8,128,128]{3,2,1,0:T(8,128)}, f32[2,8,128,128]{3,2,1,0:T(8,128)}, u32[]{:S(2)}, u32[]{:S(2)}) collective-permute-start(f32[2,8,128,128]{3,2,1,0:T(8,128)} %collective-permute-done.2.refs_4_.refs_8_), channel_id=1, source_target_pairs={{96,64},{0,96},{32,0},{97,65},{1,97},{33,1},{98,66},{2,98},{34,2},... | collective-permute-start | bytes 3145736 | tf_op jit(solution)/shard_map/ppermute | solution.py:494
  54.5 17.1 %collective-permute-start.6 = (f32[2,8,128,128]{3,2,1,0:T(8,128)}, f32[2,8,128,128]{3,2,1,0:T(8,128)}, u32[]{:S(2)}, u32[]{:S(2)}) collective-permute-start(f32[2,8,128,128]{3,2,1,0:T(8,128)} %collective-permute-done.3.refs_5_.refs_9_), channel_id=1, source_target_pairs={{96,64},{0,96},{32,0},{97,65},{1,97},{33,1},{98,66},{2,98},{34,2},... | collective-permute-start | bytes 3145736 | tf_op jit(solution)/shard_map/ppermute | solution.py:494
  61.1 26.8 %collective-permute-start.1 = (f32[4,8,128,128]{3,2,1,0:T(8,128)S(1)}, f32[4,8,128,128]{3,2,1,0:T(8,128)}, u32[]{:S(2)}, u32[]{:S(2)}) collective-permute-start(f32[4,8,128,128]{3,2,1,0:T(8,128)S(1)} %shard_map.106.refs_1_), channel_id=1, source_target_pairs={{0,16},{16,32},{32,48},{48,64},{64,80},{80,96},{96,112},{1,17},{17... | collective-permute-start | bytes 6291464 | tf_op jit(solution)/shard_map/ppermute | solution.py:483
  64.5 23.4 %collective-permute-start.5 = (f32[2,8,128,128]{3,2,1,0:T(8,128)}, f32[2,8,128,128]{3,2,1,0:T(8,128)}, u32[]{:S(2)}, u32[]{:S(2)}) collective-permute-start(f32[2,8,128,128]{3,2,1,0:T(8,128)} %collective-permute-done.4), channel_id=1, source_target_pairs={{64,32},{96,64},{0,96},{65,33},{97,65},{1,97},{66,34},{98,66},{2,9... | collective-permute-start | bytes 3145736 | tf_op jit(solution)/shard_map/ppermute | solution.py:494
  71.5 21.4 %collective-permute-start.7 = (f32[2,8,128,128]{3,2,1,0:T(8,128)}, f32[2,8,128,128]{3,2,1,0:T(8,128)}, u32[]{:S(2)}, u32[]{:S(2)}) collective-permute-start(f32[2,8,128,128]{3,2,1,0:T(8,128)} %collective-permute-done.6), channel_id=1, source_target_pairs={{64,32},{96,64},{0,96},{65,33},{97,65},{1,97},{66,34},{98,66},{2,9... | collective-permute-start | bytes 3145736 | tf_op jit(solution)/shard_map/ppermute | solution.py:494
  118.5 25.1 %collective-permute-start.13 = (f32[1024,128]{1,0:T(8,128)S(1)}, f32[1024,128]{1,0:T(8,128)S(1)}, u32[]{:S(2)}, u32[]{:S(2)}) collective-permute-start(f32[1024,128]{1,0:T(8,128)S(1)} %pad_maximum_fusion.2), channel_id=1, source_target_pairs={{0,12},{1,13},{2,14},{3,15},{4,8},{5,9},{6,10},{7,11},{8,4},{9,5},... | collective-permute-start | bytes 1572872 | tf_op jit(solution)/shard_map/ppermute | solution.py:415
  122.8 17.1 %collective-permute-start.16 = (f32[1024,128]{1,0:T(8,128)S(1)}, f32[1024,128]{1,0:T(8,128)S(1)}, u32[]{:S(2)}, u32[]{:S(2)}) collective-permute-start(f32[1024,128]{1,0:T(8,128)S(1)} %pad_maximum_fusion.3), channel_id=1, source_target_pairs={{0,1},{1,0},{2,3},{3,2},{4,5},{5,4},{6,7},{7,6},{8,9},{9,8},{10,11... | collective-permute-start | bytes 1572872 | tf_op jit(solution)/shard_map/ppermute | solution.py:415
  125.1 14.6 %collective-permute-start.19 = (f32[1024,128]{1,0:T(8,128)S(1)}, f32[1024,128]{1,0:T(8,128)S(1)}, u32[]{:S(2)}, u32[]{:S(2)}) collective-permute-start(f32[1024,128]{1,0:T(8,128)S(1)} %pad_maximum_fusion.4), channel_id=1, source_target_pairs={{0,3},{1,2},{2,1},{3,0},{4,7},{5,6},{6,5},{7,4},{8,11},{9,10},{10,... | collective-permute-start | bytes 1572872 | tf_op jit(solution)/shard_map/ppermute | solution.py:415
  139.8 14.9 %collective-permute-start.23 = (f32[2048,128]{1,0:T(8,128)S(1)}, f32[2048,128]{1,0:T(8,128)S(1)}, u32[]{:S(2)}, u32[]{:S(2)}) collective-permute-start(f32[2048,128]{1,0:T(8,128)S(1)} %constant_dynamic-update-slice_fusion.12.refs_3_), channel_id=1, source_target_pairs={{0,1},{1,0},{2,3},{3,2},{4,5},{5,4},{6,7},{7,6},{8,9},{9,8},{10,11... | collective-permute-start | bytes 3145736 | tf_op jit(solution)/shard_map/ppermute | solution.py:415
  139.9 18.2 %collective-permute-start.22 = (f32[2048,128]{1,0:T(8,128)S(1)}, f32[2048,128]{1,0:T(8,128)S(1)}, u32[]{:S(2)}, u32[]{:S(2)}) collective-permute-start(f32[2048,128]{1,0:T(8,128)S(1)} %constant_dynamic-update-slice_fusion.8.refs_2_), channel_id=1, source_target_pairs={{0,3},{1,2},{2,1},{3,0},{4,7},{5,6},{6,5},{7,4},{8,11},{9,10},{10,... | collective-permute-start | bytes 3145736 | tf_op jit(solution)/shard_map/ppermute | solution.py:415
  140.2 18.5 %collective-permute-start.20 = (f32[2112,128]{1,0:T(8,128)S(1)}, f32[2112,128]{1,0:T(8,128)S(1)}, u32[]{:S(2)}, u32[]{:S(2)}) collective-permute-start(f32[2112,128]{1,0:T(8,128)S(1)} %constant_dynamic-update-slice_fusion.refs_0_.refs_4_), channel_id=1, source_target_pairs={{0,12},{1,13},{2,14},{3,15},{4,8},{5,9},{6,10},{7,11},{8,4},{9,5},... | collective-permute-start | bytes 3244040 | tf_op jit(solution)/shard_map/ppermute | solution.py:415
  143.6 15.1 %collective-permute-start.21 = (f32[2048,128]{1,0:T(8,128)S(1)}, f32[2048,128]{1,0:T(8,128)S(1)}, u32[]{:S(2)}, u32[]{:S(2)}) collective-permute-start(f32[2048,128]{1,0:T(8,128)S(1)} %constant_dynamic-update-slice_fusion.4.refs_1_), channel_id=1, source_target_pairs={{0,4},{1,5},{2,6},{3,7},{4,0},{5,1},{6,2},{7,3},{8,12},{9,13},{10,... | collective-permute-start | bytes 3145736 | tf_op jit(solution)/shard_map/ppermute | solution.py:415
  184.8 22.3 %collective-permute-start.29 = (f32[1024,128]{1,0:T(8,128)S(1)}, f32[1024,128]{1,0:T(8,128)S(1)}, u32[]{:S(2)}, u32[]{:S(2)}) collective-permute-start(f32[1024,128]{1,0:T(8,128)S(1)} %pad_maximum_fusion.5), channel_id=1, source_target_pairs={{0,12},{1,13},{2,14},{3,15},{4,8},{5,9},{6,10},{7,11},{8,4},{9,5},... | collective-permute-start | bytes 1572872 | tf_op jit(solution)/shard_map/ppermute | solution.py:415
  186.2 17.4 %collective-permute-start.32 = (f32[1024,128]{1,0:T(8,128)S(1)}, f32[1024,128]{1,0:T(8,128)S(1)}, u32[]{:S(2)}, u32[]{:S(2)}) collective-permute-start(f32[1024,128]{1,0:T(8,128)S(1)} %pad_maximum_fusion.6), channel_id=1, source_target_pairs={{0,1},{1,0},{2,3},{3,2},{4,5},{5,4},{6,7},{7,6},{8,9},{9,8},{10,11... | collective-permute-start | bytes 1572872 | tf_op jit(solution)/shard_map/ppermute | solution.py:415
  187.3 16.1 %collective-permute-start.35 = (f32[1024,128]{1,0:T(8,128)S(1)}, f32[1024,128]{1,0:T(8,128)S(1)}, u32[]{:S(2)}, u32[]{:S(2)}) collective-permute-start(f32[1024,128]{1,0:T(8,128)S(1)} %pad_maximum_fusion.7), channel_id=1, source_target_pairs={{0,3},{1,2},{2,1},{3,0},{4,7},{5,6},{6,5},{7,4},{8,11},{9,10},{10,... | collective-permute-start | bytes 1572872 | tf_op jit(solution)/shard_map/ppermute | solution.py:415
  189.3 16.3 %collective-permute-start.26 = (f32[1056,128]{1,0:T(8,128)S(1)}, f32[1056,128]{1,0:T(8,128)S(1)}, u32[]{:S(2)}, u32[]{:S(2)}) collective-permute-start(f32[1056,128]{1,0:T(8,128)S(1)} %pad_maximum_fusion.1), channel_id=1, source_target_pairs={{0,4},{1,5},{2,6},{3,7},{4,0},{5,1},{6,2},{7,3},{8,12},{9,13},{10,... | collective-permute-start | bytes 1622024 | tf_op jit(solution)/shard_map/ppermute | solution.py:415
  203.5 14.9 %collective-permute-start.39 = (f32[2048,128]{1,0:T(8,128)S(1)}, f32[2048,128]{1,0:T(8,128)S(1)}, u32[]{:S(2)}, u32[]{:S(2)}) collective-permute-start(f32[2048,128]{1,0:T(8,128)S(1)} %constant_dynamic-update-slice_fusion.28.refs_3_), channel_id=1, source_target_pairs={{0,1},{1,0},{2,3},{3,2},{4,5},{5,4},{6,7},{7,6},{8,9},{9,8},{10,11... | collective-permute-start | bytes 3145736 | tf_op jit(solution)/shard_map/ppermute | solution.py:415
  203.7 16.1 %collective-permute-start.38 = (f32[2048,128]{1,0:T(8,128)S(1)}, f32[2048,128]{1,0:T(8,128)S(1)}, u32[]{:S(2)}, u32[]{:S(2)}) collective-permute-start(f32[2048,128]{1,0:T(8,128)S(1)} %constant_dynamic-update-slice_fusion.24.refs_2_), channel_id=1, source_target_pairs={{0,3},{1,2},{2,1},{3,0},{4,7},{5,6},{6,5},{7,4},{8,11},{9,10},{10,... | collective-permute-start | bytes 3145736 | tf_op jit(solution)/shard_map/ppermute | solution.py:415
  205.6 16.4 %collective-permute-start.36 = (f32[2112,128]{1,0:T(8,128)S(1)}, f32[2112,128]{1,0:T(8,128)S(1)}, u32[]{:S(2)}, u32[]{:S(2)}) collective-permute-start(f32[2112,128]{1,0:T(8,128)S(1)} %constant_dynamic-update-slice_fusion.16.refs_0_), channel_id=1, source_target_pairs={{0,12},{1,13},{2,14},{3,15},{4,8},{5,9},{6,10},{7,11},{8,4},{9,5},... | collective-permute-start | bytes 3244040 | tf_op jit(solution)/shard_map/ppermute | solution.py:415
  207.1 14.9 %collective-permute-start.37 = (f32[2048,128]{1,0:T(8,128)S(1)}, f32[2048,128]{1,0:T(8,128)S(1)}, u32[]{:S(2)}, u32[]{:S(2)}) collective-permute-start(f32[2048,128]{1,0:T(8,128)S(1)} %constant_dynamic-update-slice_fusion.20.refs_1_), channel_id=1, source_target_pairs={{0,4},{1,5},{2,6},{3,7},{4,0},{5,1},{6,2},{7,3},{8,12},{9,13},{10,... | collective-permute-start | bytes 3145736 | tf_op jit(solution)/shard_map/ppermute | solution.py:415
  (29 other events, 312.1 us)
Sparse Core Ops, SparseCore 0:
  10.8 73.6 all-gather.1

commit v6 on v5

--- a/solution.py
+++ b/solution.py
@@ -12,7 +12,8 @@
 PARTS = 4
 SIDE = 4
 PAIR = 2
-AHEAD = 3
+AHEAD = 4
+TOGETHER = 2
 ORDERS = ((("y", 1), ("y", 3), ("z", 1), ("z", 3)), (("y", 3), ("y", 1), ("z", 3), ("z", 1)),
           (("z", 1), ("z", 3), ("y", 1), ("y", 3)), (("z", 3), ("z", 1), ("y", 3), ("y", 1)))
 
@@ -129,7 +130,7 @@
 
 def put_quarter(slot, value, quarters):
     blk = value.shape[0]
-    per = pl.num_programs(0) // PARTS
+    per = pl.num_programs(0) * TOGETHER // PARTS
     at = pl.ds(pl.multiple_of((slot % per) * blk, blk), blk)
     for part, quarter in enumerate(quarters):
         @pl.when(slot // per == part)
@@ -251,8 +252,8 @@
     right, known_ref = refs.pop(0), refs.pop(0)
     states, outs = refs[:mode], refs[mode:-6]
     blocks, left_copy, right_copy, inner, sems, piece_sems = refs[-6:]
-    terms, _, blk, _ = left_copy.shape
-    slot = pl.program_id(0)
+    terms, slots, blk, _ = left_copy.shape
+    step = pl.program_id(0)
     coef_ref = outs[0]
     outs = outs[1:]
 
@@ -263,7 +264,7 @@
         late = blocks[pl.ds(pl.multiple_of(jnp.maximum(row - split_row, 0), 8), number), :]
         return jnp.where(row < split_row, early, late)
 
-    @pl.when(slot == 0)
+    @pl.when(step == 0)
     def _():
         copies = []
         at = 0
@@ -286,60 +287,73 @@
             sums = part if sums is None else sums + part
         coef_ref[...] = next_coefs(mode, known_ref[...], sums)
 
-    @pl.when(slot + AHEAD < pl.num_programs(0))
+    def product(slot, inner):
+        for term in range(terms):
+            row = pl.multiple_of(rows_ref[slot, term], 8)
+            first = jnp.concatenate(split(rows_of(row, blk)), axis=1)
+            value = folded(dot(first, right_factor(*split(right_copy[term, slot]))))
+            inner[term * blk : (term + 1) * blk, :] = jnp.concatenate(split(value), axis=1)
+        result = None
+        for term in range(0, terms, 2):
+            (high0, low0), (high1, low1) = (
+                split(left_copy[index, slot]) for index in (term, term + 1)
+            )
+            below = inner[term * blk : (term + 2) * blk, :]
+            part = folded(dot(jnp.concatenate([high0, high1], axis=1), below))
+            part = part + dot(jnp.concatenate([low0, low1], axis=1), below[:, :blk])
+            result = part if result is None else result + part
+        return masked(result, limit_ref[slot])
+
+    first_slot = step * TOGETHER
+
+    @pl.when(first_slot + AHEAD < slots)
     def _():
-        start_fetch(slot + AHEAD, which_ref[0], lefts, right, left_copy, right_copy, sems)
-
-    wait_fetch(slot, lefts, right, left_copy, right_copy, sems)
-    for term in range(terms):
-        row = pl.multiple_of(rows_ref[slot, term], 8)
-        first = jnp.concatenate(split(rows_of(row, blk)), axis=1)
-        value = folded(dot(first, right_factor(*split(right_copy[term, slot]))))
-        inner[term * blk : (term + 1) * blk, :] = jnp.concatenate(split(value), axis=1)
-    result = None
-    for term in range(0, terms, 2):
-        (high0, low0), (high1, low1) = (
-            split(left_copy[index, slot]) for index in (term, term + 1)
-        )
-        below = inner[term * blk : (term + 2) * blk, :]
-        part = folded(dot(jnp.concatenate([high0, high1], axis=1), below))
-        part = part + dot(jnp.concatenate([low0, low1], axis=1), below[:, :blk])
-        result = part if result is None else result + part
-    value = masked(result, limit_ref[slot])
-
+        for more in range(TOGETHER):
+            start_fetch(
+                first_slot + AHEAD + more, which_ref[0], lefts, right, left_copy, right_copy, sems
+            )
+
+    for more in range(TOGETHER):
+        wait_fetch(first_slot + more, lefts, right, left_copy, right_copy, sems)
+    values = []
+    for more in range(TOGETHER):
+        values.append(product(first_slot + more, inner.at[more]))
     scale, a0, keep, turn, a1 = (coef_ref[k : k + 1, :] for k in range(5))
-    x0 = states[0][0] * scale
-    if mode == 1:
-        y0 = value * scale
-        products = [x0 * y0]
-        send = y0
-    else:
-        y0 = states[1][0]
-        r1 = y0 - a0 * x0
-        if mode == 2:
-            z1 = value - a0 * y0
-            products = [x0 * z1, r1 * y0, r1 * z1, r1 * r1]
-            send = z1
+    for more, value in enumerate(values):
+        slot = first_slot + more
+
+        x0 = states[0][more] * scale
+        if mode == 1:
+            y0 = value * scale
+            products = [x0 * y0]
+            send = y0
         else:
-            z1 = states[2][0]
-            x1 = keep * x0 + turn * r1
-            y1 = keep * y0 + turn * z1
-            r2 = y1 - a1 * x1
-            z2 = keep * (z1 + a0 * y0) + turn * value - a1 * y1
-            outs[0][0] = x1
-            outs[1][0] = r2
-            put_sums(slot, [r2 * r2, r2 * z2], outs[2])
-            return
-    outs[0][0] = send
-    put_quarter(slot, send, outs[1:])
-    put_sums(slot, products, outs[1].at[pl.ds(outs[1].shape[0] - TAIL, TAIL), :])
+            y0 = states[1][more]
+            r1 = y0 - a0 * x0
+            if mode == 2:
+                z1 = value - a0 * y0
+                products = [x0 * z1, r1 * y0, r1 * z1, r1 * r1]
+                send = z1
+            else:
+                z1 = states[2][more]
+                x1 = keep * x0 + turn * r1
+                y1 = keep * y0 + turn * z1
+                r2 = y1 - a1 * x1
+                z2 = keep * (z1 + a0 * y0) + turn * value - a1 * y1
+                outs[0][more] = x1
+                outs[1][more] = r2
+                put_sums(slot, [r2 * r2, r2 * z2], outs[2])
+                continue
+        outs[0][more] = send
+        put_quarter(slot, send, outs[1:])
+        put_sums(slot, products, outs[1].at[pl.ds(outs[1].shape[0] - TAIL, TAIL), :])
 
 
 def apply(rows, limit, which, tails, whole, pieces, lefts, right, known, states):
     mode = len(states)
     terms, slots, blk, _ = right.shape
     vector = jax.ShapeDtypeStruct((slots, blk, blk), jnp.float32)
-    vector_spec = pl.BlockSpec((1, blk, blk), lambda s, *_: (s, 0, 0))
+    vector_spec = pl.BlockSpec((TOGETHER, blk, blk), lambda s, *_: (s, 0, 0))
     few = jax.ShapeDtypeStruct((TAIL, blk), jnp.float32)
     few_spec = whole_spec((TAIL, blk))
     if mode < 3:
@@ -358,7 +372,7 @@
         out_shape=out_shape,
         grid_spec=pltpu.PrefetchScalarGridSpec(
             num_scalar_prefetch=3,
-            grid=(slots,),
+            grid=(slots // TOGETHER,),
             in_specs=[pl.BlockSpec(memory_space=pltpu.VMEM)]
             + [pl.BlockSpec(memory_space=pl.ANY)] * sum(counts)
             + [few_spec]
@@ -368,12 +382,12 @@
                 pltpu.VMEM((total, blk), jnp.float32),
                 pltpu.VMEM(right.shape, jnp.float32),
                 pltpu.VMEM(right.shape, jnp.float32),
-                pltpu.VMEM((terms * blk, 2 * blk), jnp.bfloat16),
+                pltpu.VMEM((TOGETHER, terms * blk, 2 * blk), jnp.bfloat16),
                 pltpu.SemaphoreType.DMA((1 + len(near), slots)),
                 pltpu.SemaphoreType.DMA((max(len(pieces), 1),)),
             ],
         ),
-        compiler_params=pltpu.CompilerParams(vmem_limit_bytes=26 * MIB),
+        compiler_params=pltpu.CompilerParams(vmem_limit_bytes=28 * MIB),
         cost_estimate=pl.CostEstimate(
             flops=8 * terms * slots * blk**3, bytes_accessed=12 * right.size, transcendentals=0
         ),

time: 255 us -> 255 us (level)
  transfers between devices with their start and end apart: 47 -> 47, of which waited for: 25 -> 26; matrix products, arithmetic and copies ran while one was open for 2% -> 2% of each run, Pallas kernels for 11% -> 11%
where the time goes in v6:
time: 255 us; the launch traced here: 254 us
  waiting for transfers between devices  96.4 us (38%)
  starting transfers between devices  78.3 us (31%)
  Pallas kernels  59.6 us (23%)
  between operations  14.7 us (6%)
  local copies, waits for them, and re-layouts  4.81 us (2%)
    ppermute x38, waiting for transfers between devices, swap(): lax.ppermute(value, 'sector', [(index, partner(index, move)) for index in...  61.6 us
    ppermute x38, starting transfers between devices, swap(): lax.ppermute(value, 'sector', [(index, partner(index, move)) for index in...  51.2 us
    pallas_call x3, Pallas kernels, apply(): pl.pallas_call(functools.partial(apply_kernel, mode, counts, tails), out_...  29 us
    ppermute x2, waiting for transfers between devices, to_next_round(): near = value = lax.ppermute(value, 'chain', pairs)  20.7 us
    ppermute x4, starting transfers between devices, to_next_round(): value = lax.ppermute(value, 'chain', pairs)  15.7 us
    pallas_call x4, Pallas kernels, update(): pl.pallas_call(update_kernel, out_shape=jax.ShapeDtypeStruct((some, slots...  14.5 us
    ppermute x4, waiting for transfers between devices, to_next_round(): value = lax.ppermute(value, 'chain', pairs)  9.7 us
    pallas_call x1, Pallas kernels, join(): pl.pallas_call(functools.partial(join_kernel, starts), out_shape=jax.Shap...  9.06 us
  transfers between devices with their start and end apart: 47, of which 26 were waited for; matrix products, arithmetic and copies ran while one was open for 2% of the time, Pallas kernels for 11%

profile of v6, /device:TPU:0, one launch (start us, length us, event | category | flops | bytes accessed | tf_op | source)
XLA Modules:
  0.0 254.3 jit_solution(3713622183455983959)
XLA Ops:
  9.3 6.8 %shard_map.105.refs_0_ = f32[8,8,128,128]{3,2,1,0:T(8,128)} custom-call(f32[16,8,128,128]{3,2,1,0:T(8,128)} %bitcast.30, f32[8,128,128]{2,1,0:T(8,128)S(1)} %bitcast.26), custom_call_target="tpu_custom_call" | custom-call | flops 1073741824 | bytes 8388608 | tf_op jit(solution)/shard_map/pallas_call | solution.py:70
  16.1 3.4 %collective-permute-start = (f32[8,8,128,128]{3,2,1,0:T(8,128)}, f32[8,8,128,128]{3,2,1,0:T(8,128)}, u32[]{:S(2)}, u32[]{:S(2)}) collective-permute-start(f32[8,8,128,128]{3,2,1,0:T(8,128)} %shard_map.105.refs_0_), channel_id=1, source_target_pairs={{0,16},{16,32},{32,48},{48,64},{64,80},{80,96},{96,112},{1,17},{17... | collective-permute-start | bytes 12582920 | tf_op jit(solution)/shard_map/ppermute | solution.py:497
  26.1 3.2 %collective-permute-start.3 = (f32[2,8,128,128]{3,2,1,0:T(8,128)S(1)}, f32[2,8,128,128]{3,2,1,0:T(8,128)}, u32[]{:S(2)}, u32[]{:S(2)}) collective-permute-start(f32[2,8,128,128]{3,2,1,0:T(8,128)S(1)} %shard_map.108.refs_3_), channel_id=1, source_target_pairs={{0,16},{32,48},{64,80},{96,112},{16,96},{48,0},{80,32},{1,17},{33,... | collective-permute-start | bytes 3145736 | tf_op jit(solution)/shard_map/ppermute | solution.py:505
  29.3 8.6 %collective-permute-done.2.refs_4_.refs_8_ = f32[2,8,128,128]{3,2,1,0:T(8,128)} collective-permute-done((f32[2,8,128,128]{3,2,1,0:T(8,128)S(1)}, f32[2,8,128,128]{3,2,1,0:T(8,128)}, u32[]{:S(2)}, u32[]{:S(2)}) %collective-permute-start.2) | collective-permute-done | bytes 1048608 | tf_op jit(solution)/shard_map/ppermute | solution.py:505
  37.8 4.5 %collective-permute-start.4 = (f32[2,8,128,128]{3,2,1,0:T(8,128)}, f32[2,8,128,128]{3,2,1,0:T(8,128)}, u32[]{:S(2)}, u32[]{:S(2)}) collective-permute-start(f32[2,8,128,128]{3,2,1,0:T(8,128)} %collective-permute-done.2.refs_4_.refs_8_), channel_id=1, source_target_pairs={{96,64},{0,96},{32,0},{97,65},{1,97},{33,1},{98,66},{2,98},{34,2},... | collective-permute-start | bytes 3145736 | tf_op jit(solution)/shard_map/ppermute | solution.py:508
  42.4 12.1 %collective-permute-done.3.refs_5_.refs_9_ = f32[2,8,128,128]{3,2,1,0:T(8,128)} collective-permute-done((f32[2,8,128,128]{3,2,1,0:T(8,128)S(1)}, f32[2,8,128,128]{3,2,1,0:T(8,128)}, u32[]{:S(2)}, u32[]{:S(2)}) %collective-permute-start.3) | collective-permute-done | bytes 1048608 | tf_op jit(solution)/shard_map/ppermute | solution.py:505
  54.5 3.3 %collective-permute-start.6 = (f32[2,8,128,128]{3,2,1,0:T(8,128)}, f32[2,8,128,128]{3,2,1,0:T(8,128)}, u32[]{:S(2)}, u32[]{:S(2)}) collective-permute-start(f32[2,8,128,128]{3,2,1,0:T(8,128)} %collective-permute-done.3.refs_5_.refs_9_), channel_id=1, source_target_pairs={{96,64},{0,96},{32,0},{97,65},{1,97},{33,1},{98,66},{2,98},{34,2},... | collective-permute-start | bytes 3145736 | tf_op jit(solution)/shard_map/ppermute | solution.py:508
  57.8 3.3 %shard_map.106.refs_1_ = f32[4,8,128,128]{3,2,1,0:T(8,128)S(1)} custom-call(f32[16,8,128,128]{3,2,1,0:T(8,128)} %bitcast.33, f32[8,128,128]{2,1,0:T(8,128)S(1)} %bitcast.29), custom_call_target="tpu_custom_call" | custom-call | flops 536870912 | bytes 4194304 | tf_op jit(solution)/shard_map/pallas_call | solution.py:70
  66.9 4.7 %collective-permute-done.6 = f32[2,8,128,128]{3,2,1,0:T(8,128)} collective-permute-done((f32[2,8,128,128]{3,2,1,0:T(8,128)}, f32[2,8,128,128]{3,2,1,0:T(8,128)}, u32[]{:S(2)}, u32[]{:S(2)}) %collective-permute-start.6) | collective-permute-done | bytes 1048608 | tf_op jit(solution)/shard_map/ppermute | solution.py:508
  71.5 5.5 %collective-permute-start.7 = (f32[2,8,128,128]{3,2,1,0:T(8,128)}, f32[2,8,128,128]{3,2,1,0:T(8,128)}, u32[]{:S(2)}, u32[]{:S(2)}) collective-permute-start(f32[2,8,128,128]{3,2,1,0:T(8,128)} %collective-permute-done.6), channel_id=1, source_target_pairs={{64,32},{96,64},{0,96},{65,33},{97,65},{1,97},{66,34},{98,66},{2,9... | collective-permute-start | bytes 3145736 | tf_op jit(solution)/shard_map/ppermute | solution.py:508
  80.1 4.4 %all-gather.2.cloned.1.call-done.refs_0_ = f32[16512,128]{1,0:T(8,128)} async-done(((f32[1032,128]{1,0:T(8,128)}), f32[16512,128]{1,0:T(8,128)}) %all-gather.2.cloned.1.call-update) | async-done | bytes 8454160 | tf_op jit(solution)/shard_map/all_gather | solution.py:542
  84.5 3.4 %shard_map.104.refs_0_ = f32[16512,128]{1,0:T(8,128)S(1)} custom-call(f32[16512,128]{1,0:T(8,128)} %all-gather.2.cloned.1.call-done.refs_0_), custom_call_target="tpu_custom_call" | custom-call | bytes 16908288 | tf_op jit(solution)/shard_map/pallas_call | solution.py:450
  87.9 5.0 %collective-permute-done.7.refs_9_.refs_13_ = f32[2,8,128,128]{3,2,1,0:T(8,128)} collective-permute-done((f32[2,8,128,128]{3,2,1,0:T(8,128)}, f32[2,8,128,128]{3,2,1,0:T(8,128)}, u32[]{:S(2)}, u32[]{:S(2)}) %collective-permute-start.7) | collective-permute-done | bytes 1048608 | tf_op jit(solution)/shard_map/ppermute | solution.py:508
  92.9 9.3 %shard_map.109 = (f32[8,128]{1,0:T(8,128)S(1)}, f32[8,128,128]{2,1,0:T(8,128)S(1)}, f32[264,128]{1,0:T(8,128)S(1)}, f32[256,128]{1,0:T(8,128)S(1)}, f32[256,128]{1,0:T(8,128)S(1)}, /*index=5*/f32[256,128]{1,0:T(8,128)S(1)}) custom-call(s32[8,16]{1,0:T(8,128)S(1)} %get-tuple-element.61.rows_ref, s32[8]{0:T(128)S(1)} %get-tuple-element.32.limit_ref, ...), custom_call_target="tpu_custom_call" | custom-call | flops 2147483648 | bytes 25165824 | tf_op jit(solution)/shard_map/pallas_call | solution.py:370
  102.3 3.1 %collective-permute-start.11 = (f32[256,128]{1,0:T(8,128)S(1)}, f32[256,128]{1,0:T(8,128)S(1)}, u32[]{:S(2)}, u32[]{:S(2)}) collective-permute-start(f32[256,128]{1,0:T(8,128)S(1)} %get-tuple-element.38), channel_id=1, source_target_pairs={{0,3},{1,2},{2,1},{3,0},{4,7},{5,6},{6,5},{7,4},{8,11},{9,10},{10,... | collective-permute-start | bytes 393224 | tf_op jit(solution)/shard_map/ppermute | solution.py:429
  112.2 3.6 %collective-permute-start.15 = (f32[512,128]{1,0:T(8,128)S(1)}, f32[512,128]{1,0:T(8,128)S(1)}, u32[]{:S(2)}, u32[]{:S(2)}) collective-permute-start(f32[512,128]{1,0:T(8,128)S(1)} %pad_maximum_fusion.11), channel_id=1, source_target_pairs={{0,12},{1,13},{2,14},{3,15},{4,8},{5,9},{6,10},{7,11},{8,4},{9,5},... | collective-permute-start | bytes 786440 | tf_op jit(solution)/shard_map/ppermute | solution.py:429
  127.8 11.7 %collective-permute-done.19 = f32[1024,128]{1,0:T(8,128)S(1)} collective-permute-done((f32[1024,128]{1,0:T(8,128)S(1)}, f32[1024,128]{1,0:T(8,128)S(1)}, u32[]{:S(2)}, u32[]{:S(2)}) %collective-permute-start.19) | collective-permute-done | bytes 524320 | tf_op jit(solution)/shard_map/ppermute | solution.py:429
  140.2 3.4 %collective-permute-start.20 = (f32[2112,128]{1,0:T(8,128)S(1)}, f32[2112,128]{1,0:T(8,128)S(1)}, u32[]{:S(2)}, u32[]{:S(2)}) collective-permute-start(f32[2112,128]{1,0:T(8,128)S(1)} %constant_dynamic-update-slice_fusion.refs_0_.refs_4_), channel_id=1, source_target_pairs={{0,12},{1,13},{2,14},{3,15},{4,8},{5,9},{6,10},{7,11},{8,4},{9,5},... | collective-permute-start | bytes 3244040 | tf_op jit(solution)/shard_map/ppermute | solution.py:429
  143.7 9.1 %shard_map.111 = f32[16,8,128,128]{3,2,1,0:T(8,128)} custom-call(f32[8,8,128,128]{3,2,1,0:T(8,128)} %shard_map.105.refs_0_, f32[4,8,128,128]{3,2,1,0:T(8,128)} %copy-done, f32[2,8,128,128]{3,2,1,0:T(8,128)} %copy-done.2, f32[2,8,128,128]{3,2,1,0:T(8,128)} %copy-done.3, f32[2112,128]{1,0:T(8,128)S(1)} %constant_dynamic-update-slice_fusion.refs_0_.refs_4_), custom_call_target="tpu_custom_call" | custom-call | bytes 16777216 | tf_op jit(solution)/shard_map/pallas_call | solution.py:112
  154.5 3.6 %collective-permute-done.22.refs_3_ = f32[2048,128]{1,0:T(8,128)S(1)} collective-permute-done((f32[2048,128]{1,0:T(8,128)S(1)}, f32[2048,128]{1,0:T(8,128)S(1)}, u32[]{:S(2)}, u32[]{:S(2)}) %collective-permute-start.22) | collective-permute-done | bytes 1048608 | tf_op jit(solution)/shard_map/ppermute | solution.py:429
  158.5 10.1 %shard_map.112 = (f32[8,128]{1,0:T(8,128)S(1)}, f32[8,128,128]{2,1,0:T(8,128)S(1)}, f32[264,128]{1,0:T(8,128)S(1)}, f32[256,128]{1,0:T(8,128)S(1)}, f32[256,128]{1,0:T(8,128)S(1)}, /*index=5*/f32[256,128]{1,0:T(8,128)S(1)}) custom-call(s32[8,16]{1,0:T(8,128)S(1)} %get-tuple-element.62.rows_ref, s32[8]{0:T(128)S(1)} %get-tuple-element.32.limit_ref, ...), custom_call_target="tpu_custom_call" | custom-call | flops 2147483648 | bytes 25165824 | tf_op jit(solution)/shard_map/pallas_call | solution.py:370
  191.2 12.5 %collective-permute-done.35 = f32[1024,128]{1,0:T(8,128)S(1)} collective-permute-done((f32[1024,128]{1,0:T(8,128)S(1)}, f32[1024,128]{1,0:T(8,128)S(1)}, u32[]{:S(2)}, u32[]{:S(2)}) %collective-permute-start.35) | collective-permute-done | bytes 524320 | tf_op jit(solution)/shard_map/ppermute | solution.py:429
  208.9 9.7 %collective-permute-done.39.refs_4_ = f32[2048,128]{1,0:T(8,128)S(1)} collective-permute-done((f32[2048,128]{1,0:T(8,128)S(1)}, f32[2048,128]{1,0:T(8,128)S(1)}, u32[]{:S(2)}, u32[]{:S(2)}) %collective-permute-start.39) | collective-permute-done | bytes 1048608 | tf_op jit(solution)/shard_map/ppermute | solution.py:429
  222.4 9.5 %shard_map.114 = (f32[8,128]{1,0:T(8,128)S(1)}, f32[8,128,128]{2,1,0:T(8,128)S(1)}, f32[8,128,128]{2,1,0:T(8,128)S(1)}, f32[8,128]{1,0:T(8,128)S(1)}) custom-call(s32[8,16]{1,0:T(8,128)S(1)} %get-tuple-element.62.rows_ref, s32[8]{0:T(128)S(1)} %get-tuple-element.32.limit_ref, s32[1]{0:T(128)} %bitcast.6.which_ref, f32[8256,128]{1,0:T(8,128)S(1)} %shard_map.113.refs_0_, ...), custom_call_target="tpu_custom_call" | custom-call | flops 2147483648 | bytes 25165824 | tf_op jit(solution)/shard_map/pallas_call | solution.py:370
  (163 shorter events, 85.8 us)
Async XLA Ops:
  7.2 77.3 %all-gather.2.cloned.1.call-start = ((), (), s32[]{:S(2)}) async-start(), calls=%async_computation | async-start | bytes 8982528 | tf_op jit(solution)/shard_map/all_gather | solution.py:542
  16.1 76.8 %collective-permute-start = (f32[8,8,128,128]{3,2,1,0:T(8,128)}, f32[8,8,128,128]{3,2,1,0:T(8,128)}, u32[]{:S(2)}, u32[]{:S(2)}) collective-permute-start(f32[8,8,128,128]{3,2,1,0:T(8,128)} %shard_map.105.refs_0_), channel_id=1, source_target_pairs={{0,16},{16,32},{32,48},{48,64},{64,80},{80,96},{96,112},{1,17},{17... | collective-permute-start | bytes 12582920 | tf_op jit(solution)/shard_map/ppermute | solution.py:497
  21.6 16.2 %collective-permute-start.2 = (f32[2,8,128,128]{3,2,1,0:T(8,128)S(1)}, f32[2,8,128,128]{3,2,1,0:T(8,128)}, u32[]{:S(2)}, u32[]{:S(2)}) collective-permute-start(f32[2,8,128,128]{3,2,1,0:T(8,128)S(1)} %shard_map.107.refs_2_), channel_id=1, source_target_pairs={{0,16},{32,48},{64,80},{96,112},{16,96},{48,0},{80,32},{1,17},{33,... | collective-permute-start | bytes 3145736 | tf_op jit(solution)/shard_map/ppermute | solution.py:505
  26.1 28.4 %collective-permute-start.3 = (f32[2,8,128,128]{3,2,1,0:T(8,128)S(1)}, f32[2,8,128,128]{3,2,1,0:T(8,128)}, u32[]{:S(2)}, u32[]{:S(2)}) collective-permute-start(f32[2,8,128,128]{3,2,1,0:T(8,128)S(1)} %shard_map.108.refs_3_), channel_id=1, source_target_pairs={{0,16},{32,48},{64,80},{96,112},{16,96},{48,0},{80,32},{1,17},{33,... | collective-permute-start | bytes 3145736 | tf_op jit(solution)/shard_map/ppermute | solution.py:505
  37.8 26.7 %collective-permute-start.4 = (f32[2,8,128,128]{3,2,1,0:T(8,128)}, f32[2,8,128,128]{3,2,1,0:T(8,128)}, u32[]{:S(2)}, u32[]{:S(2)}) collective-permute-start(f32[2,8,128,128]{3,2,1,0:T(8,128)} %collective-permute-done.2.refs_4_.refs_8_), channel_id=1, source_target_pairs={{96,64},{0,96},{32,0},{97,65},{1,97},{33,1},{98,66},{2,98},{34,2},... | collective-permute-start | bytes 3145736 | tf_op jit(solution)/shard_map/ppermute | solution.py:508
  54.5 17.1 %collective-permute-start.6 = (f32[2,8,128,128]{3,2,1,0:T(8,128)}, f32[2,8,128,128]{3,2,1,0:T(8,128)}, u32[]{:S(2)}, u32[]{:S(2)}) collective-permute-start(f32[2,8,128,128]{3,2,1,0:T(8,128)} %collective-permute-done.3.refs_5_.refs_9_), channel_id=1, source_target_pairs={{96,64},{0,96},{32,0},{97,65},{1,97},{33,1},{98,66},{2,98},{34,2},... | collective-permute-start | bytes 3145736 | tf_op jit(solution)/shard_map/ppermute | solution.py:508
  61.1 26.8 %collective-permute-start.1 = (f32[4,8,128,128]{3,2,1,0:T(8,128)S(1)}, f32[4,8,128,128]{3,2,1,0:T(8,128)}, u32[]{:S(2)}, u32[]{:S(2)}) collective-permute-start(f32[4,8,128,128]{3,2,1,0:T(8,128)S(1)} %shard_map.106.refs_1_), channel_id=1, source_target_pairs={{0,16},{16,32},{32,48},{48,64},{64,80},{80,96},{96,112},{1,17},{17... | collective-permute-start | bytes 6291464 | tf_op jit(solution)/shard_map/ppermute | solution.py:497
  64.5 23.4 %collective-permute-start.5 = (f32[2,8,128,128]{3,2,1,0:T(8,128)}, f32[2,8,128,128]{3,2,1,0:T(8,128)}, u32[]{:S(2)}, u32[]{:S(2)}) collective-permute-start(f32[2,8,128,128]{3,2,1,0:T(8,128)} %collective-permute-done.4), channel_id=1, source_target_pairs={{64,32},{96,64},{0,96},{65,33},{97,65},{1,97},{66,34},{98,66},{2,9... | collective-permute-start | bytes 3145736 | tf_op jit(solution)/shard_map/ppermute | solution.py:508
  71.5 21.4 %collective-permute-start.7 = (f32[2,8,128,128]{3,2,1,0:T(8,128)}, f32[2,8,128,128]{3,2,1,0:T(8,128)}, u32[]{:S(2)}, u32[]{:S(2)}) collective-permute-start(f32[2,8,128,128]{3,2,1,0:T(8,128)} %collective-permute-done.6), channel_id=1, source_target_pairs={{64,32},{96,64},{0,96},{65,33},{97,65},{1,97},{66,34},{98,66},{2,9... | collective-permute-start | bytes 3145736 | tf_op jit(solution)/shard_map/ppermute | solution.py:508
  118.4 25.2 %collective-permute-start.13 = (f32[1024,128]{1,0:T(8,128)S(1)}, f32[1024,128]{1,0:T(8,128)S(1)}, u32[]{:S(2)}, u32[]{:S(2)}) collective-permute-start(f32[1024,128]{1,0:T(8,128)S(1)} %pad_maximum_fusion.2), channel_id=1, source_target_pairs={{0,12},{1,13},{2,14},{3,15},{4,8},{5,9},{6,10},{7,11},{8,4},{9,5},... | collective-permute-start | bytes 1572872 | tf_op jit(solution)/shard_map/ppermute | solution.py:429
  122.7 17.0 %collective-permute-start.16 = (f32[1024,128]{1,0:T(8,128)S(1)}, f32[1024,128]{1,0:T(8,128)S(1)}, u32[]{:S(2)}, u32[]{:S(2)}) collective-permute-start(f32[1024,128]{1,0:T(8,128)S(1)} %pad_maximum_fusion.3), channel_id=1, source_target_pairs={{0,1},{1,0},{2,3},{3,2},{4,5},{5,4},{6,7},{7,6},{8,9},{9,8},{10,11... | collective-permute-start | bytes 1572872 | tf_op jit(solution)/shard_map/ppermute | solution.py:429
  125.1 14.4 %collective-permute-start.19 = (f32[1024,128]{1,0:T(8,128)S(1)}, f32[1024,128]{1,0:T(8,128)S(1)}, u32[]{:S(2)}, u32[]{:S(2)}) collective-permute-start(f32[1024,128]{1,0:T(8,128)S(1)} %pad_maximum_fusion.4), channel_id=1, source_target_pairs={{0,3},{1,2},{2,1},{3,0},{4,7},{5,6},{6,5},{7,4},{8,11},{9,10},{10,... | collective-permute-start | bytes 1572872 | tf_op jit(solution)/shard_map/ppermute | solution.py:429
  139.6 14.9 %collective-permute-start.23 = (f32[2048,128]{1,0:T(8,128)S(1)}, f32[2048,128]{1,0:T(8,128)S(1)}, u32[]{:S(2)}, u32[]{:S(2)}) collective-permute-start(f32[2048,128]{1,0:T(8,128)S(1)} %constant_dynamic-update-slice_fusion.12.refs_3_), channel_id=1, source_target_pairs={{0,1},{1,0},{2,3},{3,2},{4,5},{5,4},{6,7},{7,6},{8,9},{9,8},{10,11... | collective-permute-start | bytes 3145736 | tf_op jit(solution)/shard_map/ppermute | solution.py:429
  139.7 18.3 %collective-permute-start.22 = (f32[2048,128]{1,0:T(8,128)S(1)}, f32[2048,128]{1,0:T(8,128)S(1)}, u32[]{:S(2)}, u32[]{:S(2)}) collective-permute-start(f32[2048,128]{1,0:T(8,128)S(1)} %constant_dynamic-update-slice_fusion.8.refs_2_), channel_id=1, source_target_pairs={{0,3},{1,2},{2,1},{3,0},{4,7},{5,6},{6,5},{7,4},{8,11},{9,10},{10,... | collective-permute-start | bytes 3145736 | tf_op jit(solution)/shard_map/ppermute | solution.py:429
  140.2 18.3 %collective-permute-start.20 = (f32[2112,128]{1,0:T(8,128)S(1)}, f32[2112,128]{1,0:T(8,128)S(1)}, u32[]{:S(2)}, u32[]{:S(2)}) collective-permute-start(f32[2112,128]{1,0:T(8,128)S(1)} %constant_dynamic-update-slice_fusion.refs_0_.refs_4_), channel_id=1, source_target_pairs={{0,12},{1,13},{2,14},{3,15},{4,8},{5,9},{6,10},{7,11},{8,4},{9,5},... | collective-permute-start | bytes 3244040 | tf_op jit(solution)/shard_map/ppermute | solution.py:429
  143.6 14.9 %collective-permute-start.21 = (f32[2048,128]{1,0:T(8,128)S(1)}, f32[2048,128]{1,0:T(8,128)S(1)}, u32[]{:S(2)}, u32[]{:S(2)}) collective-permute-start(f32[2048,128]{1,0:T(8,128)S(1)} %constant_dynamic-update-slice_fusion.4.refs_1_), channel_id=1, source_target_pairs={{0,4},{1,5},{2,6},{3,7},{4,0},{5,1},{6,2},{7,3},{8,12},{9,13},{10,... | collective-permute-start | bytes 3145736 | tf_op jit(solution)/shard_map/ppermute | solution.py:429
  184.7 22.7 %collective-permute-start.29 = (f32[1024,128]{1,0:T(8,128)S(1)}, f32[1024,128]{1,0:T(8,128)S(1)}, u32[]{:S(2)}, u32[]{:S(2)}) collective-permute-start(f32[1024,128]{1,0:T(8,128)S(1)} %pad_maximum_fusion.5), channel_id=1, source_target_pairs={{0,12},{1,13},{2,14},{3,15},{4,8},{5,9},{6,10},{7,11},{8,4},{9,5},... | collective-permute-start | bytes 1572872 | tf_op jit(solution)/shard_map/ppermute | solution.py:429
  186.2 17.6 %collective-permute-start.32 = (f32[1024,128]{1,0:T(8,128)S(1)}, f32[1024,128]{1,0:T(8,128)S(1)}, u32[]{:S(2)}, u32[]{:S(2)}) collective-permute-start(f32[1024,128]{1,0:T(8,128)S(1)} %pad_maximum_fusion.6), channel_id=1, source_target_pairs={{0,1},{1,0},{2,3},{3,2},{4,5},{5,4},{6,7},{7,6},{8,9},{9,8},{10,11... | collective-permute-start | bytes 1572872 | tf_op jit(solution)/shard_map/ppermute | solution.py:429
  187.6 16.2 %collective-permute-start.35 = (f32[1024,128]{1,0:T(8,128)S(1)}, f32[1024,128]{1,0:T(8,128)S(1)}, u32[]{:S(2)}, u32[]{:S(2)}) collective-permute-start(f32[1024,128]{1,0:T(8,128)S(1)} %pad_maximum_fusion.7), channel_id=1, source_target_pairs={{0,3},{1,2},{2,1},{3,0},{4,7},{5,6},{6,5},{7,4},{8,11},{9,10},{10,... | collective-permute-start | bytes 1572872 | tf_op jit(solution)/shard_map/ppermute | solution.py:429
  189.7 16.3 %collective-permute-start.26 = (f32[1056,128]{1,0:T(8,128)S(1)}, f32[1056,128]{1,0:T(8,128)S(1)}, u32[]{:S(2)}, u32[]{:S(2)}) collective-permute-start(f32[1056,128]{1,0:T(8,128)S(1)} %pad_maximum_fusion.1), channel_id=1, source_target_pairs={{0,4},{1,5},{2,6},{3,7},{4,0},{5,1},{6,2},{7,3},{8,12},{9,13},{10,... | collective-permute-start | bytes 1622024 | tf_op jit(solution)/shard_map/ppermute | solution.py:429
  203.8 14.9 %collective-permute-start.39 = (f32[2048,128]{1,0:T(8,128)S(1)}, f32[2048,128]{1,0:T(8,128)S(1)}, u32[]{:S(2)}, u32[]{:S(2)}) collective-permute-start(f32[2048,128]{1,0:T(8,128)S(1)} %constant_dynamic-update-slice_fusion.28.refs_3_), channel_id=1, source_target_pairs={{0,1},{1,0},{2,3},{3,2},{4,5},{5,4},{6,7},{7,6},{8,9},{9,8},{10,11... | collective-permute-start | bytes 3145736 | tf_op jit(solution)/shard_map/ppermute | solution.py:429
  203.9 16.1 %collective-permute-start.38 = (f32[2048,128]{1,0:T(8,128)S(1)}, f32[2048,128]{1,0:T(8,128)S(1)}, u32[]{:S(2)}, u32[]{:S(2)}) collective-permute-start(f32[2048,128]{1,0:T(8,128)S(1)} %constant_dynamic-update-slice_fusion.24.refs_2_), channel_id=1, source_target_pairs={{0,3},{1,2},{2,1},{3,0},{4,7},{5,6},{6,5},{7,4},{8,11},{9,10},{10,... | collective-permute-start | bytes 3145736 | tf_op jit(solution)/shard_map/ppermute | solution.py:429
  206.0 16.4 %collective-permute-start.36 = (f32[2112,128]{1,0:T(8,128)S(1)}, f32[2112,128]{1,0:T(8,128)S(1)}, u32[]{:S(2)}, u32[]{:S(2)}) collective-permute-start(f32[2112,128]{1,0:T(8,128)S(1)} %constant_dynamic-update-slice_fusion.16.refs_0_), channel_id=1, source_target_pairs={{0,12},{1,13},{2,14},{3,15},{4,8},{5,9},{6,10},{7,11},{8,4},{9,5},... | collective-permute-start | bytes 3244040 | tf_op jit(solution)/shard_map/ppermute | solution.py:429
  207.4 14.9 %collective-permute-start.37 = (f32[2048,128]{1,0:T(8,128)S(1)}, f32[2048,128]{1,0:T(8,128)S(1)}, u32[]{:S(2)}, u32[]{:S(2)}) collective-permute-start(f32[2048,128]{1,0:T(8,128)S(1)} %constant_dynamic-update-slice_fusion.20.refs_1_), channel_id=1, source_target_pairs={{0,4},{1,5},{2,6},{3,7},{4,0},{5,1},{6,2},{7,3},{8,12},{9,13},{10,... | collective-permute-start | bytes 3145736 | tf_op jit(solution)/shard_map/ppermute | solution.py:429
  (29 other events, 313.1 us)
Sparse Core Ops, SparseCore 0:
  10.8 73.6 all-gather.1
